TPU v7x, 128 devices: a whole 4x4x4 slice. The times are simulated.
128 devices in a mesh: leaf: 128 (over y, z, x, core).
Axes of the slice: x: 4, y: 4, z: 4, core: 2. Of those that a mesh axis runs over, the one named last changes fastest.
Arguments:
- points: bfloat16 [4096, 32, 256], P('leaf'), may hold values from -6 to 6
- weights: bfloat16 [4096, 4, 256], P('leaf'), may hold values from -6 to 6
- leaf_maps: bfloat16 [4096, 128, 256], P('leaf'), may hold values from -0.375 to 0.375
- root_maps: bfloat16 [128, 128, 4096], P('leaf'), may hold values from -0.09375 to 0.09375
- top_maps: bfloat16 [128, 128, 256], P('leaf'), may hold values from -0.375 to 0.375
- root_picks: int32 [128, 128], P('leaf'), may hold values from 0 to 8191
- top_picks: int32 [128, 128], P('leaf'), may hold values from 0 to 255
- near_lists: int32 [4096, 16], P('leaf'), may hold values from 0 to 4095, as said below
- far_lists: int32 [4096, 32], P('leaf'), may hold values from 1 to 255
Outputs:
- product: float32 [4096, 4, 256], P('leaf')
Inputs may be any that keep to these rules, and one draw needn't show every extreme that they name: near_lists[g, 0] = g, and every entry lies within 32 leaves of g; entries may repeat.
All inputs are finite; a program needn't handle non-finite values.
Results may differ from a plain program's by a relative error of at most 0.008.
Values may be sent and summed in bfloat16 or wider, within the bound.
No kernel may reach another device: no remote copies, remote signals or barrier semaphores. Data moves between devices by JAX's collectives and lax.ppermute only.
A program may use at most 64 MiB of HBM per device.

v0:
```python
import functools
import math

import jax
import jax.numpy as jnp
from jax import lax
from jax.experimental import pallas as pl
from jax.experimental.pallas import tpu as pltpu
from jax.sharding import PartitionSpec as P

gauss = 0.0625
bf16 = jnp.bfloat16
f32 = jnp.float32
NT = (((1,), (1,)), ((), ()))
FACTOR = 2.0 * gauss * math.log2(math.e)
WIDE = 128
GROUP = 8
SIDE = 4
ROOT_STEPS = (64, 32, 4, 8, 16, 2, 1)
ROOT_ROWS = 48
VMEM = pl.BlockSpec(memory_space=pltpu.VMEM)
SMEM = pl.BlockSpec(memory_space=pltpu.SMEM)


def params(mib):
    return pltpu.CompilerParams(vmem_limit_bytes=mib << 20)


def pieces(x):
    a = x.astype(bf16)
    r = x - a.astype(f32)
    b = r.astype(bf16)
    c = (r - b.astype(f32)).astype(bf16)
    return a, b, c


def norm_pieces(x):
    y = x.astype(f32)
    return pieces(-0.5 * jnp.sum(y * y, axis=0, keepdims=True))


def form_rows(x, first, second):
    dims, n = x.shape
    at = lax.broadcasted_iota(jnp.int32, (16, n), 0)
    tail = jnp.zeros((16, n), f32)
    for k in range(3):
        tail = jnp.where(at == k, first[k], tail)
        tail = jnp.where(at == 3 + k, second[k], tail)
    return jnp.concatenate([x, tail.astype(bf16), jnp.zeros((WIDE - dims - 16, n), bf16)], axis=0)


def source_form(x):
    norms = [p.astype(f32) for p in norm_pieces(x)]
    return form_rows(x, [1.0] * 3, norms).T


def target_form(x):
    norms = [p.astype(f32) for p in norm_pieces(x)]
    return form_rows(x, norms, [1.0] * 3)


def apply_map(three, maps):
    m = three.shape[0] // 3
    out = lax.dot_general(three, maps, NT, preferred_element_type=f32)
    return out[:m] + (out[m : 2 * m] + out[2 * m :])


def blocks_apply(target, sources, ws):
    p = jnp.dot(jnp.concatenate(sources, axis=0), target, preferred_element_type=f32)
    kern = jnp.exp2(p * FACTOR).astype(bf16)
    return jnp.dot(jnp.concatenate(ws, axis=1), kern, preferred_element_type=f32)


def upward_kernel(points, weights, leaf_maps, root_maps, picks, top_picks, root, root_w, stacked):
    per, dims, leaf_size = points.shape
    rank = leaf_maps.shape[1]
    want = picks[...]
    x = jnp.zeros((dims, rank), f32)
    for g in range(per):
        w = lax.dot_general(weights[g], leaf_maps[g], NT, preferred_element_type=f32)
        stacked[:, g * rank : (g + 1) * rank] = w
        at = lax.broadcasted_iota(jnp.int32, (leaf_size, rank), 0) + g * leaf_size
        hot = (at == want).astype(f32).astype(bf16)
        x = x + jnp.dot(points[g], hot, preferred_element_type=f32)
    w = apply_map(jnp.concatenate(pieces(stacked[...]), axis=0), root_maps[0])
    w = jnp.concatenate(pieces(w), axis=0)
    other = top_picks[...].astype(f32).astype(bf16)
    blank = jnp.zeros((ROOT_ROWS - dims - w.shape[0] - 1, rank), bf16)
    tail = jnp.concatenate([w, other, blank], axis=0)
    root[0] = jnp.concatenate([x.astype(bf16), tail], axis=0)
    root_w[0] = tail


def upward(points, weights, leaf_maps, root_maps, root_picks, top_picks):
    per, dims, _ = points.shape
    rhs, rank = weights.shape[1], leaf_maps.shape[1]
    return pl.pallas_call(
        upward_kernel,
        in_specs=[VMEM] * 6,
        out_specs=[VMEM] * 2,
        out_shape=[
            jax.ShapeDtypeStruct((1, ROOT_ROWS, rank), bf16),
            jax.ShapeDtypeStruct((1, ROOT_ROWS - dims, rank), bf16),
        ],
        scratch_shapes=[pltpu.VMEM((rhs, per * rank), f32)],
        compiler_params=params(60),
    )(points, weights, leaf_maps, root_maps, root_picks, top_picks)


def merge(left, right, maps):
    three = jnp.concatenate([left, right], axis=1)
    return jnp.concatenate(pieces(apply_map(three, maps)), axis=0)


def map_of(rows):
    return jnp.concatenate([rows[:128], rows[128:256]], axis=1)


def group_kernel(held, out):
    rhs = out.shape[2]
    level = [held[i, 256 : 256 + 3 * rhs] for i in range(GROUP)]
    slot = 0
    while len(level) > 1:
        level = [
            merge(level[2 * i], level[2 * i + 1], map_of(held[slot + i]))
            for i in range(len(level) // 2)
        ]
        for i, node in enumerate(level):
            out[0, slot + i] = node[:rhs]
        slot += len(level)
    out[0, slot] = level[0][rhs : 2 * rhs]
    out[0, slot + 1] = level[0][2 * rhs :]


def group_merge(held, rhs):
    return pl.pallas_call(
        group_kernel,
        in_specs=[VMEM],
        out_specs=VMEM,
        out_shape=jax.ShapeDtypeStruct((1, GROUP + 1, rhs, held.shape[-1]), bf16),
        compiler_params=params(16),
    )(held)


def slab_kernel(place, groups, maps, out):
    rhs = out.shape[2]
    me = place[0] // GROUP % SIDE
    top = GROUP - 2
    level = [
        jnp.concatenate([groups[i ^ me, top + k] for k in range(3)], axis=0) for i in range(SIDE)
    ]
    a = merge(level[0], level[1], map_of(maps[0 ^ me]))
    b = merge(level[2], level[3], map_of(maps[1 ^ me]))
    c = merge(a, b, map_of(maps[2 ^ me]))
    out[0, 0] = a[:rhs]
    out[0, 1] = b[:rhs]
    for k in range(3):
        out[0, 2 + k] = c[k * rhs : (k + 1) * rhs]


def slab_merge(place, groups, maps):
    rhs, rank = groups.shape[2:]
    return pl.pallas_call(
        slab_kernel,
        in_specs=[SMEM] + [VMEM] * 2,
        out_specs=VMEM,
        out_shape=jax.ShapeDtypeStruct((1, 5, rhs, rank), bf16),
        compiler_params=params(16),
    )(place, groups, maps)


def forms_kernel(points, first, second, sources, targets):
    per = points.shape[0]
    for i, ref in enumerate((points, first, second)):

        def prepare(g, carry, i=i, ref=ref):
            sources[i * per + g] = source_form(ref[g])
            if i == 0:
                targets[g] = target_form(ref[g])
            return carry

        lax.fori_loop(0, per, prepare, 0, unroll=16)


def forms(points, first, second):
    per, dims, leaf_size = points.shape
    return pl.pallas_call(
        forms_kernel,
        in_specs=[VMEM] * 3,
        out_specs=[VMEM] * 2,
        out_shape=[
            jax.ShapeDtypeStruct((3 * per, leaf_size, WIDE), bf16),
            jax.ShapeDtypeStruct((per, WIDE, leaf_size), bf16),
        ],
        compiler_params=params(24),
    )(points, first, second)


def field_kernel(unroll, together, start, lists, w_lists, sources, targets, ws, *rest):
    out = rest[-1]
    entries = lists.shape[1]

    def leaves(step, carry):
        totals = []
        for u in range(unroll):
            g = start + step * unroll + u
            target = targets[g]
            total = rest[0][g] if len(rest) > 1 else jnp.zeros(out.shape[1:], f32)
            for j in range(0, entries, together):
                total = total + blocks_apply(
                    target,
                    [sources[lists[g, j + k]] for k in range(together)],
                    [ws[w_lists[g, j + k]] for k in range(together)],
                )
            totals.append(total)
        for u in range(unroll):
            out[step * unroll + u] = totals[u]
        return carry

    lax.fori_loop(0, out.shape[0] // unroll, leaves, 0)


def field(start, count, lists, w_lists, sources, targets, ws, *init):
    rhs, leaf_size = ws.shape[1], targets.shape[2]
    columns = sources.shape[1]
    entries = count * lists.shape[1] * columns * leaf_size
    return pl.pallas_call(
        functools.partial(field_kernel, 4, 1024 // columns, start),
        in_specs=[SMEM] * 2 + [VMEM] * (3 + len(init)),
        out_specs=VMEM,
        out_shape=jax.ShapeDtypeStruct((count, rhs, leaf_size), f32),
        compiler_params=params(24),
        cost_estimate=pl.CostEstimate(flops=entries * 1024, bytes_accessed=1 << 20, transcendentals=0),
    )(lists, w_lists, sources, targets, ws, *init)


def tables_kernel(place, spots, own_roots, other_roots, table, maps, sources, ws, x_all, picks):
    half_roots, _, rank = own_roots.shape
    nodes = 2 * half_roots
    dims = x_all.shape[1]
    rhs = ws.shape[1]
    y_me = place[0] // (GROUP * SIDE)

    count = table.shape[1]
    for y in range(SIDE):
        ws[y * count : (y + 1) * count] = table[y]
    row = SIDE * (GROUP + 1) + 2
    tops = [
        jnp.concatenate([table[y ^ y_me, row + k] for k in range(3)], axis=0) for y in range(SIDE)
    ]
    a = merge(tops[0], tops[1], map_of(maps[0 ^ y_me]))
    b = merge(tops[2], tops[3], map_of(maps[1 ^ y_me]))
    c = merge(a, b, map_of(maps[2 ^ y_me]))
    for k, node in enumerate((c, a, b)):
        ws[SIDE * count + k] = node[:rhs]
    base = SIDE * count + 4
    ws[base : base + half_roots] = own_roots[:, dims : dims + rhs]
    ws[base + half_roots : base + nodes] = other_roots[:, dims : dims + rhs]

    picked = dims + 3 * rhs
    for held, ref in enumerate((own_roots, other_roots)):

        def copy_root(step, carry, held=held, ref=ref):
            for u in range(8):
                i = step * 8 + u
                n = spots[held * half_roots + i]
                x_all[nodes + n] = ref[i, :dims]
                picks[n] = ref[i, picked : picked + 1].astype(f32)
            return carry

        lax.fori_loop(0, half_roots // 8, copy_root, 0)
    x_all[0] = jnp.zeros((dims, rank), bf16)

    half = nodes // 2
    while half:
        group = min(half, 16)

        def select(step, carry, half=half, group=group):
            first = half + step * group
            found = []
            for u in range(group):
                n = first + u
                pair = jnp.concatenate([x_all[2 * n], x_all[2 * n + 1]], axis=1)
                at = lax.broadcasted_iota(jnp.int32, (2 * rank, rank), 0)
                hot = (at == picks[n].astype(jnp.int32)).astype(f32).astype(bf16)
                found.append(jnp.dot(pair, hot, preferred_element_type=f32).astype(bf16))
            for u in range(group):
                x_all[first + u] = found[u]
            return carry

        lax.fori_loop(0, half // group, select, 0)
        half //= 2

    def prepare(step, carry):
        found = []
        for u in range(16):
            i = step * 16 + u
            found.append(source_form(jnp.concatenate([x_all[2 * i], x_all[2 * i + 1]], axis=1)))
        for u in range(16):
            i = step * 16 + u
            sources[2 * i] = found[u][:rank]
            sources[2 * i + 1] = found[u][rank:]
        return carry

    lax.fori_loop(0, nodes // 16, prepare, 0)


def far_tables(place, spots, own_roots, other_roots, table, maps):
    nodes = 2 * own_roots.shape[0]
    rhs, rank = table.shape[2:]
    dims = ROOT_ROWS - 16
    return pl.pallas_call(
        tables_kernel,
        in_specs=[SMEM] * 2 + [VMEM] * 4,
        out_specs=[VMEM] * 2,
        out_shape=[
            jax.ShapeDtypeStruct((2 * nodes, rank, WIDE), bf16),
            jax.ShapeDtypeStruct((SIDE * table.shape[1] + 4 + nodes, rhs, rank), bf16),
        ],
        scratch_shapes=[
            pltpu.VMEM((2 * nodes, dims, rank), bf16),
            pltpu.VMEM((nodes, 1, rank), f32),
        ],
        compiler_params=params(24),
    )(place, spots, own_roots, other_roots, table, maps)


def weight_places(lists, me, count):
    y_me, z_me = me // (GROUP * SIDE), me // GROUP % SIDE

    def in_group(group, k):
        return count * ((group // SIDE) ^ y_me) + (GROUP + 1) * ((group % SIDE) ^ z_me) + k

    def in_slab(y, k):
        return count * (y ^ y_me) + SIDE * (GROUP + 1) + k

    n = lists
    d = n - 128
    turned = jnp.zeros_like(d)
    for k, mask in enumerate(ROOT_STEPS):
        turned = turned | jnp.where(((d ^ me) & mask) != 0, 1 << k, 0)
    out = SIDE * count + 4 + turned
    out = jnp.where(n < 128, in_group((n - 64) // 4, n % 4), out)
    out = jnp.where(n < 64, in_group((n - 32) // 2, 4 + n % 2), out)
    out = jnp.where(n < 32, in_group(n - 16, 6), out)
    out = jnp.where(n < 16, in_slab((n - 8) // 2, n % 2), out)
    out = jnp.where(n < 8, in_slab(n - 4, 2), out)
    return jnp.where(n < 4, SIDE * count + n - 1, out)


def home_of(node):
    if node >= 64:
        return GROUP * ((node - 64) // 4) + (node - 64) % 4
    if node >= 32:
        return GROUP * ((node - 32) // 2) + 4 + (node - 32) % 2
    if node >= 16:
        return GROUP * (node - 16) + 6
    if node >= 8:
        y, z = (node - 8) // 2, (node - 8) % 2
    elif node >= 4:
        y, z = node - 4, 2
    else:
        y, z = {2: 0, 3: 1, 1: 2, 0: 3}[node], 3
    return GROUP * (SIDE * y + z) + 7


def swap(x, mask, size):
    return lax.ppermute(x, "leaf", [(i, i ^ mask) for i in range(size)])


def both(x, mask, size):
    return jnp.concatenate([x, swap(x, mask, size)], axis=0)


def on_device(
    points, weights, leaf_maps, root_maps, top_maps, root_picks, top_picks, near_lists, far_lists
):
    per, dims, leaf_size = points.shape
    rhs = weights.shape[1]
    size = lax.axis_size("leaf")
    me = lax.axis_index("leaf")
    place = me.astype(jnp.int32).reshape(1)
    z_me = me // GROUP % SIDE

    pairs = [(i, i ^ 1) for i in range(size)]
    bridges = [(i, i + 1) for i in range(1, size - 1, 2)]
    bridges = bridges + [(j, i) for i, j in bridges]
    maps = lax.ppermute(top_maps, "leaf", [(n, home_of(n)) for n in range(size)])
    second = lax.ppermute(points, "leaf", bridges)
    w_second = lax.ppermute(weights, "leaf", bridges)
    first = lax.ppermute(points, "leaf", pairs)
    w_first = lax.ppermute(weights, "leaf", pairs)

    root, root_w = upward(points, weights, leaf_maps, root_maps, root_picks, top_picks)

    def more(root, step):
        return both(root, ROOT_STEPS[step], size)

    root = more(root, 0)
    held = jnp.concatenate([maps[:, :, :128], maps[:, :, 128:], root_w], axis=1)
    held, root = lax.optimization_barrier((held, root))
    groups = [[g * GROUP + k for k in range(GROUP)] for g in range(size // GROUP)]
    held = lax.all_gather(held, "leaf", axis=0, tiled=True, axis_index_groups=groups)
    root = more(root, 1)
    held, root = lax.optimization_barrier((held, root))
    root = more(root, 2)
    group_nodes = group_merge(held, rhs)
    spare = held[GROUP - 1 :, :256]

    local = near_lists - me * per
    side = jnp.where(me % 2 == 0, jnp.where(local < 0, 2, 1), jnp.where(local < 0, 1, 2))
    inside = jnp.logical_and(local >= 0, local < per)
    slots = jnp.where(inside, local, side * per + local % per)
    sources, targets = forms(points, first, second)
    ws = jnp.concatenate([weights, w_first, w_second], axis=0)

    parts = 4
    nears = []

    def near_part(k, slots):
        return field(k * (per // parts), per // parts, slots, slots, sources, targets, ws)

    slots, group_nodes, spare, root = lax.optimization_barrier((slots, group_nodes, spare, root))
    groups, slab_maps = [both(a, 8, size) for a in (group_nodes, spare)]
    root = more(root, 3)
    nears.append(near_part(0, slots))
    nears[0], slots, groups, slab_maps, root = lax.optimization_barrier(
        (nears[0], slots, groups, slab_maps, root)
    )
    groups, slab_maps = [both(a, 16, size) for a in (groups, slab_maps)]
    root = more(root, 4)
    nears.append(near_part(1, slots))
    nears[1], slots, groups, slab_maps, root = lax.optimization_barrier(
        (nears[1], slots, groups, slab_maps, root)
    )
    slab_nodes = slab_merge(place, groups, slab_maps)
    table = jnp.concatenate([groups.reshape(1, -1, rhs, groups.shape[-1]), slab_nodes], axis=1)
    last_maps = lax.dynamic_slice_in_dim(slab_maps, z_me ^ (SIDE - 1), 1, 0)
    slots, table, last_maps, root = lax.optimization_barrier((slots, table, last_maps, root))
    table, last_maps = [both(a, 32, size) for a in (table, last_maps)]
    root = more(root, 5)
    nears.append(near_part(2, slots))
    nears[2], slots, table, last_maps, root = lax.optimization_barrier(
        (nears[2], slots, table, last_maps, root)
    )
    table, last_maps = [both(a, 64, size) for a in (table, last_maps)]
    other_roots = swap(root, ROOT_STEPS[6], size)
    nears.append(near_part(3, slots))

    index = jnp.arange(size, dtype=jnp.int32)
    spots = place
    for k, mask in enumerate(ROOT_STEPS):
        spots = spots ^ jnp.where(((index >> k) & 1) != 0, mask, 0)
    w_lists = weight_places(far_lists, me, table.shape[1])
    near = jnp.concatenate(nears, axis=0)
    far_sources, far_ws = far_tables(place, spots, root, other_roots, table, last_maps)
    return field(0, per, far_lists, w_lists, far_sources, targets, far_ws, near)


def solution(mesh):
    leaf3 = P("leaf", None, None)
    leaf2 = P("leaf", None)
    return jax.shard_map(
        on_device,
        mesh=mesh,
        in_specs=(leaf3,) * 5 + (leaf2,) * 4,
        out_specs=leaf3,
        check_vma=False,
    )
```

profile of v0, /device:TPU:0, one launch (start us, length us, event | category | flops | bytes accessed | tf_op | source)
XLA Modules:
  0.0 166.8 jit_solution(9629062855622994678)
XLA Ops:
  0.0 0.0 collective-permute-start.4
  0.0 0.8 collective-permute-start.5
  0.8 3.0 %collective-permute-start.6 = (bf16[32,4,256]{2,1,0:T(4,128)(2,1)}, bf16[32,4,256]{2,1,0:T(4,128)(2,1)S(1)}, u32[]{:S(2)}, u32[]{:S(2)}) collective-permute-start(bf16[32,4,256]{2,1,0:T(4,128)(2,1)} %weights.1), channel_id=1, source_target_pairs={{0,1},{1,0},{2,3},{3,2},{4,5},{5,4},{6,7},{7,6},{8,9},{9,8},{10,11... | collective-permute-start | bytes 196616 | tf_op jit(solution)/shard_map/ppermute | solution.py:392
  3.8 0.7 collective-permute-start.7
  4.5 4.1 %shard_map.91 = (bf16[1,48,128]{2,1,0:T(8,128)(2,1)}, bf16[1,16,128]{2,1,0:T(8,128)(2,1)}) custom-call(bf16[32,32,256]{2,1,0:T(8,128)(2,1)} %points.3, bf16[32,4,256]{2,1,0:T(4,128)(2,1)} %weights.1, bf16[32,128,256]{2,1,0:T(8,128)(2,1)} %leaf_maps.1, bf16[1,128,4096]{2,1,0:T(8,128)(2,1)} %root_maps.1, s32[1,128]{1,0:T(1,128)} %picks.1, s32[1,128]{1,0:T(1,128)} %top_picks.1), custom_call_target="tpu_custom_call" | custom-call | tf_op jit(solution)/shard_map/pallas_call | solution.py:97
  8.6 9.9 %collective-permute-start.1 = (bf16[1,48,128]{2,1,0:T(8,128)(2,1)}, bf16[1,48,128]{2,1,0:T(8,128)(2,1)S(1)}, u32[]{:S(2)}, u32[]{:S(2)}) collective-permute-start(bf16[1,48,128]{2,1,0:T(8,128)(2,1)} %get-tuple-element.39), channel_id=1, source_target_pairs={{0,64},{1,65},{2,66},{3,67},{4,68},{5,69},{6,70},{7,71},{8,72},{9,... | collective-permute-start | bytes 36872 | tf_op jit(solution)/shard_map/ppermute | solution.py:368
  18.5 0.9 constant_dynamic-update-slice_fusion.2
  19.4 0.8 copy.11
  20.2 0.8 fusion.7.w_lists
  21.1 5.4 %collective-permute-start = (bf16[1,128,256]{2,1,0:T(8,128)(2,1)}, bf16[1,128,256]{2,1,0:T(8,128)(2,1)S(1)}, u32[]{:S(2)}, u32[]{:S(2)}) collective-permute-start(bf16[1,128,256]{2,1,0:T(8,128)(2,1)} %param.13), channel_id=1, source_target_pairs={{0,127},{1,95},{2,31},{3,63},{4,23},{5,55},{6,87},{7,119},{8,7},{9... | collective-permute-start | bytes 196616 | tf_op jit(solution)/shard_map/ppermute | solution.py:388
  26.5 0.7 pad_maximum_fusion.15
  27.2 2.4 %collective-permute-done = bf16[1,128,256]{2,1,0:T(8,128)(2,1)S(1)} collective-permute-done((bf16[1,128,256]{2,1,0:T(8,128)(2,1)}, bf16[1,128,256]{2,1,0:T(8,128)(2,1)S(1)}, u32[]{:S(2)}, u32[]{:S(2)}) %collective-permute-start) | collective-permute-done | bytes 65568 | tf_op jit(solution)/shard_map/ppermute | solution.py:388
  29.7 0.7 pad_maximum_fusion.11
  30.3 13.1 %all_gather.3.held = bf16[8,272,128]{2,1,0:T(8,128)(2,1)S(1)} all-gather(bf16[1,272,128]{2,1,0:T(8,128)(2,1)S(1)} %pad_maximum_fusion.11), channel_id=1, replica_groups={{0,1,2,3,4,5,6,7},{8,9,10,11,12,13,14,15},{16,17,18,19,20,21,22,23},{24..., dimensions={0}, use_global_device_ids=true | all-gather | bytes 626688 | tf_op jit(solution)/shard_map/all_gather | solution.py:403
  43.5 0.0 collective-permute-done.2
  43.5 1.5 collective-permute-start.3
  45.0 0.0 collective-permute-done.6
  45.1 0.4 shard_map.92
  45.5 3.6 %collective-permute-done.3 = bf16[4,48,128]{2,1,0:T(8,128)(2,1)S(1)} collective-permute-done((bf16[4,48,128]{2,1,0:T(8,128)(2,1)S(1)}, bf16[4,48,128]{2,1,0:T(8,128)(2,1)S(1)}, u32[]{:S(2)}, u32[]{:S(2)}) %collective-permute-start.3) | collective-permute-done | bytes 49184 | tf_op jit(solution)/shard_map/ppermute | solution.py:368
  49.2 0.1 collective-permute-start.8
  49.3 2.1 %collective-permute-start.10 = (bf16[8,48,128]{2,1,0:T(8,128)(2,1)S(1)}, bf16[8,48,128]{2,1,0:T(8,128)(2,1)S(1)}, u32[]{:S(2)}, u32[]{:S(2)}) collective-permute-start(bf16[8,48,128]{2,1,0:T(8,128)(2,1)S(1)} %pad_maximum_fusion.9), channel_id=1, source_target_pairs={{0,8},{1,9},{2,10},{3,11},{4,12},{5,13},{6,14},{7,15},{8,0},{9,1},... | collective-permute-start | bytes 294920 | tf_op jit(solution)/shard_map/ppermute | solution.py:368
  51.4 0.1 collective-permute-start.9
  51.5 1.5 collective-permute-done.8
  53.1 2.6 %collective-permute-done.9 = bf16[1,256,128]{2,1,0:T(8,128)(2,1)S(1)} collective-permute-done((bf16[1,256,128]{2,1,0:T(8,128)(2,1)S(1)}, bf16[1,256,128]{2,1,0:T(8,128)(2,1)S(1)}, u32[]{:S(2)}, u32[]{:S(2)}) %collective-permute-start.9) | collective-permute-done | bytes 65568 | tf_op jit(solution)/shard_map/ppermute | solution.py:368
  55.7 0.0 collective-permute-done.4.first
  55.8 2.3 %shard_map.93 = (bf16[96,256,128]{2,1,0:T(8,128)(2,1)S(1)}, bf16[32,128,256]{2,1,0:T(8,128)(2,1)S(1)}) custom-call(bf16[32,32,256]{2,1,0:T(8,128)(2,1)S(1)} %copy-done, bf16[32,32,256]{2,1,0:T(8,128)(2,1)S(1)} %collective-permute-done.4.first, bf16[32,32,256]{2,1,0:T(8,128)(2,1)S(1)} %collective-permute-done.5.second), custom_call_target="tpu_custom_call" | custom-call | tf_op jit(solution)/shard_map/pallas_call | solution.py:187
  58.1 8.2 %shard_map.94 = f32[8,4,256]{2,1,0:T(4,128)S(1)} custom-call(s32[32,16]{1,0:T(8,128)S(1)} %fusion.33.lists.w_lists, s32[32,16]{1,0:T(8,128)S(1)} %fusion.33.lists.w_lists, bf16[96,256,128]{2,1,0:T(8,128)(2,1)S(1)} %get-tuple-element.45.sources, bf16[32,128,256]{2,1,0:T(8,128)(2,1)S(1)} %get-tuple-element.46.targets, ...), custom_call_target="tpu_custom_call" | custom-call | flops 8589934592 | bytes 1048576 | tf_op jit(solution)/shard_map/pallas_call | solution.py:227
  66.3 3.7 %collective-permute-start.13 = (bf16[16,48,128]{2,1,0:T(8,128)(2,1)S(1)}, bf16[16,48,128]{2,1,0:T(8,128)(2,1)S(1)}, u32[]{:S(2)}, u32[]{:S(2)}) collective-permute-start(bf16[16,48,128]{2,1,0:T(8,128)(2,1)S(1)} %pad_maximum_fusion.4), channel_id=1, source_target_pairs={{0,16},{1,17},{2,18},{3,19},{4,20},{5,21},{6,22},{7,23},{8,24},{9,... | collective-permute-start | bytes 589832 | tf_op jit(solution)/shard_map/ppermute | solution.py:368
  69.9 0.1 collective-permute-start.12
  70.0 3.5 %collective-permute-start.11 = (bf16[2,9,4,128]{3,2,1,0:T(4,128)(2,1)S(1)}, bf16[2,9,4,128]{3,2,1,0:T(4,128)(2,1)S(1)}, u32[]{:S(2)}, u32[]{:S(2)}) collective-permute-start(bf16[2,9,4,128]{3,2,1,0:T(4,128)(2,1)S(1)} %pad_maximum_fusion.16), channel_id=1, source_target_pairs={{0,16},{1,17},{2,18},{3,19},{4,20},{5,21},{6,22},{7,23},{8,24},{9,... | collective-permute-start | bytes 55304 | tf_op jit(solution)/shard_map/ppermute | solution.py:368
  73.5 8.2 %shard_map.95 = f32[8,4,256]{2,1,0:T(4,128)S(1)} custom-call(s32[32,16]{1,0:T(8,128)S(1)} %fusion.33.lists.w_lists, s32[32,16]{1,0:T(8,128)S(1)} %fusion.33.lists.w_lists, bf16[96,256,128]{2,1,0:T(8,128)(2,1)S(1)} %get-tuple-element.45.sources, bf16[32,128,256]{2,1,0:T(8,128)(2,1)S(1)} %get-tuple-element.46.targets, ...), custom_call_target="tpu_custom_call" | custom-call | flops 8589934592 | bytes 1048576 | tf_op jit(solution)/shard_map/pallas_call | solution.py:227
  81.6 0.0 collective-permute-done.11
  81.7 0.0 collective-permute-done.12
  81.8 0.3 shard_map.96
  82.2 0.1 collective-permute-start.16
  82.2 2.1 %collective-permute-start.15 = (bf16[1,256,128]{2,1,0:T(8,128)(2,1)S(1)}, bf16[1,256,128]{2,1,0:T(8,128)(2,1)S(1)}, u32[]{:S(2)}, u32[]{:S(2)}) collective-permute-start(bf16[1,256,128]{2,1,0:T(8,128)(2,1)S(1)} %constant_dynamic-slice_fusion), channel_id=1, source_target_pairs={{0,32},{1,33},{2,34},{3,35},{4,36},{5,37},{6,38},{7,39},{8,40},{9,... | collective-permute-start | bytes 196616 | tf_op jit(solution)/shard_map/ppermute | solution.py:368
  84.3 0.1 collective-permute-start.14
  84.4 8.2 %shard_map.97 = f32[8,4,256]{2,1,0:T(4,128)S(1)} custom-call(s32[32,16]{1,0:T(8,128)S(1)} %fusion.33.lists.w_lists, s32[32,16]{1,0:T(8,128)S(1)} %fusion.33.lists.w_lists, bf16[96,256,128]{2,1,0:T(8,128)(2,1)S(1)} %get-tuple-element.45.sources, bf16[32,128,256]{2,1,0:T(8,128)(2,1)S(1)} %get-tuple-element.46.targets, ...), custom_call_target="tpu_custom_call" | custom-call | flops 8589934592 | bytes 1048576 | tf_op jit(solution)/shard_map/pallas_call | solution.py:227
  92.6 0.1 pad_maximum_fusion.10
  92.7 0.1 pad_maximum_fusion.own_roots
  92.8 0.0 copy-start.1
  92.8 3.7 %collective-permute-start.19 = (bf16[2,256,128]{2,1,0:T(8,128)(2,1)S(1)}, bf16[2,256,128]{2,1,0:T(8,128)(2,1)S(1)}, u32[]{:S(2)}, u32[]{:S(2)}) collective-permute-start(bf16[2,256,128]{2,1,0:T(8,128)(2,1)S(1)} %pad_maximum_fusion.7), channel_id=1, source_target_pairs={{0,64},{1,65},{2,66},{3,67},{4,68},{5,69},{6,70},{7,71},{8,72},{9,... | collective-permute-start | bytes 393224 | tf_op jit(solution)/shard_map/ppermute | solution.py:368
  96.5 0.1 collective-permute-start.18
  96.6 0.0 collective-permute-start.17
  96.6 8.2 %shard_map.99 = f32[8,4,256]{2,1,0:T(4,128)S(1)} custom-call(s32[32,16]{1,0:T(8,128)S(1)} %fusion.33.lists.w_lists, s32[32,16]{1,0:T(8,128)S(1)} %fusion.33.lists.w_lists, bf16[96,256,128]{2,1,0:T(8,128)(2,1)S(1)} %get-tuple-element.45.sources, bf16[32,128,256]{2,1,0:T(8,128)(2,1)S(1)} %get-tuple-element.46.targets, ...), custom_call_target="tpu_custom_call" | custom-call | flops 8589934592 | bytes 1048576 | tf_op jit(solution)/shard_map/pallas_call | solution.py:227
  104.8 0.1 pad_maximum_fusion.5.table
  105.0 6.5 %shard_map.98 = (bf16[256,128,128]{2,1,0:T(8,128)(2,1)S(1)}, bf16[296,4,128]{2,1,0:T(4,128)(2,1)S(1)}) custom-call(s32[1]{0:T(128)} %bitcast.place, s32[128]{0:T(128)S(1)} %fusion.57.spots, bf16[64,48,128]{2,1,0:T(8,128)(2,1)S(1)} %pad_maximum_fusion.own_roots, bf16[64,48,128]{2,1,0:T(8,128)(2,1)S(1)} %collective-permute-done.17.other_roots, ...), custom_call_target="tpu_custom_call" | custom-call | tf_op jit(solution)/shard_map/pallas_call | solution.py:312
  111.5 55.3 %shard_map.100 = f32[32,4,256]{2,1,0:T(4,128)} custom-call(s32[32,32]{1,0:T(8,128)S(1)} %copy-done.1, s32[32,32]{1,0:T(8,128)S(1)} %fusion.7.w_lists, bf16[256,128,128]{2,1,0:T(8,128)(2,1)S(1)} %get-tuple-element.65.sources, bf16[32,128,256]{2,1,0:T(8,128)(2,1)S(1)} %get-tuple-element.46.targets, bf16[296,4,128]{2,1,0:T(4,128)(2,1)S(1)} %get-tuple-element.66.ws, ...), custom_call_target="tpu_custom_call" | custom-call | flops 34359738368 | bytes 1048576 | tf_op jit(solution)/shard_map/pallas_call | solution.py:227
  (34 shorter events, 0.4 us)
Async XLA Ops:
  0.0 55.8 %copy-start = (bf16[32,32,256]{2,1,0:T(8,128)(2,1)S(1)}, bf16[32,32,256]{2,1,0:T(8,128)(2,1)}, u32[]{:S(2)}) copy-start(bf16[32,32,256]{2,1,0:T(8,128)(2,1)} %points.3) | copy-start | bytes 1572868
  0.0 55.7 %collective-permute-start.4 = (bf16[32,32,256]{2,1,0:T(8,128)(2,1)}, bf16[32,32,256]{2,1,0:T(8,128)(2,1)S(1)}, u32[]{:S(2)}, u32[]{:S(2)}) collective-permute-start(bf16[32,32,256]{2,1,0:T(8,128)(2,1)} %points.3), channel_id=1, source_target_pairs={{0,1},{1,0},{2,3},{3,2},{4,5},{5,4},{6,7},{7,6},{8,9},{9,8},{10,11... | collective-permute-start | bytes 1572872 | tf_op jit(solution)/shard_map/ppermute | solution.py:391
  0.0 55.7 %collective-permute-start.5 = (bf16[32,32,256]{2,1,0:T(8,128)(2,1)}, bf16[32,32,256]{2,1,0:T(8,128)(2,1)S(1)}, u32[]{:S(2)}, u32[]{:S(2)}) collective-permute-start(bf16[32,32,256]{2,1,0:T(8,128)(2,1)} %points.3), channel_id=1, source_target_pairs={{1,2},{3,4},{5,6},{7,8},{9,10},{11,12},{13,14},{15,16},{17,18},{19... | collective-permute-start | bytes 1572872 | tf_op jit(solution)/shard_map/ppermute | solution.py:389
  0.8 44.2 %collective-permute-start.6 = (bf16[32,4,256]{2,1,0:T(4,128)(2,1)}, bf16[32,4,256]{2,1,0:T(4,128)(2,1)S(1)}, u32[]{:S(2)}, u32[]{:S(2)}) collective-permute-start(bf16[32,4,256]{2,1,0:T(4,128)(2,1)} %weights.1), channel_id=1, source_target_pairs={{0,1},{1,0},{2,3},{3,2},{4,5},{5,4},{6,7},{7,6},{8,9},{9,8},{10,11... | collective-permute-start | bytes 196616 | tf_op jit(solution)/shard_map/ppermute | solution.py:392
  3.8 45.5 %collective-permute-start.7 = (bf16[32,4,256]{2,1,0:T(4,128)(2,1)}, bf16[32,4,256]{2,1,0:T(4,128)(2,1)S(1)}, u32[]{:S(2)}, u32[]{:S(2)}) collective-permute-start(bf16[32,4,256]{2,1,0:T(4,128)(2,1)} %weights.1), channel_id=1, source_target_pairs={{1,2},{3,4},{5,6},{7,8},{9,10},{11,12},{13,14},{15,16},{17,18},{19... | collective-permute-start | bytes 196616 | tf_op jit(solution)/shard_map/ppermute | solution.py:390
  8.6 12.4 %collective-permute-start.1 = (bf16[1,48,128]{2,1,0:T(8,128)(2,1)}, bf16[1,48,128]{2,1,0:T(8,128)(2,1)S(1)}, u32[]{:S(2)}, u32[]{:S(2)}) collective-permute-start(bf16[1,48,128]{2,1,0:T(8,128)(2,1)} %get-tuple-element.39), channel_id=1, source_target_pairs={{0,64},{1,65},{2,66},{3,67},{4,68},{5,69},{6,70},{7,71},{8,72},{9,... | collective-permute-start | bytes 36872 | tf_op jit(solution)/shard_map/ppermute | solution.py:368
  21.1 8.6 %collective-permute-start = (bf16[1,128,256]{2,1,0:T(8,128)(2,1)}, bf16[1,128,256]{2,1,0:T(8,128)(2,1)S(1)}, u32[]{:S(2)}, u32[]{:S(2)}) collective-permute-start(bf16[1,128,256]{2,1,0:T(8,128)(2,1)} %param.13), channel_id=1, source_target_pairs={{0,127},{1,95},{2,31},{3,63},{4,23},{5,55},{6,87},{7,119},{8,7},{9... | collective-permute-start | bytes 196616 | tf_op jit(solution)/shard_map/ppermute | solution.py:388
  30.3 13.1 %collective-permute-start.2 = (bf16[2,48,128]{2,1,0:T(8,128)(2,1)S(1)}, bf16[2,48,128]{2,1,0:T(8,128)(2,1)S(1)}, u32[]{:S(2)}, u32[]{:S(2)}) collective-permute-start(bf16[2,48,128]{2,1,0:T(8,128)(2,1)S(1)} %pad_maximum_fusion.15), channel_id=1, source_target_pairs={{0,32},{1,33},{2,34},{3,35},{4,36},{5,37},{6,38},{7,39},{8,40},{9,... | collective-permute-start | bytes 73736 | tf_op jit(solution)/shard_map/ppermute | solution.py:368
  43.5 5.7 %collective-permute-start.3 = (bf16[4,48,128]{2,1,0:T(8,128)(2,1)S(1)}, bf16[4,48,128]{2,1,0:T(8,128)(2,1)S(1)}, u32[]{:S(2)}, u32[]{:S(2)}) collective-permute-start(bf16[4,48,128]{2,1,0:T(8,128)(2,1)S(1)} %pad_maximum_fusion.12), channel_id=1, source_target_pairs={{0,4},{1,5},{2,6},{3,7},{4,0},{5,1},{6,2},{7,3},{8,12},{9,13},{10,... | collective-permute-start | bytes 147464 | tf_op jit(solution)/shard_map/ppermute | solution.py:368
  49.2 3.8 %collective-permute-start.8 = (bf16[1,9,4,128]{3,2,1,0:T(4,128)(2,1)S(1)}, bf16[1,9,4,128]{3,2,1,0:T(4,128)(2,1)S(1)}, u32[]{:S(2)}, u32[]{:S(2)}) collective-permute-start(bf16[1,9,4,128]{3,2,1,0:T(4,128)(2,1)S(1)} %shard_map.92), channel_id=1, source_target_pairs={{0,8},{1,9},{2,10},{3,11},{4,12},{5,13},{6,14},{7,15},{8,0},{9,1},... | collective-permute-start | bytes 27656 | tf_op jit(solution)/shard_map/ppermute | solution.py:368
  49.3 6.4 %collective-permute-start.10 = (bf16[8,48,128]{2,1,0:T(8,128)(2,1)S(1)}, bf16[8,48,128]{2,1,0:T(8,128)(2,1)S(1)}, u32[]{:S(2)}, u32[]{:S(2)}) collective-permute-start(bf16[8,48,128]{2,1,0:T(8,128)(2,1)S(1)} %pad_maximum_fusion.9), channel_id=1, source_target_pairs={{0,8},{1,9},{2,10},{3,11},{4,12},{5,13},{6,14},{7,15},{8,0},{9,1},... | collective-permute-start | bytes 294920 | tf_op jit(solution)/shard_map/ppermute | solution.py:368
  51.4 4.3 %collective-permute-start.9 = (bf16[1,256,128]{2,1,0:T(8,128)(2,1)S(1)}, bf16[1,256,128]{2,1,0:T(8,128)(2,1)S(1)}, u32[]{:S(2)}, u32[]{:S(2)}) collective-permute-start(bf16[1,256,128]{2,1,0:T(8,128)(2,1)S(1)} %slice.11), channel_id=1, source_target_pairs={{0,8},{1,9},{2,10},{3,11},{4,12},{5,13},{6,14},{7,15},{8,0},{9,1},... | collective-permute-start | bytes 196616 | tf_op jit(solution)/shard_map/ppermute | solution.py:368
  66.3 15.5 %collective-permute-start.13 = (bf16[16,48,128]{2,1,0:T(8,128)(2,1)S(1)}, bf16[16,48,128]{2,1,0:T(8,128)(2,1)S(1)}, u32[]{:S(2)}, u32[]{:S(2)}) collective-permute-start(bf16[16,48,128]{2,1,0:T(8,128)(2,1)S(1)} %pad_maximum_fusion.4), channel_id=1, source_target_pairs={{0,16},{1,17},{2,18},{3,19},{4,20},{5,21},{6,22},{7,23},{8,24},{9,... | collective-permute-start | bytes 589832 | tf_op jit(solution)/shard_map/ppermute | solution.py:368
  69.9 11.8 %collective-permute-start.12 = (bf16[2,256,128]{2,1,0:T(8,128)(2,1)S(1)}, bf16[2,256,128]{2,1,0:T(8,128)(2,1)S(1)}, u32[]{:S(2)}, u32[]{:S(2)}) collective-permute-start(bf16[2,256,128]{2,1,0:T(8,128)(2,1)S(1)} %pad_maximum_fusion.6), channel_id=1, source_target_pairs={{0,16},{1,17},{2,18},{3,19},{4,20},{5,21},{6,22},{7,23},{8,24},{9,... | collective-permute-start | bytes 393224 | tf_op jit(solution)/shard_map/ppermute | solution.py:368
  70.0 11.6 %collective-permute-start.11 = (bf16[2,9,4,128]{3,2,1,0:T(4,128)(2,1)S(1)}, bf16[2,9,4,128]{3,2,1,0:T(4,128)(2,1)S(1)}, u32[]{:S(2)}, u32[]{:S(2)}) collective-permute-start(bf16[2,9,4,128]{3,2,1,0:T(4,128)(2,1)S(1)} %pad_maximum_fusion.16), channel_id=1, source_target_pairs={{0,16},{1,17},{2,18},{3,19},{4,20},{5,21},{6,22},{7,23},{8,24},{9,... | collective-permute-start | bytes 55304 | tf_op jit(solution)/shard_map/ppermute | solution.py:368
  82.2 10.6 %collective-permute-start.16 = (bf16[32,48,128]{2,1,0:T(8,128)(2,1)S(1)}, bf16[32,48,128]{2,1,0:T(8,128)(2,1)S(1)}, u32[]{:S(2)}, u32[]{:S(2)}) collective-permute-start(bf16[32,48,128]{2,1,0:T(8,128)(2,1)S(1)} %pad_maximum_fusion.1), channel_id=1, source_target_pairs={{0,2},{1,3},{2,0},{3,1},{4,6},{5,7},{6,4},{7,5},{8,10},{9,11},{10,... | collective-permute-start | bytes 1179656 | tf_op jit(solution)/shard_map/ppermute | solution.py:368
  82.2 10.4 %collective-permute-start.15 = (bf16[1,256,128]{2,1,0:T(8,128)(2,1)S(1)}, bf16[1,256,128]{2,1,0:T(8,128)(2,1)S(1)}, u32[]{:S(2)}, u32[]{:S(2)}) collective-permute-start(bf16[1,256,128]{2,1,0:T(8,128)(2,1)S(1)} %constant_dynamic-slice_fusion), channel_id=1, source_target_pairs={{0,32},{1,33},{2,34},{3,35},{4,36},{5,37},{6,38},{7,39},{8,40},{9,... | collective-permute-start | bytes 196616 | tf_op jit(solution)/shard_map/ppermute | solution.py:368
  84.3 8.3 %collective-permute-start.14 = (bf16[1,41,4,128]{3,2,1,0:T(4,128)(2,1)S(1)}, bf16[1,41,4,128]{3,2,1,0:T(4,128)(2,1)S(1)}, u32[]{:S(2)}, u32[]{:S(2)}) collective-permute-start(bf16[1,41,4,128]{3,2,1,0:T(4,128)(2,1)S(1)} %pad_maximum_fusion.13), channel_id=1, source_target_pairs={{0,32},{1,33},{2,34},{3,35},{4,36},{5,37},{6,38},{7,39},{8,40},{9,... | collective-permute-start | bytes 125960 | tf_op jit(solution)/shard_map/ppermute | solution.py:368
  92.8 18.7 %copy-start.1 = (s32[32,32]{1,0:T(8,128)S(1)}, s32[32,32]{1,0:T(8,128)}, u32[]{:S(2)}) copy-start(s32[32,32]{1,0:T(8,128)} %lists.1) | copy-start | bytes 12292
  92.8 12.1 %collective-permute-start.19 = (bf16[2,256,128]{2,1,0:T(8,128)(2,1)S(1)}, bf16[2,256,128]{2,1,0:T(8,128)(2,1)S(1)}, u32[]{:S(2)}, u32[]{:S(2)}) collective-permute-start(bf16[2,256,128]{2,1,0:T(8,128)(2,1)S(1)} %pad_maximum_fusion.7), channel_id=1, source_target_pairs={{0,64},{1,65},{2,66},{3,67},{4,68},{5,69},{6,70},{7,71},{8,72},{9,... | collective-permute-start | bytes 393224 | tf_op jit(solution)/shard_map/ppermute | solution.py:368
  96.5 8.3 %collective-permute-start.18 = (bf16[2,41,4,128]{3,2,1,0:T(4,128)(2,1)S(1)}, bf16[2,41,4,128]{3,2,1,0:T(4,128)(2,1)S(1)}, u32[]{:S(2)}, u32[]{:S(2)}) collective-permute-start(bf16[2,41,4,128]{3,2,1,0:T(4,128)(2,1)S(1)} %pad_maximum_fusion.10), channel_id=1, source_target_pairs={{0,64},{1,65},{2,66},{3,67},{4,68},{5,69},{6,70},{7,71},{8,72},{9,... | collective-permute-start | bytes 251912 | tf_op jit(solution)/shard_map/ppermute | solution.py:368
  96.6 8.4 %collective-permute-start.17 = (bf16[64,48,128]{2,1,0:T(8,128)(2,1)S(1)}, bf16[64,48,128]{2,1,0:T(8,128)(2,1)S(1)}, u32[]{:S(2)}, u32[]{:S(2)}) collective-permute-start(bf16[64,48,128]{2,1,0:T(8,128)(2,1)S(1)} %pad_maximum_fusion.own_roots), channel_id=1, source_target_pairs={{0,1},{1,0},{2,3},{3,2},{4,5},{5,4},{6,7},{7,6},{8,9},{9,8},{10,11... | collective-permute-start | bytes 2359304 | tf_op jit(solution)/shard_map/ppermute | solution.py:368
where the time goes:
time: 169 us; the launch traced here: 167 us
  Pallas kernels  102 us (60%)
  starting transfers between devices  36.8 us (22%)
  blocking collectives  13.1 us (8%)
  waiting for transfers between devices  10.3 us (6%)
  other arithmetic  2.8 us (2%)
  local copies, waits for them, and re-layouts  1.74 us (1%)
    pallas_call x5, Pallas kernels, field(): pl.pallas_call(functools.partial(field_kernel, 4, 1024 // columns, start)...  88 us
    ppermute x15, starting transfers between devices, swap(): return lax.ppermute(x, 'leaf', [(i, i ^ mask) for i in range(size)])  26.9 us
    all_gather x1, blocking collectives, on_device(): lax.all_gather(held, 'leaf', axis=0, tiled=True, axis_index_groups=groups)  13.1 us
    ppermute x15, waiting for transfers between devices, swap(): return lax.ppermute(x, 'leaf', [(i, i ^ mask) for i in range(size)])  7.81 us
    pallas_call x1, Pallas kernels, far_tables(): pl.pallas_call(tables_kernel, in_specs=[SMEM] * 2 + [VMEM] * 4, out_specs...  6.51 us
    ppermute x1, starting transfers between devices, on_device(): lax.ppermute(top_maps, 'leaf', [(n, home_of(n)) for n in range(size)])  5.45 us
    pallas_call x1, Pallas kernels, upward(): pl.pallas_call(upward_kernel, in_specs=[VMEM] * 6, out_specs=[VMEM] * 2,...  4.12 us
  transfers between devices with their start and end apart: 20, of which 4 were waited for; matrix products, arithmetic and copies ran while one was open for 3% of the time, Pallas kernels for 17%

commit v1 on v0

--- a/solution.py
+++ b/solution.py
@@ -169,31 +169,41 @@
     )(place, groups, maps)
 
 
-def forms_kernel(points, first, second, sources, targets):
-    per = points.shape[0]
-    for i, ref in enumerate((points, first, second)):
-
-        def prepare(g, carry, i=i, ref=ref):
-            sources[i * per + g] = source_form(ref[g])
-            if i == 0:
-                targets[g] = target_form(ref[g])
+def forms_kernel(own, first, second, w_own, w_first, w_second, sources, targets, ws):
+    per = own.shape[0]
+    refs = ((own, w_own), (first, w_first), (second, w_second))
+    for i, (ref, w_ref) in enumerate(refs):
+
+        def prepare(step, carry, i=i, ref=ref, w_ref=w_ref):
+            found = []
+            for u in range(16):
+                x = ref[step * 16 + u]
+                found.append((source_form(x), target_form(x) if i == 0 else None))
+            for u in range(16):
+                g = step * 16 + u
+                sources[i * per + g] = found[u][0]
+                ws[i * per + g] = w_ref[g]
+                if i == 0:
+                    targets[g] = found[u][1]
             return carry
 
-        lax.fori_loop(0, per, prepare, 0, unroll=16)
-
-
-def forms(points, first, second):
-    per, dims, leaf_size = points.shape
+        lax.fori_loop(0, per // 16, prepare, 0)
+
+
+def forms(points, weights):
+    per, _, leaf_size = points[0].shape
+    rhs = weights[0].shape[1]
     return pl.pallas_call(
         forms_kernel,
-        in_specs=[VMEM] * 3,
-        out_specs=[VMEM] * 2,
+        in_specs=[VMEM] * 6,
+        out_specs=[VMEM] * 3,
         out_shape=[
             jax.ShapeDtypeStruct((3 * per, leaf_size, WIDE), bf16),
             jax.ShapeDtypeStruct((per, WIDE, leaf_size), bf16),
+            jax.ShapeDtypeStruct((3 * per, rhs, leaf_size), bf16),
         ],
         compiler_params=params(24),
-    )(points, first, second)
+    )(*points, *weights)
 
 
 def field_kernel(unroll, together, start, lists, w_lists, sources, targets, ws, *rest):
@@ -205,7 +215,7 @@
         for u in range(unroll):
             g = start + step * unroll + u
             target = targets[g]
-            total = rest[0][g] if len(rest) > 1 else jnp.zeros(out.shape[1:], f32)
+            total = jnp.zeros(out.shape[1:], f32)
             for j in range(0, entries, together):
                 total = total + blocks_apply(
                     target,
@@ -214,10 +224,13 @@
                 )
             totals.append(total)
         for u in range(unroll):
-            out[step * unroll + u] = totals[u]
+            at = step * unroll + u
+            out[at] = totals[u]
         return carry
 
     lax.fori_loop(0, out.shape[0] // unroll, leaves, 0)
+    if len(rest) > 1:
+        out[...] = out[...] + rest[0][...]
 
 
 def field(start, count, lists, w_lists, sources, targets, ws, *init):
@@ -386,16 +399,17 @@
     bridges = [(i, i + 1) for i in range(1, size - 1, 2)]
     bridges = bridges + [(j, i) for i, j in bridges]
     maps = lax.ppermute(top_maps, "leaf", [(n, home_of(n)) for n in range(size)])
+    first = lax.ppermute(points, "leaf", pairs)
+    w_first = lax.ppermute(weights, "leaf", pairs)
     second = lax.ppermute(points, "leaf", bridges)
     w_second = lax.ppermute(weights, "leaf", bridges)
-    first = lax.ppermute(points, "leaf", pairs)
-    w_first = lax.ppermute(weights, "leaf", pairs)
 
     root, root_w = upward(points, weights, leaf_maps, root_maps, root_picks, top_picks)
 
     def more(root, step):
         return both(root, ROOT_STEPS[step], size)
 
+    root, maps = lax.optimization_barrier((root, maps))
     root = more(root, 0)
     held = jnp.concatenate([maps[:, :, :128], maps[:, :, 128:], root_w], axis=1)
     held, root = lax.optimization_barrier((held, root))
@@ -411,8 +425,6 @@
     side = jnp.where(me % 2 == 0, jnp.where(local < 0, 2, 1), jnp.where(local < 0, 1, 2))
     inside = jnp.logical_and(local >= 0, local < per)
     slots = jnp.where(inside, local, side * per + local % per)
-    sources, targets = forms(points, first, second)
-    ws = jnp.concatenate([weights, w_first, w_second], axis=0)
 
     parts = 4
     nears = []
@@ -420,7 +432,10 @@
     def near_part(k, slots):
         return field(k * (per // parts), per // parts, slots, slots, sources, targets, ws)
 
-    slots, group_nodes, spare, root = lax.optimization_barrier((slots, group_nodes, spare, root))
+    sources, targets, ws = forms((points, first, second), (weights, w_first, w_second))
+    slots, sources, group_nodes, spare, root = lax.optimization_barrier(
+        (slots, sources, group_nodes, spare, root)
+    )
     groups, slab_maps = [both(a, 8, size) for a in (group_nodes, spare)]
     root = more(root, 3)
     nears.append(near_part(0, slots))

time: 169 us -> 137 us (0.81)
  Pallas kernels: 102 us -> 76.7 us
  waiting for transfers between devices: 10.3 us -> 6.49 us
  starting transfers between devices: 36.8 us -> 33.3 us
    pallas_call x5, Pallas kernels: 88 us -> 63.1 us  [field(): pl.pallas_call(functools.partial(field_kernel, 4, 1024 // columns, start)...]
    ppermute x15, starting transfers between devices: 26.9 us -> 20.8 us  [swap(): return lax.ppermute(x, 'leaf', [(i, i ^ mask) for i in range(size)])]
    ppermute x1, starting transfers between devices: 5.45 us -> 8.2 us  [on_device(): lax.ppermute(top_maps, 'leaf', [(n, home_of(n)) for n in range(size)])]
    ppermute x1, waiting for transfers between devices: 2.44 us -> 0.01 us  [on_device(): lax.ppermute(top_maps, 'leaf', [(n, home_of(n)) for n in range(size)])]
  transfers between devices with their start and end apart: 20 -> 20, of which waited for: 4 -> 2; matrix products, arithmetic and copies ran while one was open for 3% -> 3% of each run, Pallas kernels for 17% -> 27%
where the time goes in v1:
time: 137 us; the launch traced here: 136 us
  Pallas kernels  76.7 us (56%)
  starting transfers between devices  33.3 us (24%)
  blocking collectives  13.3 us (10%)
  waiting for transfers between devices  6.49 us (5%)
  other arithmetic  2.82 us (2%)
  local copies, waits for them, and re-layouts  2.68 us (2%)
    pallas_call x5, Pallas kernels, field(): pl.pallas_call(functools.partial(field_kernel, 4, 1024 // columns, start)...  63.1 us
    ppermute x15, starting transfers between devices, swap(): return lax.ppermute(x, 'leaf', [(i, i ^ mask) for i in range(size)])  20.8 us
    all_gather x1, blocking collectives, on_device(): lax.all_gather(held, 'leaf', axis=0, tiled=True, axis_index_groups=groups)  13.3 us
    ppermute x1, starting transfers between devices, on_device(): lax.ppermute(top_maps, 'leaf', [(n, home_of(n)) for n in range(size)])  8.2 us
    pallas_call x1, Pallas kernels, far_tables(): pl.pallas_call(tables_kernel, in_specs=[SMEM] * 2 + [VMEM] * 4, out_specs...  6.5 us
    ppermute x15, waiting for transfers between devices, swap(): return lax.ppermute(x, 'leaf', [(i, i ^ mask) for i in range(size)])  6.47 us
    pallas_call x1, Pallas kernels, upward(): pl.pallas_call(upward_kernel, in_specs=[VMEM] * 6, out_specs=[VMEM] * 2,...  4.13 us
    ppermute x1, starting transfers between devices, on_device(): w_first = lax.ppermute(weights, 'leaf', pairs)  2.99 us
  transfers between devices with their start and end apart: 20, of which 2 were waited for; matrix products, arithmetic and copies ran while one was open for 3% of the time, Pallas kernels for 27%

profile of v1, /device:TPU:0, one launch (start us, length us, event | category | flops | bytes accessed | tf_op | source)
XLA Modules:
  0.0 135.6 jit_solution(2170330931566466134)
XLA Ops:
  0.0 0.7 collective-permute-start.1
  0.7 3.0 %collective-permute-start.2 = (bf16[32,4,256]{2,1,0:T(4,128)(2,1)}, bf16[32,4,256]{2,1,0:T(4,128)(2,1)S(1)}, u32[]{:S(2)}, u32[]{:S(2)}) collective-permute-start(bf16[32,4,256]{2,1,0:T(4,128)(2,1)} %weights.1), channel_id=1, source_target_pairs={{0,1},{1,0},{2,3},{3,2},{4,5},{5,4},{6,7},{7,6},{8,9},{9,8},{10,11... | collective-permute-start | bytes 196616 | tf_op jit(solution)/shard_map/ppermute | solution.py:403
  3.7 0.7 collective-permute-start.3
  4.3 8.2 %collective-permute-start.4 = (bf16[1,128,256]{2,1,0:T(8,128)(2,1)}, bf16[1,128,256]{2,1,0:T(8,128)(2,1)S(1)}, u32[]{:S(2)}, u32[]{:S(2)}) collective-permute-start(bf16[1,128,256]{2,1,0:T(8,128)(2,1)} %param.13), channel_id=1, source_target_pairs={{0,127},{1,95},{2,31},{3,63},{4,23},{5,55},{6,87},{7,119},{8,7},{9... | collective-permute-start | bytes 196616 | tf_op jit(solution)/shard_map/ppermute | solution.py:401
  12.5 0.8 copy.11
  13.3 0.8 fusion.7.w_lists
  14.2 4.1 %shard_map.92 = (bf16[1,48,128]{2,1,0:T(8,128)(2,1)}, bf16[1,16,128]{2,1,0:T(8,128)(2,1)}) custom-call(bf16[32,32,256]{2,1,0:T(8,128)(2,1)} %points.1, bf16[32,4,256]{2,1,0:T(4,128)(2,1)} %weights.1, bf16[32,128,256]{2,1,0:T(8,128)(2,1)} %leaf_maps.1, bf16[1,128,4096]{2,1,0:T(8,128)(2,1)} %root_maps.1, s32[1,128]{1,0:T(1,128)} %picks.1, s32[1,128]{1,0:T(1,128)} %top_picks.1), custom_call_target="tpu_custom_call" | custom-call | tf_op jit(solution)/shard_map/pallas_call | solution.py:97
  18.3 0.0 collective-permute-done.4
  18.3 2.0 %collective-permute-start.5 = (bf16[1,48,128]{2,1,0:T(8,128)(2,1)}, bf16[1,48,128]{2,1,0:T(8,128)(2,1)S(1)}, u32[]{:S(2)}, u32[]{:S(2)}) collective-permute-start(bf16[1,48,128]{2,1,0:T(8,128)(2,1)} %get-tuple-element.46), channel_id=1, source_target_pairs={{0,64},{1,65},{2,66},{3,67},{4,68},{5,69},{6,70},{7,71},{8,72},{9,... | collective-permute-start | bytes 36872 | tf_op jit(solution)/shard_map/ppermute | solution.py:381
  20.3 0.7 pad_maximum_fusion.11
  21.0 2.8 %collective-permute-done.5 = bf16[1,48,128]{2,1,0:T(8,128)(2,1)S(1)} collective-permute-done((bf16[1,48,128]{2,1,0:T(8,128)(2,1)}, bf16[1,48,128]{2,1,0:T(8,128)(2,1)S(1)}, u32[]{:S(2)}, u32[]{:S(2)}) %collective-permute-start.5) | collective-permute-done | bytes 12320 | tf_op jit(solution)/shard_map/ppermute | solution.py:381
  23.8 0.7 pad_maximum_fusion.15
  24.5 2.2 %collective-permute-start.6 = (bf16[2,48,128]{2,1,0:T(8,128)(2,1)S(1)}, bf16[2,48,128]{2,1,0:T(8,128)(2,1)S(1)}, u32[]{:S(2)}, u32[]{:S(2)}) collective-permute-start(bf16[2,48,128]{2,1,0:T(8,128)(2,1)S(1)} %pad_maximum_fusion.15), channel_id=1, source_target_pairs={{0,32},{1,33},{2,34},{3,35},{4,36},{5,37},{6,38},{7,39},{8,40},{9,... | collective-permute-start | bytes 73736 | tf_op jit(solution)/shard_map/ppermute | solution.py:381
  26.7 13.3 %all_gather.3.held = bf16[8,272,128]{2,1,0:T(8,128)(2,1)S(1)} all-gather(bf16[1,272,128]{2,1,0:T(8,128)(2,1)S(1)} %pad_maximum_fusion.11), channel_id=1, replica_groups={{0,1,2,3,4,5,6,7},{8,9,10,11,12,13,14,15},{16,17,18,19,20,21,22,23},{24..., dimensions={0}, use_global_device_ids=true | all-gather | bytes 626688 | tf_op jit(solution)/shard_map/all_gather | solution.py:417
  40.0 0.0 collective-permute-done.6
  40.1 1.5 %collective-permute-start.7 = (bf16[4,48,128]{2,1,0:T(8,128)(2,1)S(1)}, bf16[4,48,128]{2,1,0:T(8,128)(2,1)S(1)}, u32[]{:S(2)}, u32[]{:S(2)}) collective-permute-start(bf16[4,48,128]{2,1,0:T(8,128)(2,1)S(1)} %pad_maximum_fusion.12), channel_id=1, source_target_pairs={{0,4},{1,5},{2,6},{3,7},{4,0},{5,1},{6,2},{7,3},{8,12},{9,13},{10,... | collective-permute-start | bytes 147464 | tf_op jit(solution)/shard_map/ppermute | solution.py:381
  41.6 0.4 shard_map.93
  42.1 3.6 %collective-permute-done.7 = bf16[4,48,128]{2,1,0:T(8,128)(2,1)S(1)} collective-permute-done((bf16[4,48,128]{2,1,0:T(8,128)(2,1)S(1)}, bf16[4,48,128]{2,1,0:T(8,128)(2,1)S(1)}, u32[]{:S(2)}, u32[]{:S(2)}) %collective-permute-start.7) | collective-permute-done | bytes 49184 | tf_op jit(solution)/shard_map/ppermute | solution.py:381
  45.8 0.0 collective-permute-done.3.w_second
  45.8 0.0 copy-start
  45.8 1.0 copy-done
  46.8 0.8 copy-done.1
  47.7 2.2 %shard_map.91 = (bf16[96,256,128]{2,1,0:T(8,128)(2,1)S(1)}, bf16[32,128,256]{2,1,0:T(8,128)(2,1)S(1)}, bf16[96,4,256]{2,1,0:T(4,128)(2,1)S(1)}) custom-call(bf16[32,32,256]{2,1,0:T(8,128)(2,1)S(1)} %copy-done, bf16[32,32,256]{2,1,0:T(8,128)(2,1)S(1)} %collective-permute-done.first, bf16[32,32,256]{2,1,0:T(8,128)(2,1)S(1)} %collective-permute-done.1.second, ...), custom_call_target="tpu_custom_call" | custom-call | tf_op jit(solution)/shard_map/pallas_call | solution.py:196
  49.9 0.6 collective-permute-start.10
  50.5 1.5 %collective-permute-start.9 = (bf16[1,256,128]{2,1,0:T(8,128)(2,1)S(1)}, bf16[1,256,128]{2,1,0:T(8,128)(2,1)S(1)}, u32[]{:S(2)}, u32[]{:S(2)}) collective-permute-start(bf16[1,256,128]{2,1,0:T(8,128)(2,1)S(1)} %slice.11), channel_id=1, source_target_pairs={{0,8},{1,9},{2,10},{3,11},{4,12},{5,13},{6,14},{7,15},{8,0},{9,1},... | collective-permute-start | bytes 196616 | tf_op jit(solution)/shard_map/ppermute | solution.py:381
  52.0 0.5 collective-permute-start.8
  52.6 8.2 %shard_map.94 = f32[8,4,256]{2,1,0:T(4,128)S(1)} custom-call(s32[32,16]{1,0:T(8,128)S(1)} %fusion.33.lists.w_lists, s32[32,16]{1,0:T(8,128)S(1)} %fusion.33.lists.w_lists, bf16[96,256,128]{2,1,0:T(8,128)(2,1)S(1)} %get-tuple-element.52.sources, bf16[32,128,256]{2,1,0:T(8,128)(2,1)S(1)} %get-tuple-element.53.targets, bf16[96,4,256]{2,1,0:T(4,128)(2,1)S(1)} %get-tuple-element.54.ws), custom_call_target="tpu_custom_call" | custom-call | flops 8589934592 | bytes 1048576 | tf_op jit(solution)/shard_map/pallas_call | solution.py:240
  60.8 0.0 collective-permute-done.9
  60.8 0.0 collective-permute-done.10
  60.9 3.0 %collective-permute-start.13 = (bf16[16,48,128]{2,1,0:T(8,128)(2,1)S(1)}, bf16[16,48,128]{2,1,0:T(8,128)(2,1)S(1)}, u32[]{:S(2)}, u32[]{:S(2)}) collective-permute-start(bf16[16,48,128]{2,1,0:T(8,128)(2,1)S(1)} %pad_maximum_fusion.4), channel_id=1, source_target_pairs={{0,16},{1,17},{2,18},{3,19},{4,20},{5,21},{6,22},{7,23},{8,24},{9,... | collective-permute-start | bytes 589832 | tf_op jit(solution)/shard_map/ppermute | solution.py:381
  63.8 0.6 collective-permute-start.12
  64.5 2.9 %collective-permute-start.11 = (bf16[2,9,4,128]{3,2,1,0:T(4,128)(2,1)S(1)}, bf16[2,9,4,128]{3,2,1,0:T(4,128)(2,1)S(1)}, u32[]{:S(2)}, u32[]{:S(2)}) collective-permute-start(bf16[2,9,4,128]{3,2,1,0:T(4,128)(2,1)S(1)} %pad_maximum_fusion.16), channel_id=1, source_target_pairs={{0,16},{1,17},{2,18},{3,19},{4,20},{5,21},{6,22},{7,23},{8,24},{9,... | collective-permute-start | bytes 55304 | tf_op jit(solution)/shard_map/ppermute | solution.py:381
  67.4 8.2 %shard_map.95 = f32[8,4,256]{2,1,0:T(4,128)S(1)} custom-call(s32[32,16]{1,0:T(8,128)S(1)} %fusion.33.lists.w_lists, s32[32,16]{1,0:T(8,128)S(1)} %fusion.33.lists.w_lists, bf16[96,256,128]{2,1,0:T(8,128)(2,1)S(1)} %get-tuple-element.52.sources, bf16[32,128,256]{2,1,0:T(8,128)(2,1)S(1)} %get-tuple-element.53.targets, bf16[96,4,256]{2,1,0:T(4,128)(2,1)S(1)} %get-tuple-element.54.ws), custom_call_target="tpu_custom_call" | custom-call | flops 8589934592 | bytes 1048576 | tf_op jit(solution)/shard_map/pallas_call | solution.py:240
  75.7 0.3 shard_map.96
  76.0 0.2 collective-permute-start.16
  76.2 2.0 %collective-permute-start.15 = (bf16[1,256,128]{2,1,0:T(8,128)(2,1)S(1)}, bf16[1,256,128]{2,1,0:T(8,128)(2,1)S(1)}, u32[]{:S(2)}, u32[]{:S(2)}) collective-permute-start(bf16[1,256,128]{2,1,0:T(8,128)(2,1)S(1)} %constant_dynamic-slice_fusion), channel_id=1, source_target_pairs={{0,32},{1,33},{2,34},{3,35},{4,36},{5,37},{6,38},{7,39},{8,40},{9,... | collective-permute-start | bytes 196616 | tf_op jit(solution)/shard_map/ppermute | solution.py:381
  78.2 0.1 collective-permute-start.14
  78.3 8.2 %shard_map.97 = f32[8,4,256]{2,1,0:T(4,128)S(1)} custom-call(s32[32,16]{1,0:T(8,128)S(1)} %fusion.33.lists.w_lists, s32[32,16]{1,0:T(8,128)S(1)} %fusion.33.lists.w_lists, bf16[96,256,128]{2,1,0:T(8,128)(2,1)S(1)} %get-tuple-element.52.sources, bf16[32,128,256]{2,1,0:T(8,128)(2,1)S(1)} %get-tuple-element.53.targets, bf16[96,4,256]{2,1,0:T(4,128)(2,1)S(1)} %get-tuple-element.54.ws), custom_call_target="tpu_custom_call" | custom-call | flops 8589934592 | bytes 1048576 | tf_op jit(solution)/shard_map/pallas_call | solution.py:240
  86.5 0.1 pad_maximum_fusion.10
  86.6 0.1 pad_maximum_fusion.own_roots
  86.7 0.0 copy-start.2
  86.7 2.6 %collective-permute-start.19 = (bf16[2,256,128]{2,1,0:T(8,128)(2,1)S(1)}, bf16[2,256,128]{2,1,0:T(8,128)(2,1)S(1)}, u32[]{:S(2)}, u32[]{:S(2)}) collective-permute-start(bf16[2,256,128]{2,1,0:T(8,128)(2,1)S(1)} %pad_maximum_fusion.7), channel_id=1, source_target_pairs={{0,64},{1,65},{2,66},{3,67},{4,68},{5,69},{6,70},{7,71},{8,72},{9,... | collective-permute-start | bytes 393224 | tf_op jit(solution)/shard_map/ppermute | solution.py:381
  89.3 1.0 collective-permute-start.18
  90.3 0.0 collective-permute-start.17
  90.3 8.2 %shard_map.99 = f32[8,4,256]{2,1,0:T(4,128)S(1)} custom-call(s32[32,16]{1,0:T(8,128)S(1)} %fusion.33.lists.w_lists, s32[32,16]{1,0:T(8,128)S(1)} %fusion.33.lists.w_lists, bf16[96,256,128]{2,1,0:T(8,128)(2,1)S(1)} %get-tuple-element.52.sources, bf16[32,128,256]{2,1,0:T(8,128)(2,1)S(1)} %get-tuple-element.53.targets, bf16[96,4,256]{2,1,0:T(4,128)(2,1)S(1)} %get-tuple-element.54.ws), custom_call_target="tpu_custom_call" | custom-call | flops 8589934592 | bytes 1048576 | tf_op jit(solution)/shard_map/pallas_call | solution.py:240
  98.6 0.1 pad_maximum_fusion.5.table
  98.7 6.5 %shard_map.98 = (bf16[256,128,128]{2,1,0:T(8,128)(2,1)S(1)}, bf16[296,4,128]{2,1,0:T(4,128)(2,1)S(1)}) custom-call(s32[1]{0:T(128)} %bitcast.place, s32[128]{0:T(128)S(1)} %fusion.57.spots, bf16[64,48,128]{2,1,0:T(8,128)(2,1)S(1)} %pad_maximum_fusion.own_roots, bf16[64,48,128]{2,1,0:T(8,128)(2,1)S(1)} %collective-permute-done.17.other_roots, ...), custom_call_target="tpu_custom_call" | custom-call | tf_op jit(solution)/shard_map/pallas_call | solution.py:325
  105.3 30.4 %shard_map.100 = f32[32,4,256]{2,1,0:T(4,128)} custom-call(s32[32,32]{1,0:T(8,128)S(1)} %copy-done.2, s32[32,32]{1,0:T(8,128)S(1)} %fusion.7.w_lists, bf16[256,128,128]{2,1,0:T(8,128)(2,1)S(1)} %get-tuple-element.73.sources, bf16[32,128,256]{2,1,0:T(8,128)(2,1)S(1)} %get-tuple-element.53.targets, bf16[296,4,128]{2,1,0:T(4,128)(2,1)S(1)} %get-tuple-element.74.ws, ...), custom_call_target="tpu_custom_call" | custom-call | flops 34359738368 | bytes 1048576 | tf_op jit(solution)/shard_map/pallas_call | solution.py:240
  (33 shorter events, 0.4 us)
Async XLA Ops:
  0.0 45.8 %collective-permute-start = (bf16[32,32,256]{2,1,0:T(8,128)(2,1)}, bf16[32,32,256]{2,1,0:T(8,128)(2,1)S(1)}, u32[]{:S(2)}, u32[]{:S(2)}) collective-permute-start(bf16[32,32,256]{2,1,0:T(8,128)(2,1)} %points.1), channel_id=1, source_target_pairs={{0,1},{1,0},{2,3},{3,2},{4,5},{5,4},{6,7},{7,6},{8,9},{9,8},{10,11... | collective-permute-start | bytes 1572872 | tf_op jit(solution)/shard_map/ppermute | solution.py:402
  0.0 45.8 %collective-permute-start.1 = (bf16[32,32,256]{2,1,0:T(8,128)(2,1)}, bf16[32,32,256]{2,1,0:T(8,128)(2,1)S(1)}, u32[]{:S(2)}, u32[]{:S(2)}) collective-permute-start(bf16[32,32,256]{2,1,0:T(8,128)(2,1)} %points.1), channel_id=1, source_target_pairs={{1,2},{3,4},{5,6},{7,8},{9,10},{11,12},{13,14},{15,16},{17,18},{19... | collective-permute-start | bytes 1572872 | tf_op jit(solution)/shard_map/ppermute | solution.py:404
  0.7 45.1 %collective-permute-start.2 = (bf16[32,4,256]{2,1,0:T(4,128)(2,1)}, bf16[32,4,256]{2,1,0:T(4,128)(2,1)S(1)}, u32[]{:S(2)}, u32[]{:S(2)}) collective-permute-start(bf16[32,4,256]{2,1,0:T(4,128)(2,1)} %weights.1), channel_id=1, source_target_pairs={{0,1},{1,0},{2,3},{3,2},{4,5},{5,4},{6,7},{7,6},{8,9},{9,8},{10,11... | collective-permute-start | bytes 196616 | tf_op jit(solution)/shard_map/ppermute | solution.py:403
  3.7 42.1 %collective-permute-start.3 = (bf16[32,4,256]{2,1,0:T(4,128)(2,1)}, bf16[32,4,256]{2,1,0:T(4,128)(2,1)S(1)}, u32[]{:S(2)}, u32[]{:S(2)}) collective-permute-start(bf16[32,4,256]{2,1,0:T(4,128)(2,1)} %weights.1), channel_id=1, source_target_pairs={{1,2},{3,4},{5,6},{7,8},{9,10},{11,12},{13,14},{15,16},{17,18},{19... | collective-permute-start | bytes 196616 | tf_op jit(solution)/shard_map/ppermute | solution.py:405
  4.3 14.0 %collective-permute-start.4 = (bf16[1,128,256]{2,1,0:T(8,128)(2,1)}, bf16[1,128,256]{2,1,0:T(8,128)(2,1)S(1)}, u32[]{:S(2)}, u32[]{:S(2)}) collective-permute-start(bf16[1,128,256]{2,1,0:T(8,128)(2,1)} %param.13), channel_id=1, source_target_pairs={{0,127},{1,95},{2,31},{3,63},{4,23},{5,55},{6,87},{7,119},{8,7},{9... | collective-permute-start | bytes 196616 | tf_op jit(solution)/shard_map/ppermute | solution.py:401
  18.3 5.5 %collective-permute-start.5 = (bf16[1,48,128]{2,1,0:T(8,128)(2,1)}, bf16[1,48,128]{2,1,0:T(8,128)(2,1)S(1)}, u32[]{:S(2)}, u32[]{:S(2)}) collective-permute-start(bf16[1,48,128]{2,1,0:T(8,128)(2,1)} %get-tuple-element.46), channel_id=1, source_target_pairs={{0,64},{1,65},{2,66},{3,67},{4,68},{5,69},{6,70},{7,71},{8,72},{9,... | collective-permute-start | bytes 36872 | tf_op jit(solution)/shard_map/ppermute | solution.py:381
  24.5 15.5 %collective-permute-start.6 = (bf16[2,48,128]{2,1,0:T(8,128)(2,1)S(1)}, bf16[2,48,128]{2,1,0:T(8,128)(2,1)S(1)}, u32[]{:S(2)}, u32[]{:S(2)}) collective-permute-start(bf16[2,48,128]{2,1,0:T(8,128)(2,1)S(1)} %pad_maximum_fusion.15), channel_id=1, source_target_pairs={{0,32},{1,33},{2,34},{3,35},{4,36},{5,37},{6,38},{7,39},{8,40},{9,... | collective-permute-start | bytes 73736 | tf_op jit(solution)/shard_map/ppermute | solution.py:381
  40.1 5.7 %collective-permute-start.7 = (bf16[4,48,128]{2,1,0:T(8,128)(2,1)S(1)}, bf16[4,48,128]{2,1,0:T(8,128)(2,1)S(1)}, u32[]{:S(2)}, u32[]{:S(2)}) collective-permute-start(bf16[4,48,128]{2,1,0:T(8,128)(2,1)S(1)} %pad_maximum_fusion.12), channel_id=1, source_target_pairs={{0,4},{1,5},{2,6},{3,7},{4,0},{5,1},{6,2},{7,3},{8,12},{9,13},{10,... | collective-permute-start | bytes 147464 | tf_op jit(solution)/shard_map/ppermute | solution.py:381
  45.8 1.0 copy-start
  46.8 0.8 copy-start.1
  49.9 10.9 %collective-permute-start.10 = (bf16[8,48,128]{2,1,0:T(8,128)(2,1)S(1)}, bf16[8,48,128]{2,1,0:T(8,128)(2,1)S(1)}, u32[]{:S(2)}, u32[]{:S(2)}) collective-permute-start(bf16[8,48,128]{2,1,0:T(8,128)(2,1)S(1)} %pad_maximum_fusion.9), channel_id=1, source_target_pairs={{0,8},{1,9},{2,10},{3,11},{4,12},{5,13},{6,14},{7,15},{8,0},{9,1},... | collective-permute-start | bytes 294920 | tf_op jit(solution)/shard_map/ppermute | solution.py:381
  50.5 10.2 %collective-permute-start.9 = (bf16[1,256,128]{2,1,0:T(8,128)(2,1)S(1)}, bf16[1,256,128]{2,1,0:T(8,128)(2,1)S(1)}, u32[]{:S(2)}, u32[]{:S(2)}) collective-permute-start(bf16[1,256,128]{2,1,0:T(8,128)(2,1)S(1)} %slice.11), channel_id=1, source_target_pairs={{0,8},{1,9},{2,10},{3,11},{4,12},{5,13},{6,14},{7,15},{8,0},{9,1},... | collective-permute-start | bytes 196616 | tf_op jit(solution)/shard_map/ppermute | solution.py:381
  52.0 8.7 %collective-permute-start.8 = (bf16[1,9,4,128]{3,2,1,0:T(4,128)(2,1)S(1)}, bf16[1,9,4,128]{3,2,1,0:T(4,128)(2,1)S(1)}, u32[]{:S(2)}, u32[]{:S(2)}) collective-permute-start(bf16[1,9,4,128]{3,2,1,0:T(4,128)(2,1)S(1)} %shard_map.93), channel_id=1, source_target_pairs={{0,8},{1,9},{2,10},{3,11},{4,12},{5,13},{6,14},{7,15},{8,0},{9,1},... | collective-permute-start | bytes 27656 | tf_op jit(solution)/shard_map/ppermute | solution.py:381
  60.9 14.8 %collective-permute-start.13 = (bf16[16,48,128]{2,1,0:T(8,128)(2,1)S(1)}, bf16[16,48,128]{2,1,0:T(8,128)(2,1)S(1)}, u32[]{:S(2)}, u32[]{:S(2)}) collective-permute-start(bf16[16,48,128]{2,1,0:T(8,128)(2,1)S(1)} %pad_maximum_fusion.4), channel_id=1, source_target_pairs={{0,16},{1,17},{2,18},{3,19},{4,20},{5,21},{6,22},{7,23},{8,24},{9,... | collective-permute-start | bytes 589832 | tf_op jit(solution)/shard_map/ppermute | solution.py:381
  63.8 11.8 %collective-permute-start.12 = (bf16[2,256,128]{2,1,0:T(8,128)(2,1)S(1)}, bf16[2,256,128]{2,1,0:T(8,128)(2,1)S(1)}, u32[]{:S(2)}, u32[]{:S(2)}) collective-permute-start(bf16[2,256,128]{2,1,0:T(8,128)(2,1)S(1)} %pad_maximum_fusion.6), channel_id=1, source_target_pairs={{0,16},{1,17},{2,18},{3,19},{4,20},{5,21},{6,22},{7,23},{8,24},{9,... | collective-permute-start | bytes 393224 | tf_op jit(solution)/shard_map/ppermute | solution.py:381
  64.5 11.1 %collective-permute-start.11 = (bf16[2,9,4,128]{3,2,1,0:T(4,128)(2,1)S(1)}, bf16[2,9,4,128]{3,2,1,0:T(4,128)(2,1)S(1)}, u32[]{:S(2)}, u32[]{:S(2)}) collective-permute-start(bf16[2,9,4,128]{3,2,1,0:T(4,128)(2,1)S(1)} %pad_maximum_fusion.16), channel_id=1, source_target_pairs={{0,16},{1,17},{2,18},{3,19},{4,20},{5,21},{6,22},{7,23},{8,24},{9,... | collective-permute-start | bytes 55304 | tf_op jit(solution)/shard_map/ppermute | solution.py:381
  76.0 10.6 %collective-permute-start.16 = (bf16[32,48,128]{2,1,0:T(8,128)(2,1)S(1)}, bf16[32,48,128]{2,1,0:T(8,128)(2,1)S(1)}, u32[]{:S(2)}, u32[]{:S(2)}) collective-permute-start(bf16[32,48,128]{2,1,0:T(8,128)(2,1)S(1)} %pad_maximum_fusion.1), channel_id=1, source_target_pairs={{0,2},{1,3},{2,0},{3,1},{4,6},{5,7},{6,4},{7,5},{8,10},{9,11},{10,... | collective-permute-start | bytes 1179656 | tf_op jit(solution)/shard_map/ppermute | solution.py:381
  76.2 10.4 %collective-permute-start.15 = (bf16[1,256,128]{2,1,0:T(8,128)(2,1)S(1)}, bf16[1,256,128]{2,1,0:T(8,128)(2,1)S(1)}, u32[]{:S(2)}, u32[]{:S(2)}) collective-permute-start(bf16[1,256,128]{2,1,0:T(8,128)(2,1)S(1)} %constant_dynamic-slice_fusion), channel_id=1, source_target_pairs={{0,32},{1,33},{2,34},{3,35},{4,36},{5,37},{6,38},{7,39},{8,40},{9,... | collective-permute-start | bytes 196616 | tf_op jit(solution)/shard_map/ppermute | solution.py:381
  78.2 8.3 %collective-permute-start.14 = (bf16[1,41,4,128]{3,2,1,0:T(4,128)(2,1)S(1)}, bf16[1,41,4,128]{3,2,1,0:T(4,128)(2,1)S(1)}, u32[]{:S(2)}, u32[]{:S(2)}) collective-permute-start(bf16[1,41,4,128]{3,2,1,0:T(4,128)(2,1)S(1)} %pad_maximum_fusion.13), channel_id=1, source_target_pairs={{0,32},{1,33},{2,34},{3,35},{4,36},{5,37},{6,38},{7,39},{8,40},{9,... | collective-permute-start | bytes 125960 | tf_op jit(solution)/shard_map/ppermute | solution.py:381
  86.7 18.6 %copy-start.2 = (s32[32,32]{1,0:T(8,128)S(1)}, s32[32,32]{1,0:T(8,128)}, u32[]{:S(2)}) copy-start(s32[32,32]{1,0:T(8,128)} %lists.1) | copy-start | bytes 12292
  86.7 12.0 %collective-permute-start.19 = (bf16[2,256,128]{2,1,0:T(8,128)(2,1)S(1)}, bf16[2,256,128]{2,1,0:T(8,128)(2,1)S(1)}, u32[]{:S(2)}, u32[]{:S(2)}) collective-permute-start(bf16[2,256,128]{2,1,0:T(8,128)(2,1)S(1)} %pad_maximum_fusion.7), channel_id=1, source_target_pairs={{0,64},{1,65},{2,66},{3,67},{4,68},{5,69},{6,70},{7,71},{8,72},{9,... | collective-permute-start | bytes 393224 | tf_op jit(solution)/shard_map/ppermute | solution.py:381
  89.3 9.3 %collective-permute-start.18 = (bf16[2,41,4,128]{3,2,1,0:T(4,128)(2,1)S(1)}, bf16[2,41,4,128]{3,2,1,0:T(4,128)(2,1)S(1)}, u32[]{:S(2)}, u32[]{:S(2)}) collective-permute-start(bf16[2,41,4,128]{3,2,1,0:T(4,128)(2,1)S(1)} %pad_maximum_fusion.10), channel_id=1, source_target_pairs={{0,64},{1,65},{2,66},{3,67},{4,68},{5,69},{6,70},{7,71},{8,72},{9,... | collective-permute-start | bytes 251912 | tf_op jit(solution)/shard_map/ppermute | solution.py:381
  90.3 8.4 %collective-permute-start.17 = (bf16[64,48,128]{2,1,0:T(8,128)(2,1)S(1)}, bf16[64,48,128]{2,1,0:T(8,128)(2,1)S(1)}, u32[]{:S(2)}, u32[]{:S(2)}) collective-permute-start(bf16[64,48,128]{2,1,0:T(8,128)(2,1)S(1)} %pad_maximum_fusion.own_roots), channel_id=1, source_target_pairs={{0,1},{1,0},{2,3},{3,2},{4,5},{5,4},{6,7},{7,6},{8,9},{9,8},{10,11... | collective-permute-start | bytes 2359304 | tf_op jit(solution)/shard_map/ppermute | solution.py:381

commit v2 on v1

--- a/solution.py
+++ b/solution.py
@@ -16,7 +16,7 @@
 WIDE = 128
 GROUP = 8
 SIDE = 4
-ROOT_STEPS = (64, 32, 4, 8, 16, 2, 1)
+ROOT_STEPS = (4, 64, 32, 16, 8, 2, 1)
 ROOT_ROWS = 48
 VMEM = pl.BlockSpec(memory_space=pltpu.VMEM)
 SMEM = pl.BlockSpec(memory_space=pltpu.SMEM)
@@ -112,17 +112,25 @@
     return jnp.concatenate(pieces(apply_map(three, maps)), axis=0)
 
 
+def turned(number, bits):
+    out = number * 0
+    for k in range(bits):
+        out = out | (((number >> k) & 1) << (bits - 1 - k))
+    return out
+
+
 def map_of(rows):
     return jnp.concatenate([rows[:128], rows[128:256]], axis=1)
 
 
-def group_kernel(held, out):
+def group_kernel(place, held, out):
     rhs = out.shape[2]
-    level = [held[i, 256 : 256 + 3 * rhs] for i in range(GROUP)]
+    me = place[0] % GROUP
+    level = [held[turned(i ^ me, 3), 256 : 256 + 3 * rhs] for i in range(GROUP)]
     slot = 0
     while len(level) > 1:
         level = [
-            merge(level[2 * i], level[2 * i + 1], map_of(held[slot + i]))
+            merge(level[2 * i], level[2 * i + 1], map_of(held[turned((slot + i) ^ me, 3)]))
             for i in range(len(level) // 2)
         ]
         for i, node in enumerate(level):
@@ -132,14 +140,14 @@
     out[0, slot + 1] = level[0][2 * rhs :]
 
 
-def group_merge(held, rhs):
+def group_merge(place, held, rhs):
     return pl.pallas_call(
         group_kernel,
-        in_specs=[VMEM],
+        in_specs=[SMEM, VMEM],
         out_specs=VMEM,
         out_shape=jax.ShapeDtypeStruct((1, GROUP + 1, rhs, held.shape[-1]), bf16),
         compiler_params=params(16),
-    )(held)
+    )(place, held)
 
 
 def slab_kernel(place, groups, maps, out):
@@ -147,11 +155,12 @@
     me = place[0] // GROUP % SIDE
     top = GROUP - 2
     level = [
-        jnp.concatenate([groups[i ^ me, top + k] for k in range(3)], axis=0) for i in range(SIDE)
+        jnp.concatenate([groups[turned(i ^ me, 2), top + k] for k in range(3)], axis=0)
+        for i in range(SIDE)
     ]
-    a = merge(level[0], level[1], map_of(maps[0 ^ me]))
-    b = merge(level[2], level[3], map_of(maps[1 ^ me]))
-    c = merge(a, b, map_of(maps[2 ^ me]))
+    a = merge(level[0], level[1], map_of(maps[turned(0 ^ me, 2)]))
+    b = merge(level[2], level[3], map_of(maps[turned(1 ^ me, 2)]))
+    c = merge(a, b, map_of(maps[turned(2 ^ me, 2)]))
     out[0, 0] = a[:rhs]
     out[0, 1] = b[:rhs]
     for k in range(3):
@@ -259,11 +268,12 @@
         ws[y * count : (y + 1) * count] = table[y]
     row = SIDE * (GROUP + 1) + 2
     tops = [
-        jnp.concatenate([table[y ^ y_me, row + k] for k in range(3)], axis=0) for y in range(SIDE)
+        jnp.concatenate([table[turned(y ^ y_me, 2), row + k] for k in range(3)], axis=0)
+        for y in range(SIDE)
     ]
-    a = merge(tops[0], tops[1], map_of(maps[0 ^ y_me]))
-    b = merge(tops[2], tops[3], map_of(maps[1 ^ y_me]))
-    c = merge(a, b, map_of(maps[2 ^ y_me]))
+    a = merge(tops[0], tops[1], map_of(maps[turned(0 ^ y_me, 2)]))
+    b = merge(tops[2], tops[3], map_of(maps[turned(1 ^ y_me, 2)]))
+    c = merge(a, b, map_of(maps[turned(2 ^ y_me, 2)]))
     for k, node in enumerate((c, a, b)):
         ws[SIDE * count + k] = node[:rhs]
     base = SIDE * count + 4
@@ -342,17 +352,18 @@
     y_me, z_me = me // (GROUP * SIDE), me // GROUP % SIDE
 
     def in_group(group, k):
-        return count * ((group // SIDE) ^ y_me) + (GROUP + 1) * ((group % SIDE) ^ z_me) + k
+        y, z = turned((group // SIDE) ^ y_me, 2), turned((group % SIDE) ^ z_me, 2)
+        return count * y + (GROUP + 1) * z + k
 
     def in_slab(y, k):
-        return count * (y ^ y_me) + SIDE * (GROUP + 1) + k
+        return count * turned(y ^ y_me, 2) + SIDE * (GROUP + 1) + k
 
     n = lists
     d = n - 128
-    turned = jnp.zeros_like(d)
+    spot = jnp.zeros_like(d)
     for k, mask in enumerate(ROOT_STEPS):
-        turned = turned | jnp.where(((d ^ me) & mask) != 0, 1 << k, 0)
-    out = SIDE * count + 4 + turned
+        spot = spot | jnp.where(((d ^ me) & mask) != 0, 1 << k, 0)
+    out = SIDE * count + 4 + spot
     out = jnp.where(n < 128, in_group((n - 64) // 4, n % 4), out)
     out = jnp.where(n < 64, in_group((n - 32) // 2, 4 + n % 2), out)
     out = jnp.where(n < 32, in_group(n - 16, 6), out)
@@ -406,61 +417,50 @@
 
     root, root_w = upward(points, weights, leaf_maps, root_maps, root_picks, top_picks)
 
-    def more(root, step):
-        return both(root, ROOT_STEPS[step], size)
-
-    root, maps = lax.optimization_barrier((root, maps))
-    root = more(root, 0)
-    held = jnp.concatenate([maps[:, :, :128], maps[:, :, 128:], root_w], axis=1)
-    held, root = lax.optimization_barrier((held, root))
-    groups = [[g * GROUP + k for k in range(GROUP)] for g in range(size // GROUP)]
-    held = lax.all_gather(held, "leaf", axis=0, tiled=True, axis_index_groups=groups)
-    root = more(root, 1)
-    held, root = lax.optimization_barrier((held, root))
-    root = more(root, 2)
-    group_nodes = group_merge(held, rhs)
-    spare = held[GROUP - 1 :, :256]
-
     local = near_lists - me * per
     side = jnp.where(me % 2 == 0, jnp.where(local < 0, 2, 1), jnp.where(local < 0, 1, 2))
     inside = jnp.logical_and(local >= 0, local < per)
     slots = jnp.where(inside, local, side * per + local % per)
 
-    parts = 4
+    tie = lax.optimization_barrier
     nears = []
 
-    def near_part(k, slots):
-        return field(k * (per // parts), per // parts, slots, slots, sources, targets, ws)
-
+    def swaps(step, mask, *arrays):
+        return [both(a, mask, size) for a in arrays], both(root, ROOT_STEPS[step], size)
+
+    def near_part(count):
+        start = sum(n.shape[0] for n in nears)
+        nears.append(field(start, count, slots, slots, sources, targets, ws))
+
+    held = jnp.concatenate([maps[:, :, :128], maps[:, :, 128:], root_w], axis=1)
+    (held,), root = swaps(0, 4, held)
     sources, targets, ws = forms((points, first, second), (weights, w_first, w_second))
-    slots, sources, group_nodes, spare, root = lax.optimization_barrier(
-        (slots, sources, group_nodes, spare, root)
-    )
-    groups, slab_maps = [both(a, 8, size) for a in (group_nodes, spare)]
-    root = more(root, 3)
-    nears.append(near_part(0, slots))
-    nears[0], slots, groups, slab_maps, root = lax.optimization_barrier(
-        (nears[0], slots, groups, slab_maps, root)
-    )
-    groups, slab_maps = [both(a, 16, size) for a in (groups, slab_maps)]
-    root = more(root, 4)
-    nears.append(near_part(1, slots))
-    nears[1], slots, groups, slab_maps, root = lax.optimization_barrier(
-        (nears[1], slots, groups, slab_maps, root)
-    )
-    slab_nodes = slab_merge(place, groups, slab_maps)
+    sources, slots, held, root = tie((sources, slots, held, root))
+    (held,), root = swaps(1, 2, held)
+    near_part(4)
+    nears[-1], slots, held, root = tie((nears[-1], slots, held, root))
+    (held,), root = swaps(2, 1, held)
+    near_part(4)
+    nears[-1], slots, held, root = tie((nears[-1], slots, held, root))
+    groups = group_merge(place, held, rhs)
+    spare = lax.dynamic_slice_in_dim(held, turned((GROUP - 1) ^ (me % GROUP), 3), 1, 0)[:, :256]
+    slots, groups, spare, root = tie((slots, groups, spare, root))
+    (groups, spare), root = swaps(3, 16, groups, spare)
+    near_part(4)
+    nears[-1], slots, groups, spare, root = tie((nears[-1], slots, groups, spare, root))
+    (groups, spare), root = swaps(4, 8, groups, spare)
+    near_part(4)
+    nears[-1], slots, groups, spare, root = tie((nears[-1], slots, groups, spare, root))
+    slab_nodes = slab_merge(place, groups, spare)
     table = jnp.concatenate([groups.reshape(1, -1, rhs, groups.shape[-1]), slab_nodes], axis=1)
-    last_maps = lax.dynamic_slice_in_dim(slab_maps, z_me ^ (SIDE - 1), 1, 0)
-    slots, table, last_maps, root = lax.optimization_barrier((slots, table, last_maps, root))
+    last_maps = lax.dynamic_slice_in_dim(spare, turned((SIDE - 1) ^ z_me, 2), 1, 0)
+    slots, table, last_maps, root = tie((slots, table, last_maps, root))
+    (table, last_maps), root = swaps(5, 64, table, last_maps)
+    near_part(8)
+    nears[-1], slots, table, last_maps, root = tie((nears[-1], slots, table, last_maps, root))
     table, last_maps = [both(a, 32, size) for a in (table, last_maps)]
-    root = more(root, 5)
-    nears.append(near_part(2, slots))
-    nears[2], slots, table, last_maps, root = lax.optimization_barrier(
-        (nears[2], slots, table, last_maps, root)
-    )
-    table, last_maps = [both(a, 64, size) for a in (table, last_maps)]
     other_roots = swap(root, ROOT_STEPS[6], size)
-    nears.append(near_part(3, slots))
+    near_part(8)
 
     index = jnp.arange(size, dtype=jnp.int32)
     spots = place

time: 137 us -> 138 us (level)
  blocking collectives: 13.3 us -> 0 us
  starting transfers between devices: 33.3 us -> 39.7 us
  waiting for transfers between devices: 6.49 us -> 11.7 us
  Pallas kernels: 76.7 us -> 78.8 us
    all_gather x1 -> x0, blocking collectives: 13.3 us -> none  [on_device(): lax.all_gather(held, 'leaf', axis=0, tiled=True, axis_index_groups=groups)]
    ppermute x15 -> x18, starting transfers between devices: 20.8 us -> 27.2 us  [swap(): return lax.ppermute(x, 'leaf', [(i, i ^ mask) for i in range(size)])]
    ppermute x15 -> x18, waiting for transfers between devices: 6.47 us -> 11.7 us  [swap(): return lax.ppermute(x, 'leaf', [(i, i ^ mask) for i in range(size)])]
    pallas_call x5 -> x7, Pallas kernels: 63.1 us -> 65.1 us  [field(): pl.pallas_call(functools.partial(field_kernel, 4, 1024 // columns, start)...]
  transfers between devices with their start and end apart: 20 -> 23, of which waited for: 2 -> 4; matrix products, arithmetic and copies ran while one was open for 3% -> 3% of each run, Pallas kernels for 27% -> 28%
where the time goes in v2:
time: 138 us; the launch traced here: 137 us
  Pallas kernels  78.8 us (57%)
  starting transfers between devices  39.7 us (29%)
  waiting for transfers between devices  11.7 us (8%)
  other arithmetic  3.55 us (3%)
  local copies, waits for them, and re-layouts  2.73 us (2%)
    pallas_call x7, Pallas kernels, field(): pl.pallas_call(functools.partial(field_kernel, 4, 1024 // columns, start)...  65.1 us
    ppermute x18, starting transfers between devices, swap(): return lax.ppermute(x, 'leaf', [(i, i ^ mask) for i in range(size)])  27.2 us
    ppermute x18, waiting for transfers between devices, swap(): return lax.ppermute(x, 'leaf', [(i, i ^ mask) for i in range(size)])  11.7 us
    ppermute x1, starting transfers between devices, on_device(): lax.ppermute(top_maps, 'leaf', [(n, home_of(n)) for n in range(size)])  8.2 us
    pallas_call x1, Pallas kernels, far_tables(): pl.pallas_call(tables_kernel, in_specs=[SMEM] * 2 + [VMEM] * 4, out_specs...  6.5 us
    pallas_call x1, Pallas kernels, upward(): pl.pallas_call(upward_kernel, in_specs=[VMEM] * 6, out_specs=[VMEM] * 2,...  4.13 us
    ppermute x1, starting transfers between devices, on_device(): w_first = lax.ppermute(weights, 'leaf', pairs)  2.99 us
  transfers between devices with their start and end apart: 23, of which 4 were waited for; matrix products, arithmetic and copies ran while one was open for 3% of the time, Pallas kernels for 28%

profile of v2, /device:TPU:0, one launch (start us, length us, event | category | flops | bytes accessed | tf_op | source)
XLA Modules:
  0.0 136.8 jit_solution(16556623540735841141)
XLA Ops:
  0.0 0.7 collective-permute-start.1
  0.7 3.0 %collective-permute-start.2 = (bf16[32,4,256]{2,1,0:T(4,128)(2,1)}, bf16[32,4,256]{2,1,0:T(4,128)(2,1)S(1)}, u32[]{:S(2)}, u32[]{:S(2)}) collective-permute-start(bf16[32,4,256]{2,1,0:T(4,128)(2,1)} %weights.1), channel_id=1, source_target_pairs={{0,1},{1,0},{2,3},{3,2},{4,5},{5,4},{6,7},{7,6},{8,9},{9,8},{10,11... | collective-permute-start | bytes 196616 | tf_op jit(solution)/shard_map/ppermute | solution.py:414
  3.7 0.7 collective-permute-start.3
  4.3 8.2 %collective-permute-start.4 = (bf16[1,128,256]{2,1,0:T(8,128)(2,1)}, bf16[1,128,256]{2,1,0:T(8,128)(2,1)S(1)}, u32[]{:S(2)}, u32[]{:S(2)}) collective-permute-start(bf16[1,128,256]{2,1,0:T(8,128)(2,1)} %param.13), channel_id=1, source_target_pairs={{0,127},{1,95},{2,31},{3,63},{4,23},{5,55},{6,87},{7,119},{8,7},{9... | collective-permute-start | bytes 196616 | tf_op jit(solution)/shard_map/ppermute | solution.py:412
  12.5 0.8 copy.10
  13.3 0.9 fusion.16.w_lists
  14.2 4.1 %shard_map.92 = (bf16[1,48,128]{2,1,0:T(8,128)(2,1)}, bf16[1,16,128]{2,1,0:T(8,128)(2,1)}) custom-call(bf16[32,32,256]{2,1,0:T(8,128)(2,1)} %points.1, bf16[32,4,256]{2,1,0:T(4,128)(2,1)} %weights.1, bf16[32,128,256]{2,1,0:T(8,128)(2,1)} %leaf_maps.1, bf16[1,128,4096]{2,1,0:T(8,128)(2,1)} %root_maps.1, s32[1,128]{1,0:T(1,128)} %picks.1, s32[1,128]{1,0:T(1,128)} %top_picks.1), custom_call_target="tpu_custom_call" | custom-call | tf_op jit(solution)/shard_map/pallas_call | solution.py:97
  18.4 3.1 %collective-permute-start.6 = (bf16[1,48,128]{2,1,0:T(8,128)(2,1)}, bf16[1,48,128]{2,1,0:T(8,128)(2,1)S(1)}, u32[]{:S(2)}, u32[]{:S(2)}) collective-permute-start(bf16[1,48,128]{2,1,0:T(8,128)(2,1)} %get-tuple-element.49), channel_id=1, source_target_pairs={{0,4},{1,5},{2,6},{3,7},{4,0},{5,1},{6,2},{7,3},{8,12},{9,13},{10,... | collective-permute-start | bytes 36872 | tf_op jit(solution)/shard_map/ppermute | solution.py:392
  21.5 0.7 pad_maximum_fusion.13
  22.2 1.7 %collective-permute-done.6 = bf16[1,48,128]{2,1,0:T(8,128)(2,1)S(1)} collective-permute-done((bf16[1,48,128]{2,1,0:T(8,128)(2,1)}, bf16[1,48,128]{2,1,0:T(8,128)(2,1)S(1)}, u32[]{:S(2)}, u32[]{:S(2)}) %collective-permute-start.6) | collective-permute-done | bytes 12320 | tf_op jit(solution)/shard_map/ppermute | solution.py:392
  23.8 3.0 %collective-permute-start.5 = (bf16[1,272,128]{2,1,0:T(8,128)(2,1)S(1)}, bf16[1,272,128]{2,1,0:T(8,128)(2,1)S(1)}, u32[]{:S(2)}, u32[]{:S(2)}) collective-permute-start(bf16[1,272,128]{2,1,0:T(8,128)(2,1)S(1)} %pad_maximum_fusion.13), channel_id=1, source_target_pairs={{0,4},{1,5},{2,6},{3,7},{4,0},{5,1},{6,2},{7,3},{8,12},{9,13},{10,... | collective-permute-start | bytes 208904 | tf_op jit(solution)/shard_map/ppermute | solution.py:392
  26.9 0.7 pad_maximum_fusion.17
  27.6 2.2 %collective-permute-done.5 = bf16[1,272,128]{2,1,0:T(8,128)(2,1)S(1)} collective-permute-done((bf16[1,272,128]{2,1,0:T(8,128)(2,1)S(1)}, bf16[1,272,128]{2,1,0:T(8,128)(2,1)S(1)}, u32[]{:S(2)}, u32[]{:S(2)}) %collective-permute-start.5) | collective-permute-done | bytes 69664 | tf_op jit(solution)/shard_map/ppermute | solution.py:392
  29.8 0.7 pad_maximum_fusion.8
  30.5 1.0 copy-done
  31.6 0.8 copy-done.1
  32.4 2.2 %shard_map.91 = (bf16[96,256,128]{2,1,0:T(8,128)(2,1)S(1)}, bf16[32,128,256]{2,1,0:T(8,128)(2,1)S(1)}, bf16[96,4,256]{2,1,0:T(4,128)(2,1)S(1)}) custom-call(bf16[32,32,256]{2,1,0:T(8,128)(2,1)S(1)} %copy-done, bf16[32,32,256]{2,1,0:T(8,128)(2,1)S(1)} %collective-permute-done.first, bf16[32,32,256]{2,1,0:T(8,128)(2,1)S(1)} %collective-permute-done.1.second, ...), custom_call_target="tpu_custom_call" | custom-call | tf_op jit(solution)/shard_map/pallas_call | solution.py:205
  34.7 1.9 %collective-permute-start.8 = (bf16[2,48,128]{2,1,0:T(8,128)(2,1)S(1)}, bf16[2,48,128]{2,1,0:T(8,128)(2,1)S(1)}, u32[]{:S(2)}, u32[]{:S(2)}) collective-permute-start(bf16[2,48,128]{2,1,0:T(8,128)(2,1)S(1)} %pad_maximum_fusion.17), channel_id=1, source_target_pairs={{0,64},{1,65},{2,66},{3,67},{4,68},{5,69},{6,70},{7,71},{8,72},{9,... | collective-permute-start | bytes 73736 | tf_op jit(solution)/shard_map/ppermute | solution.py:392
  36.6 2.8 %collective-permute-start.7 = (bf16[2,272,128]{2,1,0:T(8,128)(2,1)S(1)}, bf16[2,272,128]{2,1,0:T(8,128)(2,1)S(1)}, u32[]{:S(2)}, u32[]{:S(2)}) collective-permute-start(bf16[2,272,128]{2,1,0:T(8,128)(2,1)S(1)} %pad_maximum_fusion.8), channel_id=1, source_target_pairs={{0,2},{1,3},{2,0},{3,1},{4,6},{5,7},{6,4},{7,5},{8,10},{9,11},{10,... | collective-permute-start | bytes 417800 | tf_op jit(solution)/shard_map/ppermute | solution.py:392
  39.4 4.6 %shard_map.93 = f32[4,4,256]{2,1,0:T(4,128)S(1)} custom-call(s32[32,16]{1,0:T(8,128)S(1)} %fusion.19.lists.w_lists, s32[32,16]{1,0:T(8,128)S(1)} %fusion.19.lists.w_lists, bf16[96,256,128]{2,1,0:T(8,128)(2,1)S(1)} %get-tuple-element.51.sources, bf16[32,128,256]{2,1,0:T(8,128)(2,1)S(1)} %get-tuple-element.52.targets, bf16[96,4,256]{2,1,0:T(4,128)(2,1)S(1)} %get-tuple-element.53.ws), custom_call_target="tpu_custom_call" | custom-call | flops 4294967296 | bytes 1048576 | tf_op jit(solution)/shard_map/pallas_call | solution.py:249
  44.1 0.1 collective-permute-start.10
  44.2 0.3 collective-permute-start.9
  44.4 4.6 %shard_map.94 = f32[4,4,256]{2,1,0:T(4,128)S(1)} custom-call(s32[32,16]{1,0:T(8,128)S(1)} %fusion.19.lists.w_lists, s32[32,16]{1,0:T(8,128)S(1)} %fusion.19.lists.w_lists, bf16[96,256,128]{2,1,0:T(8,128)(2,1)S(1)} %get-tuple-element.51.sources, bf16[32,128,256]{2,1,0:T(8,128)(2,1)S(1)} %get-tuple-element.52.targets, bf16[96,4,256]{2,1,0:T(4,128)(2,1)S(1)} %get-tuple-element.53.ws), custom_call_target="tpu_custom_call" | custom-call | flops 4294967296 | bytes 1048576 | tf_op jit(solution)/shard_map/pallas_call | solution.py:249
  49.2 0.5 shard_map.95
  49.6 2.6 %collective-permute-start.13 = (bf16[8,48,128]{2,1,0:T(8,128)(2,1)S(1)}, bf16[8,48,128]{2,1,0:T(8,128)(2,1)S(1)}, u32[]{:S(2)}, u32[]{:S(2)}) collective-permute-start(bf16[8,48,128]{2,1,0:T(8,128)(2,1)S(1)} %pad_maximum_fusion.11), channel_id=1, source_target_pairs={{0,16},{1,17},{2,18},{3,19},{4,20},{5,21},{6,22},{7,23},{8,24},{9,... | collective-permute-start | bytes 294920 | tf_op jit(solution)/shard_map/ppermute | solution.py:392
  52.2 1.0 collective-permute-start.12
  53.3 2.5 %collective-permute-start.11 = (bf16[1,9,4,128]{3,2,1,0:T(4,128)(2,1)S(1)}, bf16[1,9,4,128]{3,2,1,0:T(4,128)(2,1)S(1)}, u32[]{:S(2)}, u32[]{:S(2)}) collective-permute-start(bf16[1,9,4,128]{3,2,1,0:T(4,128)(2,1)S(1)} %shard_map.95), channel_id=1, source_target_pairs={{0,16},{1,17},{2,18},{3,19},{4,20},{5,21},{6,22},{7,23},{8,24},{9,... | collective-permute-start | bytes 27656 | tf_op jit(solution)/shard_map/ppermute | solution.py:392
  55.8 4.6 %shard_map.96 = f32[4,4,256]{2,1,0:T(4,128)S(1)} custom-call(s32[32,16]{1,0:T(8,128)S(1)} %fusion.19.lists.w_lists, s32[32,16]{1,0:T(8,128)S(1)} %fusion.19.lists.w_lists, bf16[96,256,128]{2,1,0:T(8,128)(2,1)S(1)} %get-tuple-element.51.sources, bf16[32,128,256]{2,1,0:T(8,128)(2,1)S(1)} %get-tuple-element.52.targets, bf16[96,4,256]{2,1,0:T(4,128)(2,1)S(1)} %get-tuple-element.53.ws), custom_call_target="tpu_custom_call" | custom-call | flops 4294967296 | bytes 1048576 | tf_op jit(solution)/shard_map/pallas_call | solution.py:249
  60.5 1.0 collective-permute-start.16
  61.5 1.1 collective-permute-start.15
  62.6 1.0 collective-permute-start.14
  63.5 4.6 %shard_map.97 = f32[4,4,256]{2,1,0:T(4,128)S(1)} custom-call(s32[32,16]{1,0:T(8,128)S(1)} %fusion.19.lists.w_lists, s32[32,16]{1,0:T(8,128)S(1)} %fusion.19.lists.w_lists, bf16[96,256,128]{2,1,0:T(8,128)(2,1)S(1)} %get-tuple-element.51.sources, bf16[32,128,256]{2,1,0:T(8,128)(2,1)S(1)} %get-tuple-element.52.targets, bf16[96,4,256]{2,1,0:T(4,128)(2,1)S(1)} %get-tuple-element.53.ws), custom_call_target="tpu_custom_call" | custom-call | flops 4294967296 | bytes 1048576 | tf_op jit(solution)/shard_map/pallas_call | solution.py:249
  68.2 2.1 %collective-permute-done.14 = bf16[2,9,4,128]{3,2,1,0:T(4,128)(2,1)S(1)} collective-permute-done((bf16[2,9,4,128]{3,2,1,0:T(4,128)(2,1)S(1)}, bf16[2,9,4,128]{3,2,1,0:T(4,128)(2,1)S(1)}, u32[]{:S(2)}, u32[]{:S(2)}) %collective-permute-start.14) | collective-permute-done | bytes 18464 | tf_op jit(solution)/shard_map/ppermute | solution.py:392
  70.4 0.3 shard_map.98
  70.7 0.9 collective-permute-start.19
  71.6 1.4 %collective-permute-start.18 = (bf16[1,256,128]{2,1,0:T(8,128)(2,1)S(1)}, bf16[1,256,128]{2,1,0:T(8,128)(2,1)S(1)}, u32[]{:S(2)}, u32[]{:S(2)}) collective-permute-start(bf16[1,256,128]{2,1,0:T(8,128)(2,1)S(1)} %constant_dynamic-slice_fusion), channel_id=1, source_target_pairs={{0,64},{1,65},{2,66},{3,67},{4,68},{5,69},{6,70},{7,71},{8,72},{9,... | collective-permute-start | bytes 196616 | tf_op jit(solution)/shard_map/ppermute | solution.py:392
  73.0 2.1 %collective-permute-start.17 = (bf16[1,41,4,128]{3,2,1,0:T(4,128)(2,1)S(1)}, bf16[1,41,4,128]{3,2,1,0:T(4,128)(2,1)S(1)}, u32[]{:S(2)}, u32[]{:S(2)}) collective-permute-start(bf16[1,41,4,128]{3,2,1,0:T(4,128)(2,1)S(1)} %pad_maximum_fusion.15), channel_id=1, source_target_pairs={{0,64},{1,65},{2,66},{3,67},{4,68},{5,69},{6,70},{7,71},{8,72},{9,... | collective-permute-start | bytes 125960 | tf_op jit(solution)/shard_map/ppermute | solution.py:392
  75.2 8.2 %shard_map.99 = f32[8,4,256]{2,1,0:T(4,128)S(1)} custom-call(s32[32,16]{1,0:T(8,128)S(1)} %fusion.19.lists.w_lists, s32[32,16]{1,0:T(8,128)S(1)} %fusion.19.lists.w_lists, bf16[96,256,128]{2,1,0:T(8,128)(2,1)S(1)} %get-tuple-element.51.sources, bf16[32,128,256]{2,1,0:T(8,128)(2,1)S(1)} %get-tuple-element.52.targets, bf16[96,4,256]{2,1,0:T(4,128)(2,1)S(1)} %get-tuple-element.53.ws), custom_call_target="tpu_custom_call" | custom-call | flops 8589934592 | bytes 1048576 | tf_op jit(solution)/shard_map/pallas_call | solution.py:249
  83.4 0.1 pad_maximum_fusion.12
  83.5 0.1 pad_maximum_fusion.own_roots
  83.6 0.1 collective-permute-start.20
  83.7 8.2 %shard_map.101 = f32[8,4,256]{2,1,0:T(4,128)S(1)} custom-call(s32[32,16]{1,0:T(8,128)S(1)} %fusion.19.lists.w_lists, s32[32,16]{1,0:T(8,128)S(1)} %fusion.19.lists.w_lists, bf16[96,256,128]{2,1,0:T(8,128)(2,1)S(1)} %get-tuple-element.51.sources, bf16[32,128,256]{2,1,0:T(8,128)(2,1)S(1)} %get-tuple-element.52.targets, ...), custom_call_target="tpu_custom_call" | custom-call | flops 8589934592 | bytes 1048576 | tf_op jit(solution)/shard_map/pallas_call | solution.py:249
  91.8 1.2 collective-permute-start.22
  93.0 1.1 collective-permute-start.21
  94.1 5.7 %collective-permute-done.21 = bf16[2,41,4,128]{3,2,1,0:T(4,128)(2,1)S(1)} collective-permute-done((bf16[2,41,4,128]{3,2,1,0:T(4,128)(2,1)S(1)}, bf16[2,41,4,128]{3,2,1,0:T(4,128)(2,1)S(1)}, u32[]{:S(2)}, u32[]{:S(2)}) %collective-permute-start.21) | collective-permute-done | bytes 84000 | tf_op jit(solution)/shard_map/ppermute | solution.py:392
  99.8 0.1 pad_maximum_fusion.7.table
  100.0 6.5 %shard_map.100 = (bf16[256,128,128]{2,1,0:T(8,128)(2,1)S(1)}, bf16[296,4,128]{2,1,0:T(4,128)(2,1)S(1)}) custom-call(s32[1]{0:T(128)} %bitcast.place, s32[128]{0:T(128)S(1)} %fusion.43.spots, bf16[64,48,128]{2,1,0:T(8,128)(2,1)S(1)} %pad_maximum_fusion.own_roots, bf16[64,48,128]{2,1,0:T(8,128)(2,1)S(1)} %collective-permute-done.20.other_roots, ...), custom_call_target="tpu_custom_call" | custom-call | tf_op jit(solution)/shard_map/pallas_call | solution.py:335
  106.5 30.4 %shard_map.102 = f32[32,4,256]{2,1,0:T(4,128)} custom-call(s32[32,32]{1,0:T(8,128)S(1)} %copy-done.2, s32[32,32]{1,0:T(8,128)S(1)} %fusion.16.w_lists, bf16[256,128,128]{2,1,0:T(8,128)(2,1)S(1)} %get-tuple-element.81.sources, bf16[32,128,256]{2,1,0:T(8,128)(2,1)S(1)} %get-tuple-element.52.targets, bf16[296,4,128]{2,1,0:T(4,128)(2,1)S(1)} %get-tuple-element.82.ws, ...), custom_call_target="tpu_custom_call" | custom-call | flops 34359738368 | bytes 1048576 | tf_op jit(solution)/shard_map/pallas_call | solution.py:249
  (48 shorter events, 0.5 us)
Async XLA Ops:
  0.0 30.5 %collective-permute-start = (bf16[32,32,256]{2,1,0:T(8,128)(2,1)}, bf16[32,32,256]{2,1,0:T(8,128)(2,1)S(1)}, u32[]{:S(2)}, u32[]{:S(2)}) collective-permute-start(bf16[32,32,256]{2,1,0:T(8,128)(2,1)} %points.1), channel_id=1, source_target_pairs={{0,1},{1,0},{2,3},{3,2},{4,5},{5,4},{6,7},{7,6},{8,9},{9,8},{10,11... | collective-permute-start | bytes 1572872 | tf_op jit(solution)/shard_map/ppermute | solution.py:413
  0.0 30.5 %collective-permute-start.1 = (bf16[32,32,256]{2,1,0:T(8,128)(2,1)}, bf16[32,32,256]{2,1,0:T(8,128)(2,1)S(1)}, u32[]{:S(2)}, u32[]{:S(2)}) collective-permute-start(bf16[32,32,256]{2,1,0:T(8,128)(2,1)} %points.1), channel_id=1, source_target_pairs={{1,2},{3,4},{5,6},{7,8},{9,10},{11,12},{13,14},{15,16},{17,18},{19... | collective-permute-start | bytes 1572872 | tf_op jit(solution)/shard_map/ppermute | solution.py:415
  0.7 29.8 %collective-permute-start.2 = (bf16[32,4,256]{2,1,0:T(4,128)(2,1)}, bf16[32,4,256]{2,1,0:T(4,128)(2,1)S(1)}, u32[]{:S(2)}, u32[]{:S(2)}) collective-permute-start(bf16[32,4,256]{2,1,0:T(4,128)(2,1)} %weights.1), channel_id=1, source_target_pairs={{0,1},{1,0},{2,3},{3,2},{4,5},{5,4},{6,7},{7,6},{8,9},{9,8},{10,11... | collective-permute-start | bytes 196616 | tf_op jit(solution)/shard_map/ppermute | solution.py:414
  3.7 26.8 %collective-permute-start.3 = (bf16[32,4,256]{2,1,0:T(4,128)(2,1)}, bf16[32,4,256]{2,1,0:T(4,128)(2,1)S(1)}, u32[]{:S(2)}, u32[]{:S(2)}) collective-permute-start(bf16[32,4,256]{2,1,0:T(4,128)(2,1)} %weights.1), channel_id=1, source_target_pairs={{1,2},{3,4},{5,6},{7,8},{9,10},{11,12},{13,14},{15,16},{17,18},{19... | collective-permute-start | bytes 196616 | tf_op jit(solution)/shard_map/ppermute | solution.py:416
  4.3 14.0 %collective-permute-start.4 = (bf16[1,128,256]{2,1,0:T(8,128)(2,1)}, bf16[1,128,256]{2,1,0:T(8,128)(2,1)S(1)}, u32[]{:S(2)}, u32[]{:S(2)}) collective-permute-start(bf16[1,128,256]{2,1,0:T(8,128)(2,1)} %param.13), channel_id=1, source_target_pairs={{0,127},{1,95},{2,31},{3,63},{4,23},{5,55},{6,87},{7,119},{8,7},{9... | collective-permute-start | bytes 196616 | tf_op jit(solution)/shard_map/ppermute | solution.py:412
  18.4 5.5 %collective-permute-start.6 = (bf16[1,48,128]{2,1,0:T(8,128)(2,1)}, bf16[1,48,128]{2,1,0:T(8,128)(2,1)S(1)}, u32[]{:S(2)}, u32[]{:S(2)}) collective-permute-start(bf16[1,48,128]{2,1,0:T(8,128)(2,1)} %get-tuple-element.49), channel_id=1, source_target_pairs={{0,4},{1,5},{2,6},{3,7},{4,0},{5,1},{6,2},{7,3},{8,12},{9,13},{10,... | collective-permute-start | bytes 36872 | tf_op jit(solution)/shard_map/ppermute | solution.py:392
  23.8 5.9 %collective-permute-start.5 = (bf16[1,272,128]{2,1,0:T(8,128)(2,1)S(1)}, bf16[1,272,128]{2,1,0:T(8,128)(2,1)S(1)}, u32[]{:S(2)}, u32[]{:S(2)}) collective-permute-start(bf16[1,272,128]{2,1,0:T(8,128)(2,1)S(1)} %pad_maximum_fusion.13), channel_id=1, source_target_pairs={{0,4},{1,5},{2,6},{3,7},{4,0},{5,1},{6,2},{7,3},{8,12},{9,13},{10,... | collective-permute-start | bytes 208904 | tf_op jit(solution)/shard_map/ppermute | solution.py:392
  30.5 1.0 copy-start
  31.6 0.8 copy-start.1
  34.7 9.4 %collective-permute-start.8 = (bf16[2,48,128]{2,1,0:T(8,128)(2,1)S(1)}, bf16[2,48,128]{2,1,0:T(8,128)(2,1)S(1)}, u32[]{:S(2)}, u32[]{:S(2)}) collective-permute-start(bf16[2,48,128]{2,1,0:T(8,128)(2,1)S(1)} %pad_maximum_fusion.17), channel_id=1, source_target_pairs={{0,64},{1,65},{2,66},{3,67},{4,68},{5,69},{6,70},{7,71},{8,72},{9,... | collective-permute-start | bytes 73736 | tf_op jit(solution)/shard_map/ppermute | solution.py:392
  36.6 7.5 %collective-permute-start.7 = (bf16[2,272,128]{2,1,0:T(8,128)(2,1)S(1)}, bf16[2,272,128]{2,1,0:T(8,128)(2,1)S(1)}, u32[]{:S(2)}, u32[]{:S(2)}) collective-permute-start(bf16[2,272,128]{2,1,0:T(8,128)(2,1)S(1)} %pad_maximum_fusion.8), channel_id=1, source_target_pairs={{0,2},{1,3},{2,0},{3,1},{4,6},{5,7},{6,4},{7,5},{8,10},{9,11},{10,... | collective-permute-start | bytes 417800 | tf_op jit(solution)/shard_map/ppermute | solution.py:392
  44.1 5.0 %collective-permute-start.10 = (bf16[4,48,128]{2,1,0:T(8,128)(2,1)S(1)}, bf16[4,48,128]{2,1,0:T(8,128)(2,1)S(1)}, u32[]{:S(2)}, u32[]{:S(2)}) collective-permute-start(bf16[4,48,128]{2,1,0:T(8,128)(2,1)S(1)} %pad_maximum_fusion.14), channel_id=1, source_target_pairs={{0,32},{1,33},{2,34},{3,35},{4,36},{5,37},{6,38},{7,39},{8,40},{9,... | collective-permute-start | bytes 147464 | tf_op jit(solution)/shard_map/ppermute | solution.py:392
  44.2 4.9 %collective-permute-start.9 = (bf16[4,272,128]{2,1,0:T(8,128)(2,1)S(1)}, bf16[4,272,128]{2,1,0:T(8,128)(2,1)S(1)}, u32[]{:S(2)}, u32[]{:S(2)}) collective-permute-start(bf16[4,272,128]{2,1,0:T(8,128)(2,1)S(1)} %pad_maximum_fusion.3), channel_id=1, source_target_pairs={{0,1},{1,0},{2,3},{3,2},{4,5},{5,4},{6,7},{7,6},{8,9},{9,8},{10,11... | collective-permute-start | bytes 835592 | tf_op jit(solution)/shard_map/ppermute | solution.py:392
  49.6 10.8 %collective-permute-start.13 = (bf16[8,48,128]{2,1,0:T(8,128)(2,1)S(1)}, bf16[8,48,128]{2,1,0:T(8,128)(2,1)S(1)}, u32[]{:S(2)}, u32[]{:S(2)}) collective-permute-start(bf16[8,48,128]{2,1,0:T(8,128)(2,1)S(1)} %pad_maximum_fusion.11), channel_id=1, source_target_pairs={{0,16},{1,17},{2,18},{3,19},{4,20},{5,21},{6,22},{7,23},{8,24},{9,... | collective-permute-start | bytes 294920 | tf_op jit(solution)/shard_map/ppermute | solution.py:392
  52.2 8.2 %collective-permute-start.12 = (bf16[1,256,128]{2,1,0:T(8,128)(2,1)S(1)}, bf16[1,256,128]{2,1,0:T(8,128)(2,1)S(1)}, u32[]{:S(2)}, u32[]{:S(2)}) collective-permute-start(bf16[1,256,128]{2,1,0:T(8,128)(2,1)S(1)} %constant_dynamic-slice_fusion.1), channel_id=1, source_target_pairs={{0,16},{1,17},{2,18},{3,19},{4,20},{5,21},{6,22},{7,23},{8,24},{9,... | collective-permute-start | bytes 196616 | tf_op jit(solution)/shard_map/ppermute | solution.py:392
  53.3 7.1 %collective-permute-start.11 = (bf16[1,9,4,128]{3,2,1,0:T(4,128)(2,1)S(1)}, bf16[1,9,4,128]{3,2,1,0:T(4,128)(2,1)S(1)}, u32[]{:S(2)}, u32[]{:S(2)}) collective-permute-start(bf16[1,9,4,128]{3,2,1,0:T(4,128)(2,1)S(1)} %shard_map.95), channel_id=1, source_target_pairs={{0,16},{1,17},{2,18},{3,19},{4,20},{5,21},{6,22},{7,23},{8,24},{9,... | collective-permute-start | bytes 27656 | tf_op jit(solution)/shard_map/ppermute | solution.py:392
  60.5 9.8 %collective-permute-start.16 = (bf16[16,48,128]{2,1,0:T(8,128)(2,1)S(1)}, bf16[16,48,128]{2,1,0:T(8,128)(2,1)S(1)}, u32[]{:S(2)}, u32[]{:S(2)}) collective-permute-start(bf16[16,48,128]{2,1,0:T(8,128)(2,1)S(1)} %pad_maximum_fusion.6), channel_id=1, source_target_pairs={{0,8},{1,9},{2,10},{3,11},{4,12},{5,13},{6,14},{7,15},{8,0},{9,1},... | collective-permute-start | bytes 589832 | tf_op jit(solution)/shard_map/ppermute | solution.py:392
  61.5 8.8 %collective-permute-start.15 = (bf16[2,256,128]{2,1,0:T(8,128)(2,1)S(1)}, bf16[2,256,128]{2,1,0:T(8,128)(2,1)S(1)}, u32[]{:S(2)}, u32[]{:S(2)}) collective-permute-start(bf16[2,256,128]{2,1,0:T(8,128)(2,1)S(1)} %pad_maximum_fusion.9), channel_id=1, source_target_pairs={{0,8},{1,9},{2,10},{3,11},{4,12},{5,13},{6,14},{7,15},{8,0},{9,1},... | collective-permute-start | bytes 393224 | tf_op jit(solution)/shard_map/ppermute | solution.py:392
  62.6 7.6 %collective-permute-start.14 = (bf16[2,9,4,128]{3,2,1,0:T(4,128)(2,1)S(1)}, bf16[2,9,4,128]{3,2,1,0:T(4,128)(2,1)S(1)}, u32[]{:S(2)}, u32[]{:S(2)}) collective-permute-start(bf16[2,9,4,128]{3,2,1,0:T(4,128)(2,1)S(1)} %pad_maximum_fusion.18), channel_id=1, source_target_pairs={{0,8},{1,9},{2,10},{3,11},{4,12},{5,13},{6,14},{7,15},{8,0},{9,1},... | collective-permute-start | bytes 55304 | tf_op jit(solution)/shard_map/ppermute | solution.py:392
  70.7 12.7 %collective-permute-start.19 = (bf16[32,48,128]{2,1,0:T(8,128)(2,1)S(1)}, bf16[32,48,128]{2,1,0:T(8,128)(2,1)S(1)}, u32[]{:S(2)}, u32[]{:S(2)}) collective-permute-start(bf16[32,48,128]{2,1,0:T(8,128)(2,1)S(1)} %pad_maximum_fusion.2), channel_id=1, source_target_pairs={{0,2},{1,3},{2,0},{3,1},{4,6},{5,7},{6,4},{7,5},{8,10},{9,11},{10,... | collective-permute-start | bytes 1179656 | tf_op jit(solution)/shard_map/ppermute | solution.py:392
  71.6 11.8 %collective-permute-start.18 = (bf16[1,256,128]{2,1,0:T(8,128)(2,1)S(1)}, bf16[1,256,128]{2,1,0:T(8,128)(2,1)S(1)}, u32[]{:S(2)}, u32[]{:S(2)}) collective-permute-start(bf16[1,256,128]{2,1,0:T(8,128)(2,1)S(1)} %constant_dynamic-slice_fusion), channel_id=1, source_target_pairs={{0,64},{1,65},{2,66},{3,67},{4,68},{5,69},{6,70},{7,71},{8,72},{9,... | collective-permute-start | bytes 196616 | tf_op jit(solution)/shard_map/ppermute | solution.py:392
  73.0 10.3 %collective-permute-start.17 = (bf16[1,41,4,128]{3,2,1,0:T(4,128)(2,1)S(1)}, bf16[1,41,4,128]{3,2,1,0:T(4,128)(2,1)S(1)}, u32[]{:S(2)}, u32[]{:S(2)}) collective-permute-start(bf16[1,41,4,128]{3,2,1,0:T(4,128)(2,1)S(1)} %pad_maximum_fusion.15), channel_id=1, source_target_pairs={{0,64},{1,65},{2,66},{3,67},{4,68},{5,69},{6,70},{7,71},{8,72},{9,... | collective-permute-start | bytes 125960 | tf_op jit(solution)/shard_map/ppermute | solution.py:392
  83.6 22.9 %copy-start.2 = (s32[32,32]{1,0:T(8,128)S(1)}, s32[32,32]{1,0:T(8,128)}, u32[]{:S(2)}) copy-start(s32[32,32]{1,0:T(8,128)} %lists.1) | copy-start | bytes 12292
  83.6 16.4 %collective-permute-start.20 = (bf16[64,48,128]{2,1,0:T(8,128)(2,1)S(1)}, bf16[64,48,128]{2,1,0:T(8,128)(2,1)S(1)}, u32[]{:S(2)}, u32[]{:S(2)}) collective-permute-start(bf16[64,48,128]{2,1,0:T(8,128)(2,1)S(1)} %pad_maximum_fusion.own_roots), channel_id=1, source_target_pairs={{0,1},{1,0},{2,3},{3,2},{4,5},{5,4},{6,7},{7,6},{8,9},{9,8},{10,11... | collective-permute-start | bytes 2359304 | tf_op jit(solution)/shard_map/ppermute | solution.py:392
  91.8 8.1 %collective-permute-start.22 = (bf16[2,256,128]{2,1,0:T(8,128)(2,1)S(1)}, bf16[2,256,128]{2,1,0:T(8,128)(2,1)S(1)}, u32[]{:S(2)}, u32[]{:S(2)}) collective-permute-start(bf16[2,256,128]{2,1,0:T(8,128)(2,1)S(1)} %pad_maximum_fusion.10), channel_id=1, source_target_pairs={{0,32},{1,33},{2,34},{3,35},{4,36},{5,37},{6,38},{7,39},{8,40},{9,... | collective-permute-start | bytes 393224 | tf_op jit(solution)/shard_map/ppermute | solution.py:392
  93.0 6.7 %collective-permute-start.21 = (bf16[2,41,4,128]{3,2,1,0:T(4,128)(2,1)S(1)}, bf16[2,41,4,128]{3,2,1,0:T(4,128)(2,1)S(1)}, u32[]{:S(2)}, u32[]{:S(2)}) collective-permute-start(bf16[2,41,4,128]{3,2,1,0:T(4,128)(2,1)S(1)} %pad_maximum_fusion.12), channel_id=1, source_target_pairs={{0,32},{1,33},{2,34},{3,35},{4,36},{5,37},{6,38},{7,39},{8,40},{9,... | collective-permute-start | bytes 251912 | tf_op jit(solution)/shard_map/ppermute | solution.py:392

commit v3 on v2

v3 whole, which is shorter than its diff:
```python
import functools
import math

import jax
import jax.numpy as jnp
from jax import lax
from jax.experimental import pallas as pl
from jax.experimental.pallas import tpu as pltpu
from jax.sharding import PartitionSpec as P

gauss = 0.0625
bf16 = jnp.bfloat16
f32 = jnp.float32
NT = (((1,), (1,)), ((), ()))
FACTOR = 2.0 * gauss * math.log2(math.e)
WIDE = 128
GROUP = 8
SIDE = 4
ROOT_STEPS = (4, 64, 32, 16, 8, 2, 1)
ROOT_ROWS = 48
MAP_ROWS = 256
GROUP_ROWS = 48
SLAB_ROWS = 32
VMEM = pl.BlockSpec(memory_space=pltpu.VMEM)
SMEM = pl.BlockSpec(memory_space=pltpu.SMEM)


def params(mib):
    return pltpu.CompilerParams(vmem_limit_bytes=mib << 20)


def pieces(x):
    a = x.astype(bf16)
    r = x - a.astype(f32)
    b = r.astype(bf16)
    c = (r - b.astype(f32)).astype(bf16)
    return a, b, c


def norm_pieces(x):
    y = x.astype(f32)
    return pieces(-0.5 * jnp.sum(y * y, axis=0, keepdims=True))


def form_rows(x, first, second):
    dims, n = x.shape
    at = lax.broadcasted_iota(jnp.int32, (16, n), 0)
    tail = jnp.zeros((16, n), f32)
    for k in range(3):
        tail = jnp.where(at == k, first[k], tail)
        tail = jnp.where(at == 3 + k, second[k], tail)
    return jnp.concatenate([x, tail.astype(bf16), jnp.zeros((WIDE - dims - 16, n), bf16)], axis=0)


def source_form(x):
    norms = [p.astype(f32) for p in norm_pieces(x)]
    return form_rows(x, [1.0] * 3, norms).T


def target_form(x):
    norms = [p.astype(f32) for p in norm_pieces(x)]
    return form_rows(x, norms, [1.0] * 3)


def apply_map(three, maps):
    m = three.shape[0] // 3
    out = lax.dot_general(three, maps, NT, preferred_element_type=f32)
    return out[:m] + (out[m : 2 * m] + out[2 * m :])


def blocks_apply(target, sources, ws):
    p = jnp.dot(jnp.concatenate(sources, axis=0), target, preferred_element_type=f32)
    kern = jnp.exp2(p * FACTOR).astype(bf16)
    return jnp.dot(jnp.concatenate(ws, axis=1), kern, preferred_element_type=f32)


def upward_kernel(points, weights, leaf_maps, root_maps, picks, top_picks, root, stacked):
    per, dims, leaf_size = points.shape
    rank = leaf_maps.shape[1]
    want = picks[...]
    x = jnp.zeros((dims, rank), f32)
    for g in range(per):
        w = lax.dot_general(weights[g], leaf_maps[g], NT, preferred_element_type=f32)
        stacked[:, g * rank : (g + 1) * rank] = w
        at = lax.broadcasted_iota(jnp.int32, (leaf_size, rank), 0) + g * leaf_size
        hot = (at == want).astype(f32).astype(bf16)
        x = x + jnp.dot(points[g], hot, preferred_element_type=f32)
    w = apply_map(jnp.concatenate(pieces(stacked[...]), axis=0), root_maps[0])
    w = jnp.concatenate(pieces(w), axis=0)
    other = top_picks[...].astype(f32).astype(bf16)
    blank = jnp.zeros((ROOT_ROWS - dims - w.shape[0] - 1, rank), bf16)
    tail = jnp.concatenate([w, other, blank], axis=0)
    root[0] = jnp.concatenate([x.astype(bf16), tail], axis=0)


def upward(points, weights, leaf_maps, root_maps, root_picks, top_picks):
    per, dims, _ = points.shape
    rhs, rank = weights.shape[1], leaf_maps.shape[1]
    return pl.pallas_call(
        upward_kernel,
        in_specs=[VMEM] * 6,
        out_specs=VMEM,
        out_shape=jax.ShapeDtypeStruct((1, ROOT_ROWS, rank), bf16),
        scratch_shapes=[pltpu.VMEM((rhs, per * rank), f32)],
        compiler_params=params(60),
    )(points, weights, leaf_maps, root_maps, root_picks, top_picks)


def merge(left, right, maps):
    three = jnp.concatenate([left, right], axis=1)
    return jnp.concatenate(pieces(apply_map(three, maps)), axis=0)


def turned(number, bits):
    out = number * 0
    for k in range(bits):
        out = out | (((number >> k) & 1) << (bits - 1 - k))
    return out


def map_of(rows):
    return jnp.concatenate([rows[: MAP_ROWS // 2], rows[MAP_ROWS // 2 : MAP_ROWS]], axis=1)


def padded(parts, rows):
    have = sum(part.shape[0] for part in parts)
    blank = jnp.zeros((rows - have, parts[0].shape[1]), bf16)
    return jnp.concatenate(parts + [blank], axis=0)


def group_kernel(rhs, place, held, roots, out):
    me = place[0] % GROUP
    first = MAP_ROWS + roots.shape[1] - 16
    level = [held[turned(i ^ me, 3), first : first + 3 * rhs] for i in range(GROUP)]
    slot = 0
    rows = []
    while len(level) > 1:
        level = [
            merge(level[2 * i], level[2 * i + 1], map_of(held[turned((slot + i) ^ me, 3), :MAP_ROWS]))
            for i in range(len(level) // 2)
        ]
        rows += [node[:rhs] for node in level]
        slot += len(level)
    out[0, :MAP_ROWS] = held[turned((GROUP - 1) ^ me, 3), :MAP_ROWS]
    out[0, MAP_ROWS : MAP_ROWS + GROUP_ROWS] = padded(rows + [level[0][rhs:]], GROUP_ROWS)
    for i in range(GROUP):
        at = MAP_ROWS + GROUP_ROWS + i * ROOT_ROWS
        out[0, at : at + ROOT_ROWS] = roots[i]


def group_merge(rhs, place, held, roots):
    rows = MAP_ROWS + GROUP_ROWS + GROUP * ROOT_ROWS
    return pl.pallas_call(
        functools.partial(group_kernel, rhs),
        in_specs=[SMEM] + [VMEM] * 2,
        out_specs=VMEM,
        out_shape=jax.ShapeDtypeStruct((1, rows, held.shape[-1]), bf16),
        compiler_params=params(16),
    )(place, held, roots)


def slab_kernel(rhs, place, held, out, roots):
    me = place[0] // GROUP % SIDE
    top = MAP_ROWS + (GROUP - 2) * rhs
    level = [held[turned(i ^ me, 2), top : top + 3 * rhs] for i in range(SIDE)]
    maps = [map_of(held[turned(i ^ me, 2), :MAP_ROWS]) for i in range(SIDE - 1)]
    a = merge(level[0], level[1], maps[0])
    b = merge(level[2], level[3], maps[1])
    c = merge(a, b, maps[2])
    out[0, :MAP_ROWS] = held[turned((SIDE - 1) ^ me, 2), :MAP_ROWS]
    for i in range(SIDE):
        at = MAP_ROWS + i * GROUP_ROWS
        out[0, at : at + GROUP_ROWS] = held[i, MAP_ROWS : MAP_ROWS + GROUP_ROWS]
        for k in range(GROUP):
            at = MAP_ROWS + GROUP_ROWS + k * ROOT_ROWS
            roots[i * GROUP + k] = held[i, at : at + ROOT_ROWS]
    at = MAP_ROWS + SIDE * GROUP_ROWS
    out[0, at : at + SLAB_ROWS] = padded([a[:rhs], b[:rhs], c], SLAB_ROWS)


def slab_merge(rhs, place, held):
    rank = held.shape[-1]
    rows = MAP_ROWS + SIDE * GROUP_ROWS + SLAB_ROWS
    return pl.pallas_call(
        functools.partial(slab_kernel, rhs),
        in_specs=[SMEM, VMEM],
        out_specs=[VMEM] * 2,
        out_shape=[
            jax.ShapeDtypeStruct((1, rows, rank), bf16),
            jax.ShapeDtypeStruct((SIDE * GROUP, ROOT_ROWS, rank), bf16),
        ],
        compiler_params=params(16),
    )(place, held)


def forms_kernel(own, first, second, w_own, w_first, w_second, sources, targets, ws):
    per = own.shape[0]
    refs = ((own, w_own), (first, w_first), (second, w_second))
    for i, (ref, w_ref) in enumerate(refs):

        def prepare(step, carry, i=i, ref=ref, w_ref=w_ref):
            found = []
            for u in range(16):
                x = ref[step * 16 + u]
                found.append((source_form(x), target_form(x) if i == 0 else None))
            for u in range(16):
                g = step * 16 + u
                sources[i * per + g] = found[u][0]
                ws[i * per + g] = w_ref[g]
                if i == 0:
                    targets[g] = found[u][1]
            return carry

        lax.fori_loop(0, per // 16, prepare, 0)


def forms(points, weights):
    per, _, leaf_size = points[0].shape
    rhs = weights[0].shape[1]
    return pl.pallas_call(
        forms_kernel,
        in_specs=[VMEM] * 6,
        out_specs=[VMEM] * 3,
        out_shape=[
            jax.ShapeDtypeStruct((3 * per, leaf_size, WIDE), bf16),
            jax.ShapeDtypeStruct((per, WIDE, leaf_size), bf16),
            jax.ShapeDtypeStruct((3 * per, rhs, leaf_size), bf16),
        ],
        compiler_params=params(24),
    )(*points, *weights)


def near_place(place, per, leaf):
    local = leaf - place[0] * per
    odd = place[0] % 2
    below = (2 - odd) * per + per
    above = (1 + odd) * per - per
    return local + jnp.where(local < 0, below, jnp.where(local >= per, above, 0))


def field_kernel(unroll, together, start, near, place, lists, sources, targets, ws, *rest):
    out = rest[-1]
    per = targets.shape[0]
    entries = lists.shape[0] if near else lists.shape[1]

    def leaves(step, carry):
        totals = []
        for u in range(unroll):
            g = start + step * unroll + u
            target = targets[g]
            total = jnp.zeros(out.shape[1:], f32)
            for j in range(0, entries, together):
                if near:
                    ids = [near_place(place, per, lists[j + k, g]) for k in range(together)]
                else:
                    ids = [lists[g, j + k] for k in range(together)]
                total = total + blocks_apply(target, [sources[i] for i in ids], [ws[i] for i in ids])
            totals.append(total)
        for u in range(unroll):
            out[step * unroll + u] = totals[u]
        return carry

    lax.fori_loop(0, out.shape[0] // unroll, leaves, 0)
    if len(rest) > 1:
        out[...] = out[...] + rest[0][...]


def field(near, start, count, place, lists, sources, targets, ws, *init):
    rhs, leaf_size = ws.shape[1], targets.shape[2]
    columns = sources.shape[1]
    entries = count * lists.shape[0 if near else 1] * columns * leaf_size
    return pl.pallas_call(
        functools.partial(field_kernel, 4, 1024 // columns, start, near),
        in_specs=[SMEM] * 2 + [VMEM] * (3 + len(init)),
        out_specs=VMEM,
        out_shape=jax.ShapeDtypeStruct((count, rhs, leaf_size), f32),
        compiler_params=params(24),
        cost_estimate=pl.CostEstimate(flops=entries * 1024, bytes_accessed=1 << 20, transcendentals=0),
    )(place, lists, sources, targets, ws, *init)


def tables_kernel(rhs, place, spots, own_roots, other_roots, held, sources, ws, x_all, picks):
    half_roots, _, rank = own_roots.shape
    nodes = 2 * half_roots
    dims = x_all.shape[1]
    y_me = place[0] // (GROUP * SIDE)
    z_me = place[0] // GROUP % SIDE

    tops = []
    for y in range(SIDE):
        at = turned(y ^ y_me, 2)
        for z in range(SIDE):
            group = SIDE * y + z
            first = pl.multiple_of(MAP_ROWS + GROUP_ROWS * turned(z ^ z_me, 2), 16)
            rows = held[at, pl.ds(first, GROUP_ROWS)]
            base = [64 + 4 * group + i for i in range(4)] + [32 + 2 * group, 33 + 2 * group, 16 + group]
            for k, n in enumerate(base):
                ws[n] = rows[k * rhs : (k + 1) * rhs]
        first = MAP_ROWS + SIDE * GROUP_ROWS
        rows = held[at, first : first + SLAB_ROWS]
        for k, n in enumerate((2 * SIDE + 2 * y, 2 * SIDE + 2 * y + 1, SIDE + y)):
            ws[n] = rows[k * rhs : (k + 1) * rhs]
        tops.append(rows[2 * rhs : 5 * rhs])
    maps = [map_of(held[turned(y ^ y_me, 2), :MAP_ROWS]) for y in range(SIDE - 1)]
    a = merge(tops[0], tops[1], maps[0])
    b = merge(tops[2], tops[3], maps[1])
    c = merge(a, b, maps[2])
    for n, node in ((1, c), (2, a), (3, b)):
        ws[n] = node[:rhs]
    ws[0] = jnp.zeros((rhs, rank), bf16)

    picked = dims + 3 * rhs
    for held, ref in enumerate((own_roots, other_roots)):

        def copy_root(step, carry, held=held, ref=ref):
            for u in range(8):
                i = step * 8 + u
                n = spots[held * half_roots + i]
                x_all[nodes + n] = ref[i, :dims]
                ws[nodes + n] = ref[i, dims : dims + rhs]
                picks[n] = ref[i, picked : picked + 1].astype(f32)
            return carry

        lax.fori_loop(0, half_roots // 8, copy_root, 0)
    x_all[0] = jnp.zeros((dims, rank), bf16)

    half = nodes // 2
    while half:
        group = min(half, 16)

        def select(step, carry, half=half, group=group):
            first = half + step * group
            found = []
            for u in range(group):
                n = first + u
                pair = jnp.concatenate([x_all[2 * n], x_all[2 * n + 1]], axis=1)
                at = lax.broadcasted_iota(jnp.int32, (2 * rank, rank), 0)
                hot = (at == picks[n].astype(jnp.int32)).astype(f32).astype(bf16)
                found.append(jnp.dot(pair, hot, preferred_element_type=f32).astype(bf16))
            for u in range(group):
                x_all[first + u] = found[u]
            return carry

        lax.fori_loop(0, half // group, select, 0)
        half //= 2

    def prepare(step, carry):
        found = []
        for u in range(16):
            i = step * 16 + u
            found.append(source_form(jnp.concatenate([x_all[2 * i], x_all[2 * i + 1]], axis=1)))
        for u in range(16):
            i = step * 16 + u
            sources[2 * i] = found[u][:rank]
            sources[2 * i + 1] = found[u][rank:]
        return carry

    lax.fori_loop(0, nodes // 16, prepare, 0)


def far_tables(rhs, place, spots, own_roots, other_roots, held):
    nodes = 2 * own_roots.shape[0]
    rank = own_roots.shape[2]
    dims = ROOT_ROWS - 16
    return pl.pallas_call(
        functools.partial(tables_kernel, rhs),
        in_specs=[SMEM] * 2 + [VMEM] * 3,
        out_specs=[VMEM] * 2,
        out_shape=[
            jax.ShapeDtypeStruct((2 * nodes, rank, WIDE), bf16),
            jax.ShapeDtypeStruct((2 * nodes, rhs, rank), bf16),
        ],
        scratch_shapes=[
            pltpu.VMEM((2 * nodes, dims, rank), bf16),
            pltpu.VMEM((nodes, 1, rank), f32),
        ],
        compiler_params=params(24),
    )(place, spots, own_roots, other_roots, held)


def home_of(node):
    if node >= 64:
        return GROUP * ((node - 64) // 4) + (node - 64) % 4
    if node >= 32:
        return GROUP * ((node - 32) // 2) + 4 + (node - 32) % 2
    if node >= 16:
        return GROUP * (node - 16) + 6
    if node >= 8:
        y, z = (node - 8) // 2, (node - 8) % 2
    elif node >= 4:
        y, z = node - 4, 2
    else:
        y, z = {2: 0, 3: 1, 1: 2, 0: 3}[node], 3
    return GROUP * (SIDE * y + z) + 7


def swap(x, mask, size):
    return lax.ppermute(x, "leaf", [(i, i ^ mask) for i in range(size)])


def both(x, mask, size):
    return jnp.concatenate([x, swap(x, mask, size)], axis=0)


def on_device(
    points, weights, leaf_maps, root_maps, top_maps, root_picks, top_picks, near_lists, far_lists
):
    per, dims, leaf_size = points.shape
    rhs = weights.shape[1]
    size = lax.axis_size("leaf")
    me = lax.axis_index("leaf")
    place = me.astype(jnp.int32).reshape(1)

    pairs = [(i, i ^ 1) for i in range(size)]
    bridges = [(i, i + 1) for i in range(1, size - 1, 2)]
    bridges = bridges + [(j, i) for i, j in bridges]
    maps = lax.ppermute(top_maps, "leaf", [(n, home_of(n)) for n in range(size)])
    first = lax.ppermute(points, "leaf", pairs)
    w_first = lax.ppermute(weights, "leaf", pairs)
    second = lax.ppermute(points, "leaf", bridges)
    w_second = lax.ppermute(weights, "leaf", bridges)

    root = upward(points, weights, leaf_maps, root_maps, root_picks, top_picks)

    tie = lax.optimization_barrier
    columns = near_lists.T
    nears = []

    def swaps(step, mask, array, roots):
        return both(array, mask, size), both(roots, ROOT_STEPS[step], size)

    def near_part(count):
        start = sum(n.shape[0] for n in nears)
        nears.append(field(True, start, count, place, columns, sources, targets, ws))

    half = maps.shape[2] // 2
    held = jnp.concatenate([maps[:, :, :half], maps[:, :, half:], root], axis=1)
    held = both(held, 4, size)
    root = held[:, MAP_ROWS:]
    sources, targets, ws = forms((points, first, second), (weights, w_first, w_second))
    sources, columns, held, root = tie((sources, columns, held, root))
    held, root = swaps(1, 2, held, root)
    near_part(4)
    nears[-1], columns, held, root = tie((nears[-1], columns, held, root))
    held, root = swaps(2, 1, held, root)
    near_part(4)
    nears[-1], columns, held, root = tie((nears[-1], columns, held, root))
    held = group_merge(rhs, place, held, root)
    columns, held = tie((columns, held))
    held = both(held, 16, size)
    near_part(4)
    nears[-1], columns, held = tie((nears[-1], columns, held))
    held = both(held, 8, size)
    near_part(4)
    nears[-1], columns, held = tie((nears[-1], columns, held))
    held, root = slab_merge(rhs, place, held)
    columns, held, root = tie((columns, held, root))
    held, root = swaps(5, 64, held, root)
    near_part(8)
    nears[-1], columns, held, root = tie((nears[-1], columns, held, root))
    held = both(held, 32, size)
    other_roots = swap(root, ROOT_STEPS[6], size)
    near_part(8)
    nears[-1], held, root, other_roots = tie((nears[-1], held, root, other_roots))

    index = jnp.arange(size, dtype=jnp.int32)
    spots = place
    for k, mask in enumerate(ROOT_STEPS):
        spots = spots ^ jnp.where(((index >> k) & 1) != 0, mask, 0)
    near = jnp.concatenate(nears, axis=0)
    far_sources, far_ws = far_tables(rhs, place, spots, root, other_roots, held)
    return field(False, 0, per, place, far_lists, far_sources, targets, far_ws, near)


def solution(mesh):
    leaf3 = P("leaf", None, None)
    leaf2 = P("leaf", None)
    return jax.shard_map(
        on_device,
        mesh=mesh,
        in_specs=(leaf3,) * 5 + (leaf2,) * 4,
        out_specs=leaf3,
        check_vma=False,
    )
```

time: 138 us -> 125 us (0.906)
  starting transfers between devices: 39.7 us -> 25.8 us
  waiting for transfers between devices: 11.7 us -> 16.1 us
  Pallas kernels: 78.8 us -> 76.2 us
  other arithmetic: 3.55 us -> 1.8 us
    ppermute x18 -> x11, starting transfers between devices: 27.2 us -> 11.6 us  [swap(): return lax.ppermute(x, 'leaf', [(i, i ^ mask) for i in range(size)])]
    ppermute x18 -> x11, waiting for transfers between devices: 11.7 us -> 16.1 us  [swap(): return lax.ppermute(x, 'leaf', [(i, i ^ mask) for i in range(size)])]
    ppermute x1, starting transfers between devices: 0.01 us -> 3.06 us  [on_device(): first = lax.ppermute(points, 'leaf', pairs)]
    pallas_call x11, Pallas kernels: 76.5 us -> 74 us  [the longest x7 62.5 us: field(): pl.pallas_call(functools.partial(field_kernel, 4, 1024 // columns, start,...]
  transfers between devices with their start and end apart: 23 -> 16, of which waited for: 4 -> 5; matrix products, arithmetic and copies ran while one was open for 3% -> 1% of each run, Pallas kernels for 28% -> 30%
where the time goes in v3:
time: 125 us; the launch traced here: 123 us
  Pallas kernels  76.2 us (61%)
  starting transfers between devices  25.8 us (21%)
  waiting for transfers between devices  16.1 us (13%)
  local copies, waits for them, and re-layouts  2.64 us (2%)
  other arithmetic  1.8 us (1%)
    pallas_call x7, Pallas kernels, field(): pl.pallas_call(functools.partial(field_kernel, 4, 1024 // columns, start,...  62.5 us
    ppermute x11, waiting for transfers between devices, swap(): return lax.ppermute(x, 'leaf', [(i, i ^ mask) for i in range(size)])  16.1 us
    ppermute x11, starting transfers between devices, swap(): return lax.ppermute(x, 'leaf', [(i, i ^ mask) for i in range(size)])  11.6 us
    ppermute x1, starting transfers between devices, on_device(): lax.ppermute(top_maps, 'leaf', [(n, home_of(n)) for n in range(size)])  8.21 us
    pallas_call x1, Pallas kernels, far_tables(): pl.pallas_call(functools.partial(tables_kernel, rhs), in_specs=[SMEM] * 2...  6.58 us
    pallas_call x1, Pallas kernels, upward(): pl.pallas_call(upward_kernel, in_specs=[VMEM] * 6, out_specs=VMEM, out_sh...  4.12 us
    ppermute x1, starting transfers between devices, on_device(): first = lax.ppermute(points, 'leaf', pairs)  3.06 us
    unnamed x13, local copies, waits for them, and re-layouts  2.62 us
  transfers between devices with their start and end apart: 16, of which 5 were waited for; matrix products, arithmetic and copies ran while one was open for 1% of the time, Pallas kernels for 30%

profile of v3, /device:TPU:0, one launch (start us, length us, event | category | flops | bytes accessed | tf_op | source)
XLA Modules:
  0.0 122.8 jit_solution(9120784286959530756)
XLA Ops:
  0.0 8.2 %collective-permute-start.4 = (bf16[1,128,256]{2,1,0:T(8,128)(2,1)}, bf16[1,128,256]{2,1,0:T(8,128)(2,1)S(1)}, u32[]{:S(2)}, u32[]{:S(2)}) collective-permute-start(bf16[1,128,256]{2,1,0:T(8,128)(2,1)} %param.13), channel_id=1, source_target_pairs={{0,127},{1,95},{2,31},{3,63},{4,23},{5,55},{6,87},{7,119},{8,7},{9... | collective-permute-start | bytes 196616 | tf_op jit(solution)/shard_map/ppermute | solution.py:417
  8.2 0.7 collective-permute-start.3
  8.9 1.6 %collective-permute-start.2 = (bf16[32,4,256]{2,1,0:T(4,128)(2,1)}, bf16[32,4,256]{2,1,0:T(4,128)(2,1)S(1)}, u32[]{:S(2)}, u32[]{:S(2)}) collective-permute-start(bf16[32,4,256]{2,1,0:T(4,128)(2,1)} %weights.1), channel_id=1, source_target_pairs={{0,1},{1,0},{2,3},{3,2},{4,5},{5,4},{6,7},{7,6},{8,9},{9,8},{10,11... | collective-permute-start | bytes 196616 | tf_op jit(solution)/shard_map/ppermute | solution.py:419
  10.5 0.7 collective-permute-start.1
  11.2 3.1 %collective-permute-start = (bf16[32,32,256]{2,1,0:T(8,128)(2,1)}, bf16[32,32,256]{2,1,0:T(8,128)(2,1)S(1)}, u32[]{:S(2)}, u32[]{:S(2)}) collective-permute-start(bf16[32,32,256]{2,1,0:T(8,128)(2,1)} %points.1), channel_id=1, source_target_pairs={{0,1},{1,0},{2,3},{3,2},{4,5},{5,4},{6,7},{7,6},{8,9},{9,8},{10,11... | collective-permute-start | bytes 1572872 | tf_op jit(solution)/shard_map/ppermute | solution.py:418
  14.2 4.1 %shard_map.92 = bf16[1,48,128]{2,1,0:T(8,128)(2,1)} custom-call(bf16[32,32,256]{2,1,0:T(8,128)(2,1)} %points.1, bf16[32,4,256]{2,1,0:T(4,128)(2,1)} %weights.1, bf16[32,128,256]{2,1,0:T(8,128)(2,1)} %leaf_maps.1, bf16[1,128,4096]{2,1,0:T(8,128)(2,1)} %root_maps.1, s32[1,128]{1,0:T(1,128)} %picks.1, s32[1,128]{1,0:T(1,128)} %top_picks.1), custom_call_target="tpu_custom_call" | custom-call | tf_op jit(solution)/shard_map/pallas_call | solution.py:99
  18.4 0.0 collective-permute-done.4
  18.4 0.7 pad_maximum_fusion.9
  19.1 2.1 %collective-permute-start.5 = (bf16[1,304,128]{2,1,0:T(8,128)(2,1)S(1)}, bf16[1,304,128]{2,1,0:T(8,128)(2,1)S(1)}, u32[]{:S(2)}, u32[]{:S(2)}) collective-permute-start(bf16[1,304,128]{2,1,0:T(8,128)(2,1)S(1)} %pad_maximum_fusion.9), channel_id=1, source_target_pairs={{0,4},{1,5},{2,6},{3,7},{4,0},{5,1},{6,2},{7,3},{8,12},{9,13},{10,... | collective-permute-start | bytes 233480 | tf_op jit(solution)/shard_map/ppermute | solution.py:398
  21.2 3.8 %collective-permute-done.5 = bf16[1,304,128]{2,1,0:T(8,128)(2,1)S(1)} collective-permute-done((bf16[1,304,128]{2,1,0:T(8,128)(2,1)S(1)}, bf16[1,304,128]{2,1,0:T(8,128)(2,1)S(1)}, u32[]{:S(2)}, u32[]{:S(2)}) %collective-permute-start.5) | collective-permute-done | bytes 77856 | tf_op jit(solution)/shard_map/ppermute | solution.py:398
  25.0 0.7 pad_maximum_fusion.7
  25.7 0.0 collective-permute-done.3.w_second
  25.8 0.0 collective-permute-done.first
  25.8 0.0 copy-start
  25.8 1.0 copy-done
  26.8 0.8 copy-done.1
  27.7 2.2 %shard_map.91 = (bf16[96,256,128]{2,1,0:T(8,128)(2,1)S(1)}, bf16[32,128,256]{2,1,0:T(8,128)(2,1)S(1)}, bf16[96,4,256]{2,1,0:T(4,128)(2,1)S(1)}) custom-call(bf16[32,32,256]{2,1,0:T(8,128)(2,1)S(1)} %copy-done, bf16[32,32,256]{2,1,0:T(8,128)(2,1)S(1)} %collective-permute-done.first, bf16[32,32,256]{2,1,0:T(8,128)(2,1)S(1)} %collective-permute-done.1.second, ...), custom_call_target="tpu_custom_call" | custom-call | tf_op jit(solution)/shard_map/pallas_call | solution.py:220
  29.9 4.0 %collective-permute-start.7 = (bf16[2,48,128]{2,1,0:T(8,128)(2,1)S(1)}, bf16[2,48,128]{2,1,0:T(8,128)(2,1)S(1)}, u32[]{:S(2)}, u32[]{:S(2)}) collective-permute-start(bf16[2,48,128]{2,1,0:T(8,128)(2,1)S(1)} %slice.14), channel_id=1, source_target_pairs={{0,64},{1,65},{2,66},{3,67},{4,68},{5,69},{6,70},{7,71},{8,72},{9,... | collective-permute-start | bytes 73736 | tf_op jit(solution)/shard_map/ppermute | solution.py:398
  33.9 0.0 collective-permute-start.6
  33.9 0.7 copy-done.3
  34.6 4.2 %shard_map.93 = f32[4,4,256]{2,1,0:T(4,128)S(1)} custom-call(s32[1]{0:T(128)} %bitcast.place, s32[16,32]{1,0:T(8,128)S(1)} %bitcast.2, bf16[96,256,128]{2,1,0:T(8,128)(2,1)S(1)} %get-tuple-element.45.sources, bf16[32,128,256]{2,1,0:T(8,128)(2,1)S(1)} %get-tuple-element.46.targets, bf16[96,4,256]{2,1,0:T(4,128)(2,1)S(1)} %get-tuple-element.47.ws), custom_call_target="tpu_custom_call" | custom-call | flops 4294967296 | bytes 1048576 | tf_op jit(solution)/shard_map/pallas_call | solution.py:272
  38.9 0.3 collective-permute-done.6
  39.2 0.1 collective-permute-start.8
  39.3 4.2 %shard_map.94 = f32[4,4,256]{2,1,0:T(4,128)S(1)} custom-call(s32[1]{0:T(128)} %bitcast.place, s32[16,32]{1,0:T(8,128)S(1)} %bitcast.3, bf16[96,256,128]{2,1,0:T(8,128)(2,1)S(1)} %get-tuple-element.45.sources, bf16[32,128,256]{2,1,0:T(8,128)(2,1)S(1)} %get-tuple-element.46.targets, bf16[96,4,256]{2,1,0:T(4,128)(2,1)S(1)} %get-tuple-element.47.ws), custom_call_target="tpu_custom_call" | custom-call | flops 4294967296 | bytes 1048576 | tf_op jit(solution)/shard_map/pallas_call | solution.py:272
  43.5 0.2 collective-permute-start.9
  43.7 4.1 %collective-permute-done.9 = bf16[4,48,128]{2,1,0:T(8,128)(2,1)S(1)} collective-permute-done((bf16[4,48,128]{2,1,0:T(8,128)(2,1)S(1)}, bf16[4,48,128]{2,1,0:T(8,128)(2,1)S(1)}, u32[]{:S(2)}, u32[]{:S(2)}) %collective-permute-start.9) | collective-permute-done | bytes 49184 | tf_op jit(solution)/shard_map/ppermute | solution.py:398
  47.8 0.0 collective-permute-done.8
  47.8 0.1 pad_maximum_fusion.2.held
  47.9 0.5 shard_map.95
  48.4 0.3 collective-permute-start.10
  48.7 4.2 %shard_map.96 = f32[4,4,256]{2,1,0:T(4,128)S(1)} custom-call(s32[1]{0:T(128)} %bitcast.place, s32[16,32]{1,0:T(8,128)S(1)} %bitcast.4, bf16[96,256,128]{2,1,0:T(8,128)(2,1)S(1)} %get-tuple-element.45.sources, bf16[32,128,256]{2,1,0:T(8,128)(2,1)S(1)} %get-tuple-element.46.targets, bf16[96,4,256]{2,1,0:T(4,128)(2,1)S(1)} %get-tuple-element.47.ws), custom_call_target="tpu_custom_call" | custom-call | flops 4294967296 | bytes 1048576 | tf_op jit(solution)/shard_map/pallas_call | solution.py:272
  52.9 3.1 %collective-permute-done.10 = bf16[1,688,128]{2,1,0:T(8,128)(2,1)S(1)} collective-permute-done((bf16[1,688,128]{2,1,0:T(8,128)(2,1)S(1)}, bf16[1,688,128]{2,1,0:T(8,128)(2,1)S(1)}, u32[]{:S(2)}, u32[]{:S(2)}) %collective-permute-start.10) | collective-permute-done | bytes 176160 | tf_op jit(solution)/shard_map/ppermute | solution.py:398
  56.1 0.1 collective-permute-start.11
  56.2 4.2 %shard_map.97 = f32[4,4,256]{2,1,0:T(4,128)S(1)} custom-call(s32[1]{0:T(128)} %bitcast.place, s32[16,32]{1,0:T(8,128)S(1)} %bitcast.5, bf16[96,256,128]{2,1,0:T(8,128)(2,1)S(1)} %get-tuple-element.45.sources, bf16[32,128,256]{2,1,0:T(8,128)(2,1)S(1)} %get-tuple-element.46.targets, bf16[96,4,256]{2,1,0:T(4,128)(2,1)S(1)} %get-tuple-element.47.ws), custom_call_target="tpu_custom_call" | custom-call | flops 4294967296 | bytes 1048576 | tf_op jit(solution)/shard_map/pallas_call | solution.py:272
  60.4 4.7 %collective-permute-done.11 = bf16[2,688,128]{2,1,0:T(8,128)(2,1)S(1)} collective-permute-done((bf16[2,688,128]{2,1,0:T(8,128)(2,1)S(1)}, bf16[2,688,128]{2,1,0:T(8,128)(2,1)S(1)}, u32[]{:S(2)}, u32[]{:S(2)}) %collective-permute-start.11) | collective-permute-done | bytes 352288 | tf_op jit(solution)/shard_map/ppermute | solution.py:398
  65.1 0.1 pad_maximum_fusion.1.held
  65.2 0.3 shard_map.98
  65.5 2.3 %collective-permute-start.12 = (bf16[1,480,128]{2,1,0:T(8,128)(2,1)S(1)}, bf16[1,480,128]{2,1,0:T(8,128)(2,1)S(1)}, u32[]{:S(2)}, u32[]{:S(2)}) collective-permute-start(bf16[1,480,128]{2,1,0:T(8,128)(2,1)S(1)} %get-tuple-element.65), channel_id=1, source_target_pairs={{0,64},{1,65},{2,66},{3,67},{4,68},{5,69},{6,70},{7,71},{8,72},{9,... | collective-permute-start | bytes 368648 | tf_op jit(solution)/shard_map/ppermute | solution.py:398
  67.8 1.7 %collective-permute-start.13 = (bf16[32,48,128]{2,1,0:T(8,128)(2,1)S(1)}, bf16[32,48,128]{2,1,0:T(8,128)(2,1)S(1)}, u32[]{:S(2)}, u32[]{:S(2)}) collective-permute-start(bf16[32,48,128]{2,1,0:T(8,128)(2,1)S(1)} %get-tuple-element.66), channel_id=1, source_target_pairs={{0,2},{1,3},{2,0},{3,1},{4,6},{5,7},{6,4},{7,5},{8,10},{9,11},{10,... | collective-permute-start | bytes 1179656 | tf_op jit(solution)/shard_map/ppermute | solution.py:398
  69.6 7.8 %shard_map.99 = f32[8,4,256]{2,1,0:T(4,128)S(1)} custom-call(s32[1]{0:T(128)} %bitcast.place, s32[16,32]{1,0:T(8,128)S(1)} %bitcast.6, bf16[96,256,128]{2,1,0:T(8,128)(2,1)S(1)} %get-tuple-element.45.sources, bf16[32,128,256]{2,1,0:T(8,128)(2,1)S(1)} %get-tuple-element.46.targets, bf16[96,4,256]{2,1,0:T(4,128)(2,1)S(1)} %get-tuple-element.47.ws), custom_call_target="tpu_custom_call" | custom-call | flops 8589934592 | bytes 1048576 | tf_op jit(solution)/shard_map/pallas_call | solution.py:272
  77.3 0.0 collective-permute-done.12
  77.4 0.1 pad_maximum_fusion.own_roots
  77.5 0.0 copy-start.2
  77.5 0.8 collective-permute-start.14
  78.3 7.8 %shard_map.100 = f32[8,4,256]{2,1,0:T(4,128)S(1)} custom-call(s32[1]{0:T(128)} %bitcast.place, s32[16,32]{1,0:T(8,128)S(1)} %bitcast.7, bf16[96,256,128]{2,1,0:T(8,128)(2,1)S(1)} %get-tuple-element.45.sources, bf16[32,128,256]{2,1,0:T(8,128)(2,1)S(1)} %get-tuple-element.46.targets, bf16[96,4,256]{2,1,0:T(4,128)(2,1)S(1)} %get-tuple-element.47.ws), custom_call_target="tpu_custom_call" | custom-call | flops 8589934592 | bytes 1048576 | tf_op jit(solution)/shard_map/pallas_call | solution.py:272
  86.1 0.0 collective-permute-done.14
  86.2 6.6 %shard_map.101 = (bf16[256,128,128]{2,1,0:T(8,128)(2,1)S(1)}, bf16[256,4,128]{2,1,0:T(4,128)(2,1)S(1)}) custom-call(s32[1]{0:T(128)} %bitcast.place, s32[128]{0:T(128)S(1)} %fusion.6.spots, bf16[64,48,128]{2,1,0:T(8,128)(2,1)S(1)} %pad_maximum_fusion.own_roots, bf16[64,48,128]{2,1,0:T(8,128)(2,1)S(1)} %collective-permute-done.15.other_roots, ...), custom_call_target="tpu_custom_call" | custom-call | tf_op jit(solution)/shard_map/pallas_call | solution.py:365
  92.8 30.1 %shard_map.102 = f32[32,4,256]{2,1,0:T(4,128)} custom-call(s32[1]{0:T(128)} %bitcast.place, s32[32,32]{1,0:T(8,128)S(1)} %copy-done.2, bf16[256,128,128]{2,1,0:T(8,128)(2,1)S(1)} %get-tuple-element.73.sources, bf16[32,128,256]{2,1,0:T(8,128)(2,1)S(1)} %get-tuple-element.46.targets, bf16[256,4,128]{2,1,0:T(4,128)(2,1)S(1)} %get-tuple-element.74.ws, ...), custom_call_target="tpu_custom_call" | custom-call | flops 34359738368 | bytes 1048576 | tf_op jit(solution)/shard_map/pallas_call | solution.py:272
  (24 shorter events, 0.3 us)
Async XLA Ops:
  0.0 18.4 %collective-permute-start.4 = (bf16[1,128,256]{2,1,0:T(8,128)(2,1)}, bf16[1,128,256]{2,1,0:T(8,128)(2,1)S(1)}, u32[]{:S(2)}, u32[]{:S(2)}) collective-permute-start(bf16[1,128,256]{2,1,0:T(8,128)(2,1)} %param.13), channel_id=1, source_target_pairs={{0,127},{1,95},{2,31},{3,63},{4,23},{5,55},{6,87},{7,119},{8,7},{9... | collective-permute-start | bytes 196616 | tf_op jit(solution)/shard_map/ppermute | solution.py:417
  8.2 17.5 %collective-permute-start.3 = (bf16[32,4,256]{2,1,0:T(4,128)(2,1)}, bf16[32,4,256]{2,1,0:T(4,128)(2,1)S(1)}, u32[]{:S(2)}, u32[]{:S(2)}) collective-permute-start(bf16[32,4,256]{2,1,0:T(4,128)(2,1)} %weights.1), channel_id=1, source_target_pairs={{1,2},{3,4},{5,6},{7,8},{9,10},{11,12},{13,14},{15,16},{17,18},{19... | collective-permute-start | bytes 196616 | tf_op jit(solution)/shard_map/ppermute | solution.py:421
  8.9 16.9 %collective-permute-start.2 = (bf16[32,4,256]{2,1,0:T(4,128)(2,1)}, bf16[32,4,256]{2,1,0:T(4,128)(2,1)S(1)}, u32[]{:S(2)}, u32[]{:S(2)}) collective-permute-start(bf16[32,4,256]{2,1,0:T(4,128)(2,1)} %weights.1), channel_id=1, source_target_pairs={{0,1},{1,0},{2,3},{3,2},{4,5},{5,4},{6,7},{7,6},{8,9},{9,8},{10,11... | collective-permute-start | bytes 196616 | tf_op jit(solution)/shard_map/ppermute | solution.py:419
  10.5 15.3 %collective-permute-start.1 = (bf16[32,32,256]{2,1,0:T(8,128)(2,1)}, bf16[32,32,256]{2,1,0:T(8,128)(2,1)S(1)}, u32[]{:S(2)}, u32[]{:S(2)}) collective-permute-start(bf16[32,32,256]{2,1,0:T(8,128)(2,1)} %points.1), channel_id=1, source_target_pairs={{1,2},{3,4},{5,6},{7,8},{9,10},{11,12},{13,14},{15,16},{17,18},{19... | collective-permute-start | bytes 1572872 | tf_op jit(solution)/shard_map/ppermute | solution.py:420
  11.2 14.6 %collective-permute-start = (bf16[32,32,256]{2,1,0:T(8,128)(2,1)}, bf16[32,32,256]{2,1,0:T(8,128)(2,1)S(1)}, u32[]{:S(2)}, u32[]{:S(2)}) collective-permute-start(bf16[32,32,256]{2,1,0:T(8,128)(2,1)} %points.1), channel_id=1, source_target_pairs={{0,1},{1,0},{2,3},{3,2},{4,5},{5,4},{6,7},{7,6},{8,9},{9,8},{10,11... | collective-permute-start | bytes 1572872 | tf_op jit(solution)/shard_map/ppermute | solution.py:418
  19.1 5.9 %collective-permute-start.5 = (bf16[1,304,128]{2,1,0:T(8,128)(2,1)S(1)}, bf16[1,304,128]{2,1,0:T(8,128)(2,1)S(1)}, u32[]{:S(2)}, u32[]{:S(2)}) collective-permute-start(bf16[1,304,128]{2,1,0:T(8,128)(2,1)S(1)} %pad_maximum_fusion.9), channel_id=1, source_target_pairs={{0,4},{1,5},{2,6},{3,7},{4,0},{5,1},{6,2},{7,3},{8,12},{9,13},{10,... | collective-permute-start | bytes 233480 | tf_op jit(solution)/shard_map/ppermute | solution.py:398
  25.8 1.0 copy-start
  26.8 0.8 copy-start.1
  29.9 8.9 %collective-permute-start.7 = (bf16[2,48,128]{2,1,0:T(8,128)(2,1)S(1)}, bf16[2,48,128]{2,1,0:T(8,128)(2,1)S(1)}, u32[]{:S(2)}, u32[]{:S(2)}) collective-permute-start(bf16[2,48,128]{2,1,0:T(8,128)(2,1)S(1)} %slice.14), channel_id=1, source_target_pairs={{0,64},{1,65},{2,66},{3,67},{4,68},{5,69},{6,70},{7,71},{8,72},{9,... | collective-permute-start | bytes 73736 | tf_op jit(solution)/shard_map/ppermute | solution.py:398
  33.9 5.2 %collective-permute-start.6 = (bf16[2,304,128]{2,1,0:T(8,128)(2,1)S(1)}, bf16[2,304,128]{2,1,0:T(8,128)(2,1)S(1)}, u32[]{:S(2)}, u32[]{:S(2)}) collective-permute-start(bf16[2,304,128]{2,1,0:T(8,128)(2,1)S(1)} %pad_maximum_fusion.7), channel_id=1, source_target_pairs={{0,2},{1,3},{2,0},{3,1},{4,6},{5,7},{6,4},{7,5},{8,10},{9,11},{10,... | collective-permute-start | bytes 466952 | tf_op jit(solution)/shard_map/ppermute | solution.py:398
  33.9 0.7 copy-start.3
  39.2 8.6 %collective-permute-start.8 = (bf16[4,304,128]{2,1,0:T(8,128)(2,1)S(1)}, bf16[4,304,128]{2,1,0:T(8,128)(2,1)S(1)}, u32[]{:S(2)}, u32[]{:S(2)}) collective-permute-start(bf16[4,304,128]{2,1,0:T(8,128)(2,1)S(1)} %pad_maximum_fusion.5), channel_id=1, source_target_pairs={{0,1},{1,0},{2,3},{3,2},{4,5},{5,4},{6,7},{7,6},{8,9},{9,8},{10,11... | collective-permute-start | bytes 933896 | tf_op jit(solution)/shard_map/ppermute | solution.py:398
  43.5 4.3 %collective-permute-start.9 = (bf16[4,48,128]{2,1,0:T(8,128)(2,1)S(1)}, bf16[4,48,128]{2,1,0:T(8,128)(2,1)S(1)}, u32[]{:S(2)}, u32[]{:S(2)}) collective-permute-start(bf16[4,48,128]{2,1,0:T(8,128)(2,1)S(1)} %pad_maximum_fusion.10), channel_id=1, source_target_pairs={{0,32},{1,33},{2,34},{3,35},{4,36},{5,37},{6,38},{7,39},{8,40},{9,... | collective-permute-start | bytes 147464 | tf_op jit(solution)/shard_map/ppermute | solution.py:398
  48.4 7.7 %collective-permute-start.10 = (bf16[1,688,128]{2,1,0:T(8,128)(2,1)S(1)}, bf16[1,688,128]{2,1,0:T(8,128)(2,1)S(1)}, u32[]{:S(2)}, u32[]{:S(2)}) collective-permute-start(bf16[1,688,128]{2,1,0:T(8,128)(2,1)S(1)} %shard_map.95), channel_id=1, source_target_pairs={{0,16},{1,17},{2,18},{3,19},{4,20},{5,21},{6,22},{7,23},{8,24},{9,... | collective-permute-start | bytes 528392 | tf_op jit(solution)/shard_map/ppermute | solution.py:398
  56.1 9.0 %collective-permute-start.11 = (bf16[2,688,128]{2,1,0:T(8,128)(2,1)S(1)}, bf16[2,688,128]{2,1,0:T(8,128)(2,1)S(1)}, u32[]{:S(2)}, u32[]{:S(2)}) collective-permute-start(bf16[2,688,128]{2,1,0:T(8,128)(2,1)S(1)} %pad_maximum_fusion.4), channel_id=1, source_target_pairs={{0,8},{1,9},{2,10},{3,11},{4,12},{5,13},{6,14},{7,15},{8,0},{9,1},... | collective-permute-start | bytes 1056776 | tf_op jit(solution)/shard_map/ppermute | solution.py:398
  65.5 11.8 %collective-permute-start.12 = (bf16[1,480,128]{2,1,0:T(8,128)(2,1)S(1)}, bf16[1,480,128]{2,1,0:T(8,128)(2,1)S(1)}, u32[]{:S(2)}, u32[]{:S(2)}) collective-permute-start(bf16[1,480,128]{2,1,0:T(8,128)(2,1)S(1)} %get-tuple-element.65), channel_id=1, source_target_pairs={{0,64},{1,65},{2,66},{3,67},{4,68},{5,69},{6,70},{7,71},{8,72},{9,... | collective-permute-start | bytes 368648 | tf_op jit(solution)/shard_map/ppermute | solution.py:398
  67.8 9.6 %collective-permute-start.13 = (bf16[32,48,128]{2,1,0:T(8,128)(2,1)S(1)}, bf16[32,48,128]{2,1,0:T(8,128)(2,1)S(1)}, u32[]{:S(2)}, u32[]{:S(2)}) collective-permute-start(bf16[32,48,128]{2,1,0:T(8,128)(2,1)S(1)} %get-tuple-element.66), channel_id=1, source_target_pairs={{0,2},{1,3},{2,0},{3,1},{4,6},{5,7},{6,4},{7,5},{8,10},{9,11},{10,... | collective-permute-start | bytes 1179656 | tf_op jit(solution)/shard_map/ppermute | solution.py:398
  77.5 15.3 %copy-start.2 = (s32[32,32]{1,0:T(8,128)S(1)}, s32[32,32]{1,0:T(8,128)}, u32[]{:S(2)}) copy-start(s32[32,32]{1,0:T(8,128)} %lists.1) | copy-start | bytes 12292
  77.5 8.6 %collective-permute-start.14 = (bf16[2,480,128]{2,1,0:T(8,128)(2,1)S(1)}, bf16[2,480,128]{2,1,0:T(8,128)(2,1)S(1)}, u32[]{:S(2)}, u32[]{:S(2)}) collective-permute-start(bf16[2,480,128]{2,1,0:T(8,128)(2,1)S(1)} %pad_maximum_fusion.6), channel_id=1, source_target_pairs={{0,32},{1,33},{2,34},{3,35},{4,36},{5,37},{6,38},{7,39},{8,40},{9,... | collective-permute-start | bytes 737288 | tf_op jit(solution)/shard_map/ppermute | solution.py:398
  78.3 7.9 %collective-permute-start.15 = (bf16[64,48,128]{2,1,0:T(8,128)(2,1)S(1)}, bf16[64,48,128]{2,1,0:T(8,128)(2,1)S(1)}, u32[]{:S(2)}, u32[]{:S(2)}) collective-permute-start(bf16[64,48,128]{2,1,0:T(8,128)(2,1)S(1)} %pad_maximum_fusion.own_roots), channel_id=1, source_target_pairs={{0,1},{1,0},{2,3},{3,2},{4,5},{5,4},{6,7},{7,6},{8,9},{9,8},{10,11... | collective-permute-start | bytes 2359304 | tf_op jit(solution)/shard_map/ppermute | solution.py:398

commit v4 on v3

--- a/solution.py
+++ b/solution.py
@@ -193,41 +193,62 @@
     )(place, held)
 
 
-def forms_kernel(own, first, second, w_own, w_first, w_second, sources, targets, ws):
-    per = own.shape[0]
-    refs = ((own, w_own), (first, w_first), (second, w_second))
-    for i, (ref, w_ref) in enumerate(refs):
-
-        def prepare(step, carry, i=i, ref=ref, w_ref=w_ref):
-            found = []
-            for u in range(16):
-                x = ref[step * 16 + u]
-                found.append((source_form(x), target_form(x) if i == 0 else None))
-            for u in range(16):
-                g = step * 16 + u
-                sources[i * per + g] = found[u][0]
-                ws[i * per + g] = w_ref[g]
-                if i == 0:
-                    targets[g] = found[u][1]
-            return carry
-
-        lax.fori_loop(0, per // 16, prepare, 0)
-
-
-def forms(points, weights):
-    per, _, leaf_size = points[0].shape
-    rhs = weights[0].shape[1]
-    return pl.pallas_call(
-        forms_kernel,
-        in_specs=[VMEM] * 6,
+def fill_forms(first, points, weights, sources, ws, targets=None):
+    per = points.shape[0]
+
+    def prepare(step, carry):
+        found = []
+        for u in range(16):
+            x = points[step * 16 + u]
+            found.append((source_form(x), None if targets is None else target_form(x)))
+        for u in range(16):
+            g = step * 16 + u
+            sources[first + g] = found[u][0]
+            ws[first + g] = weights[g]
+            if targets is not None:
+                targets[g] = found[u][1]
+        return carry
+
+    lax.fori_loop(0, per // 16, prepare, 0)
+
+
+def own_kernel(points, weights, sources, ws, targets):
+    fill_forms(0, points, weights, sources, ws, targets)
+
+
+def own_forms(points, weights):
+    per, _, leaf_size = points.shape
+    return pl.pallas_call(
+        own_kernel,
+        in_specs=[VMEM] * 2,
         out_specs=[VMEM] * 3,
         out_shape=[
             jax.ShapeDtypeStruct((3 * per, leaf_size, WIDE), bf16),
+            jax.ShapeDtypeStruct((3 * per,) + weights.shape[1:], bf16),
             jax.ShapeDtypeStruct((per, WIDE, leaf_size), bf16),
-            jax.ShapeDtypeStruct((3 * per, rhs, leaf_size), bf16),
         ],
         compiler_params=params(24),
-    )(*points, *weights)
+    )(points, weights)
+
+
+def other_kernel(first, second, w_first, w_second, _, __, sources, ws):
+    per = first.shape[0]
+    fill_forms(per, first, w_first, sources, ws)
+    fill_forms(2 * per, second, w_second, sources, ws)
+
+
+def other_forms(first, second, w_first, w_second, sources, ws):
+    return pl.pallas_call(
+        other_kernel,
+        in_specs=[VMEM] * 6,
+        out_specs=[VMEM] * 2,
+        out_shape=[
+            jax.ShapeDtypeStruct(sources.shape, bf16),
+            jax.ShapeDtypeStruct(ws.shape, bf16),
+        ],
+        input_output_aliases={4: 0, 5: 1},
+        compiler_params=params(24),
+    )(first, second, w_first, w_second, sources, ws)
 
 
 def near_place(place, per, leaf):
@@ -435,23 +456,24 @@
 
     half = maps.shape[2] // 2
     held = jnp.concatenate([maps[:, :, :half], maps[:, :, half:], root], axis=1)
+    held, points, weights = tie((held, points, weights))
     held = both(held, 4, size)
+    sources, ws, targets = own_forms(points, weights)
+    held, sources = tie((held, sources))
     root = held[:, MAP_ROWS:]
-    sources, targets, ws = forms((points, first, second), (weights, w_first, w_second))
+    sources, ws = other_forms(first, second, w_first, w_second, sources, ws)
     sources, columns, held, root = tie((sources, columns, held, root))
     held, root = swaps(1, 2, held, root)
     near_part(4)
     nears[-1], columns, held, root = tie((nears[-1], columns, held, root))
     held, root = swaps(2, 1, held, root)
-    near_part(4)
-    nears[-1], columns, held, root = tie((nears[-1], columns, held, root))
     held = group_merge(rhs, place, held, root)
     columns, held = tie((columns, held))
     held = both(held, 16, size)
-    near_part(4)
+    near_part(8)
     nears[-1], columns, held = tie((nears[-1], columns, held))
     held = both(held, 8, size)
-    near_part(4)
+    near_part(8)
     nears[-1], columns, held = tie((nears[-1], columns, held))
     held, root = slab_merge(rhs, place, held)
     columns, held, root = tie((columns, held, root))
@@ -460,7 +482,7 @@
     nears[-1], columns, held, root = tie((nears[-1], columns, held, root))
     held = both(held, 32, size)
     other_roots = swap(root, ROOT_STEPS[6], size)
-    near_part(8)
+    near_part(4)
     nears[-1], held, root, other_roots = tie((nears[-1], held, root, other_roots))
 
     index = jnp.arange(size, dtype=jnp.int32)

time: 125 us -> 115 us (0.920); the launches traced: 123 us -> 115 us
  waiting for transfers between devices: 16.1 us -> 9.68 us
    ppermute x11, waiting for transfers between devices: 16.1 us -> 9.66 us  [swap(): return lax.ppermute(x, 'leaf', [(i, i ^ mask) for i in range(size)])]
    ppermute x11, starting transfers between devices: 11.6 us -> 15.9 us  [swap(): return lax.ppermute(x, 'leaf', [(i, i ^ mask) for i in range(size)])]
    ppermute x1, starting transfers between devices: 3.06 us -> 0.3 us  [on_device(): first = lax.ppermute(points, 'leaf', pairs)]
    pallas_call x7 -> x6, Pallas kernels: 62.5 us -> 61.4 us  [field(): pl.pallas_call(functools.partial(field_kernel, 4, 1024 // columns, start,...]
    unnamed x13 -> x12, local copies, waits for them, and re-layouts: 2.62 us -> 1.92 us
  transfers between devices with their start and end apart: 16 -> 16, of which waited for: 5 -> 5; matrix products, arithmetic and copies ran while one was open for 1% -> 1% of each run, Pallas kernels for 30% -> 32%
where the time goes in v4:
time: 115 us
  Pallas kernels  75.1 us (65%)
  starting transfers between devices  26.5 us (23%)
  waiting for transfers between devices  9.68 us (8%)
  local copies, waits for them, and re-layouts  1.94 us (2%)
    pallas_call x6, Pallas kernels, field(): pl.pallas_call(functools.partial(field_kernel, 4, 1024 // columns, start,...  61.4 us
    ppermute x11, starting transfers between devices, swap(): return lax.ppermute(x, 'leaf', [(i, i ^ mask) for i in range(size)])  15.9 us
    ppermute x11, waiting for transfers between devices, swap(): return lax.ppermute(x, 'leaf', [(i, i ^ mask) for i in range(size)])  9.66 us
    ppermute x1, starting transfers between devices, on_device(): lax.ppermute(top_maps, 'leaf', [(n, home_of(n)) for n in range(size)])  8.21 us
    pallas_call x1, Pallas kernels, far_tables(): pl.pallas_call(functools.partial(tables_kernel, rhs), in_specs=[SMEM] * 2...  6.58 us
    pallas_call x1, Pallas kernels, upward(): pl.pallas_call(upward_kernel, in_specs=[VMEM] * 6, out_specs=VMEM, out_sh...  4.12 us
  transfers between devices with their start and end apart: 16, of which 5 were waited for; matrix products, arithmetic and copies ran while one was open for 1% of the time, Pallas kernels for 32%

profile of v4, /device:TPU:0, one launch (start us, length us, event | category | flops | bytes accessed | tf_op | source)
XLA Modules:
  0.0 114.6 jit_solution(12719722695300528994)
XLA Ops:
  0.0 8.2 %collective-permute-start.4 = (bf16[1,128,256]{2,1,0:T(8,128)(2,1)}, bf16[1,128,256]{2,1,0:T(8,128)(2,1)S(1)}, u32[]{:S(2)}, u32[]{:S(2)}) collective-permute-start(bf16[1,128,256]{2,1,0:T(8,128)(2,1)} %param.13), channel_id=1, source_target_pairs={{0,127},{1,95},{2,31},{3,63},{4,23},{5,55},{6,87},{7,119},{8,7},{9... | collective-permute-start | bytes 196616 | tf_op jit(solution)/shard_map/ppermute | solution.py:438
  8.2 0.3 collective-permute-start
  8.5 0.7 collective-permute-start.1
  9.2 4.1 %shard_map.91 = bf16[1,48,128]{2,1,0:T(8,128)(2,1)} custom-call(bf16[32,32,256]{2,1,0:T(8,128)(2,1)} %points.2, bf16[32,4,256]{2,1,0:T(4,128)(2,1)} %weights.2, bf16[32,128,256]{2,1,0:T(8,128)(2,1)} %leaf_maps.1, bf16[1,128,4096]{2,1,0:T(8,128)(2,1)} %root_maps.1, s32[1,128]{1,0:T(1,128)} %picks.1, s32[1,128]{1,0:T(1,128)} %top_picks.1), custom_call_target="tpu_custom_call" | custom-call | tf_op jit(solution)/shard_map/pallas_call | solution.py:99
  13.3 0.0 collective-permute-done.4
  13.3 0.7 pad_maximum_fusion.9
  14.0 2.1 %collective-permute-start.5 = (bf16[1,304,128]{2,1,0:T(8,128)(2,1)S(1)}, bf16[1,304,128]{2,1,0:T(8,128)(2,1)S(1)}, u32[]{:S(2)}, u32[]{:S(2)}) collective-permute-start(bf16[1,304,128]{2,1,0:T(8,128)(2,1)S(1)} %pad_maximum_fusion.9), channel_id=1, source_target_pairs={{0,4},{1,5},{2,6},{3,7},{4,0},{5,1},{6,2},{7,3},{8,12},{9,13},{10,... | collective-permute-start | bytes 233480 | tf_op jit(solution)/shard_map/ppermute | solution.py:419
  16.2 0.7 collective-permute-start.2
  16.9 0.7 collective-permute-start.3
  17.5 0.0 copy-start
  17.5 1.0 copy-done
  18.6 0.8 copy-done.1
  19.4 0.8 shard_map.92
  20.2 0.2 collective-permute-done.5
  20.4 0.0 collective-permute-done.2.w_first
  20.4 0.0 collective-permute-done.3.w_second
  20.4 0.0 collective-permute-done.first
  20.5 1.5 %shard_map.93 = (bf16[96,256,128]{2,1,0:T(8,128)(2,1)S(1)}, bf16[96,4,256]{2,1,0:T(4,128)(2,1)S(1)}) custom-call(bf16[32,32,256]{2,1,0:T(8,128)(2,1)S(1)} %collective-permute-done.first, bf16[32,32,256]{2,1,0:T(8,128)(2,1)S(1)} %collective-permute-done.1.second, ...), custom_call_target="tpu_custom_call", output_to_operand_aliasing={{0}: (4, {}), {1}: (5, {})} | custom-call | tf_op jit(solution)/shard_map/pallas_call | solution.py:241
  21.9 8.6 %collective-permute-start.7 = (bf16[2,48,128]{2,1,0:T(8,128)(2,1)S(1)}, bf16[2,48,128]{2,1,0:T(8,128)(2,1)S(1)}, u32[]{:S(2)}, u32[]{:S(2)}) collective-permute-start(bf16[2,48,128]{2,1,0:T(8,128)(2,1)S(1)} %slice.11), channel_id=1, source_target_pairs={{0,64},{1,65},{2,66},{3,67},{4,68},{5,69},{6,70},{7,71},{8,72},{9,... | collective-permute-start | bytes 73736 | tf_op jit(solution)/shard_map/ppermute | solution.py:419
  30.5 4.2 %shard_map.94 = f32[4,4,256]{2,1,0:T(4,128)S(1)} custom-call(s32[1]{0:T(128)} %bitcast.place, s32[16,32]{1,0:T(8,128)S(1)} %bitcast.2, bf16[96,256,128]{2,1,0:T(8,128)(2,1)S(1)} %get-tuple-element.55.sources, bf16[32,128,256]{2,1,0:T(8,128)(2,1)S(1)} %get-tuple-element.56.targets, bf16[96,4,256]{2,1,0:T(4,128)(2,1)S(1)} %get-tuple-element.57.ws), custom_call_target="tpu_custom_call" | custom-call | flops 4294967296 | bytes 1048576 | tf_op jit(solution)/shard_map/pallas_call | solution.py:293
  34.7 1.0 collective-permute-done.6
  35.8 0.1 collective-permute-start.8
  35.9 1.1 collective-permute-start.9
  37.0 3.1 %collective-permute-done.9 = bf16[4,48,128]{2,1,0:T(8,128)(2,1)S(1)} collective-permute-done((bf16[4,48,128]{2,1,0:T(8,128)(2,1)S(1)}, bf16[4,48,128]{2,1,0:T(8,128)(2,1)S(1)}, u32[]{:S(2)}, u32[]{:S(2)}) %collective-permute-start.9) | collective-permute-done | bytes 49184 | tf_op jit(solution)/shard_map/ppermute | solution.py:419
  40.1 0.1 pad_maximum_fusion.2.held
  40.2 0.5 shard_map.95
  40.7 0.3 collective-permute-start.10
  40.9 7.7 %shard_map.96 = f32[8,4,256]{2,1,0:T(4,128)S(1)} custom-call(s32[1]{0:T(128)} %bitcast.place, s32[16,32]{1,0:T(8,128)S(1)} %bitcast.3, bf16[96,256,128]{2,1,0:T(8,128)(2,1)S(1)} %get-tuple-element.55.sources, bf16[32,128,256]{2,1,0:T(8,128)(2,1)S(1)} %get-tuple-element.56.targets, bf16[96,4,256]{2,1,0:T(4,128)(2,1)S(1)} %get-tuple-element.57.ws), custom_call_target="tpu_custom_call" | custom-call | flops 8589934592 | bytes 1048576 | tf_op jit(solution)/shard_map/pallas_call | solution.py:293
  48.7 0.0 collective-permute-done.10
  48.7 0.1 collective-permute-start.11
  48.8 7.7 %shard_map.97 = f32[8,4,256]{2,1,0:T(4,128)S(1)} custom-call(s32[1]{0:T(128)} %bitcast.place, s32[16,32]{1,0:T(8,128)S(1)} %bitcast.4, bf16[96,256,128]{2,1,0:T(8,128)(2,1)S(1)} %get-tuple-element.55.sources, bf16[32,128,256]{2,1,0:T(8,128)(2,1)S(1)} %get-tuple-element.56.targets, bf16[96,4,256]{2,1,0:T(4,128)(2,1)S(1)} %get-tuple-element.57.ws), custom_call_target="tpu_custom_call" | custom-call | flops 8589934592 | bytes 1048576 | tf_op jit(solution)/shard_map/pallas_call | solution.py:293
  56.6 2.1 %collective-permute-done.11 = bf16[2,688,128]{2,1,0:T(8,128)(2,1)S(1)} collective-permute-done((bf16[2,688,128]{2,1,0:T(8,128)(2,1)S(1)}, bf16[2,688,128]{2,1,0:T(8,128)(2,1)S(1)}, u32[]{:S(2)}, u32[]{:S(2)}) %collective-permute-start.11) | collective-permute-done | bytes 352288 | tf_op jit(solution)/shard_map/ppermute | solution.py:419
  58.7 0.1 pad_maximum_fusion.1.held
  58.7 0.3 shard_map.98
  59.1 1.1 collective-permute-start.13
  60.2 1.3 %collective-permute-start.12 = (bf16[1,480,128]{2,1,0:T(8,128)(2,1)S(1)}, bf16[1,480,128]{2,1,0:T(8,128)(2,1)S(1)}, u32[]{:S(2)}, u32[]{:S(2)}) collective-permute-start(bf16[1,480,128]{2,1,0:T(8,128)(2,1)S(1)} %get-tuple-element.72), channel_id=1, source_target_pairs={{0,64},{1,65},{2,66},{3,67},{4,68},{5,69},{6,70},{7,71},{8,72},{9,... | collective-permute-start | bytes 368648 | tf_op jit(solution)/shard_map/ppermute | solution.py:419
  61.4 7.7 %shard_map.99 = f32[8,4,256]{2,1,0:T(4,128)S(1)} custom-call(s32[1]{0:T(128)} %bitcast.place, s32[16,32]{1,0:T(8,128)S(1)} %bitcast.5, bf16[96,256,128]{2,1,0:T(8,128)(2,1)S(1)} %get-tuple-element.55.sources, bf16[32,128,256]{2,1,0:T(8,128)(2,1)S(1)} %get-tuple-element.56.targets, bf16[96,4,256]{2,1,0:T(4,128)(2,1)S(1)} %get-tuple-element.57.ws), custom_call_target="tpu_custom_call" | custom-call | flops 8589934592 | bytes 1048576 | tf_op jit(solution)/shard_map/pallas_call | solution.py:293
  69.2 0.0 collective-permute-done.12
  69.2 0.0 collective-permute-done.13
  69.2 0.1 pad_maximum_fusion.own_roots
  69.3 0.1 collective-permute-start.15
  69.4 0.0 copy-start.2
  69.4 1.2 %collective-permute-start.14 = (bf16[2,480,128]{2,1,0:T(8,128)(2,1)S(1)}, bf16[2,480,128]{2,1,0:T(8,128)(2,1)S(1)}, u32[]{:S(2)}, u32[]{:S(2)}) collective-permute-start(bf16[2,480,128]{2,1,0:T(8,128)(2,1)S(1)} %pad_maximum_fusion.6), channel_id=1, source_target_pairs={{0,32},{1,33},{2,34},{3,35},{4,36},{5,37},{6,38},{7,39},{8,40},{9,... | collective-permute-start | bytes 737288 | tf_op jit(solution)/shard_map/ppermute | solution.py:419
  70.7 4.2 %shard_map.100 = f32[4,4,256]{2,1,0:T(4,128)S(1)} custom-call(s32[1]{0:T(128)} %bitcast.place, s32[16,32]{1,0:T(8,128)S(1)} %bitcast.6, bf16[96,256,128]{2,1,0:T(8,128)(2,1)S(1)} %get-tuple-element.55.sources, bf16[32,128,256]{2,1,0:T(8,128)(2,1)S(1)} %get-tuple-element.56.targets, bf16[96,4,256]{2,1,0:T(4,128)(2,1)S(1)} %get-tuple-element.57.ws), custom_call_target="tpu_custom_call" | custom-call | flops 4294967296 | bytes 1048576 | tf_op jit(solution)/shard_map/pallas_call | solution.py:293
  74.9 3.2 %collective-permute-done.14 = bf16[2,480,128]{2,1,0:T(8,128)(2,1)S(1)} collective-permute-done((bf16[2,480,128]{2,1,0:T(8,128)(2,1)S(1)}, bf16[2,480,128]{2,1,0:T(8,128)(2,1)S(1)}, u32[]{:S(2)}, u32[]{:S(2)}) %collective-permute-start.14) | collective-permute-done | bytes 245792 | tf_op jit(solution)/shard_map/ppermute | solution.py:419
  78.1 0.0 collective-permute-done.15.other_roots
  78.1 6.6 %shard_map.101 = (bf16[256,128,128]{2,1,0:T(8,128)(2,1)S(1)}, bf16[256,4,128]{2,1,0:T(4,128)(2,1)S(1)}) custom-call(s32[1]{0:T(128)} %bitcast.place, s32[128]{0:T(128)S(1)} %fusion.6.spots, bf16[64,48,128]{2,1,0:T(8,128)(2,1)S(1)} %pad_maximum_fusion.own_roots, bf16[64,48,128]{2,1,0:T(8,128)(2,1)S(1)} %collective-permute-done.15.other_roots, ...), custom_call_target="tpu_custom_call" | custom-call | tf_op jit(solution)/shard_map/pallas_call | solution.py:386
  84.7 29.8 %shard_map.102 = f32[32,4,256]{2,1,0:T(4,128)} custom-call(s32[1]{0:T(128)} %bitcast.place, s32[32,32]{1,0:T(8,128)S(1)} %copy-done.2, bf16[256,128,128]{2,1,0:T(8,128)(2,1)S(1)} %get-tuple-element.80.sources, bf16[32,128,256]{2,1,0:T(8,128)(2,1)S(1)} %get-tuple-element.56.targets, bf16[256,4,128]{2,1,0:T(4,128)(2,1)S(1)} %get-tuple-element.81.ws, ...), custom_call_target="tpu_custom_call" | custom-call | flops 34359738368 | bytes 1048576 | tf_op jit(solution)/shard_map/pallas_call | solution.py:293
  (23 shorter events, 0.3 us)
Async XLA Ops:
  0.0 30.5 %copy-start.3 = (s32[32,16]{0,1:T(8,128)S(1)}, s32[32,16]{0,1:T(8,128)}, u32[]{:S(2)}) copy-start(s32[32,16]{0,1:T(8,128)} %param.16) | copy-start | bytes 6148
  0.0 13.3 %collective-permute-start.4 = (bf16[1,128,256]{2,1,0:T(8,128)(2,1)}, bf16[1,128,256]{2,1,0:T(8,128)(2,1)S(1)}, u32[]{:S(2)}, u32[]{:S(2)}) collective-permute-start(bf16[1,128,256]{2,1,0:T(8,128)(2,1)} %param.13), channel_id=1, source_target_pairs={{0,127},{1,95},{2,31},{3,63},{4,23},{5,55},{6,87},{7,119},{8,7},{9... | collective-permute-start | bytes 196616 | tf_op jit(solution)/shard_map/ppermute | solution.py:438
  8.2 12.2 %collective-permute-start = (bf16[32,32,256]{2,1,0:T(8,128)(2,1)}, bf16[32,32,256]{2,1,0:T(8,128)(2,1)S(1)}, u32[]{:S(2)}, u32[]{:S(2)}) collective-permute-start(bf16[32,32,256]{2,1,0:T(8,128)(2,1)} %points.2), channel_id=1, source_target_pairs={{0,1},{1,0},{2,3},{3,2},{4,5},{5,4},{6,7},{7,6},{8,9},{9,8},{10,11... | collective-permute-start | bytes 1572872 | tf_op jit(solution)/shard_map/ppermute | solution.py:439
  8.5 11.9 %collective-permute-start.1 = (bf16[32,32,256]{2,1,0:T(8,128)(2,1)}, bf16[32,32,256]{2,1,0:T(8,128)(2,1)S(1)}, u32[]{:S(2)}, u32[]{:S(2)}) collective-permute-start(bf16[32,32,256]{2,1,0:T(8,128)(2,1)} %points.2), channel_id=1, source_target_pairs={{1,2},{3,4},{5,6},{7,8},{9,10},{11,12},{13,14},{15,16},{17,18},{19... | collective-permute-start | bytes 1572872 | tf_op jit(solution)/shard_map/ppermute | solution.py:441
  14.0 6.3 %collective-permute-start.5 = (bf16[1,304,128]{2,1,0:T(8,128)(2,1)S(1)}, bf16[1,304,128]{2,1,0:T(8,128)(2,1)S(1)}, u32[]{:S(2)}, u32[]{:S(2)}) collective-permute-start(bf16[1,304,128]{2,1,0:T(8,128)(2,1)S(1)} %pad_maximum_fusion.9), channel_id=1, source_target_pairs={{0,4},{1,5},{2,6},{3,7},{4,0},{5,1},{6,2},{7,3},{8,12},{9,13},{10,... | collective-permute-start | bytes 233480 | tf_op jit(solution)/shard_map/ppermute | solution.py:419
  16.2 4.2 %collective-permute-start.2 = (bf16[32,4,256]{2,1,0:T(4,128)(2,1)}, bf16[32,4,256]{2,1,0:T(4,128)(2,1)S(1)}, u32[]{:S(2)}, u32[]{:S(2)}) collective-permute-start(bf16[32,4,256]{2,1,0:T(4,128)(2,1)} %weights.2), channel_id=1, source_target_pairs={{0,1},{1,0},{2,3},{3,2},{4,5},{5,4},{6,7},{7,6},{8,9},{9,8},{10,11... | collective-permute-start | bytes 196616 | tf_op jit(solution)/shard_map/ppermute | solution.py:440
  16.9 3.6 %collective-permute-start.3 = (bf16[32,4,256]{2,1,0:T(4,128)(2,1)}, bf16[32,4,256]{2,1,0:T(4,128)(2,1)S(1)}, u32[]{:S(2)}, u32[]{:S(2)}) collective-permute-start(bf16[32,4,256]{2,1,0:T(4,128)(2,1)} %weights.2), channel_id=1, source_target_pairs={{1,2},{3,4},{5,6},{7,8},{9,10},{11,12},{13,14},{15,16},{17,18},{19... | collective-permute-start | bytes 196616 | tf_op jit(solution)/shard_map/ppermute | solution.py:442
  17.5 1.0 copy-start
  18.6 0.8 copy-start.1
  21.9 12.8 %collective-permute-start.7 = (bf16[2,48,128]{2,1,0:T(8,128)(2,1)S(1)}, bf16[2,48,128]{2,1,0:T(8,128)(2,1)S(1)}, u32[]{:S(2)}, u32[]{:S(2)}) collective-permute-start(bf16[2,48,128]{2,1,0:T(8,128)(2,1)S(1)} %slice.11), channel_id=1, source_target_pairs={{0,64},{1,65},{2,66},{3,67},{4,68},{5,69},{6,70},{7,71},{8,72},{9,... | collective-permute-start | bytes 73736 | tf_op jit(solution)/shard_map/ppermute | solution.py:419
  30.5 5.2 %collective-permute-start.6 = (bf16[2,304,128]{2,1,0:T(8,128)(2,1)S(1)}, bf16[2,304,128]{2,1,0:T(8,128)(2,1)S(1)}, u32[]{:S(2)}, u32[]{:S(2)}) collective-permute-start(bf16[2,304,128]{2,1,0:T(8,128)(2,1)S(1)} %pad_maximum_fusion.7), channel_id=1, source_target_pairs={{0,2},{1,3},{2,0},{3,1},{4,6},{5,7},{6,4},{7,5},{8,10},{9,11},{10,... | collective-permute-start | bytes 466952 | tf_op jit(solution)/shard_map/ppermute | solution.py:419
  35.8 4.3 %collective-permute-start.8 = (bf16[4,304,128]{2,1,0:T(8,128)(2,1)S(1)}, bf16[4,304,128]{2,1,0:T(8,128)(2,1)S(1)}, u32[]{:S(2)}, u32[]{:S(2)}) collective-permute-start(bf16[4,304,128]{2,1,0:T(8,128)(2,1)S(1)} %pad_maximum_fusion.5), channel_id=1, source_target_pairs={{0,1},{1,0},{2,3},{3,2},{4,5},{5,4},{6,7},{7,6},{8,9},{9,8},{10,11... | collective-permute-start | bytes 933896 | tf_op jit(solution)/shard_map/ppermute | solution.py:419
  35.9 4.2 %collective-permute-start.9 = (bf16[4,48,128]{2,1,0:T(8,128)(2,1)S(1)}, bf16[4,48,128]{2,1,0:T(8,128)(2,1)S(1)}, u32[]{:S(2)}, u32[]{:S(2)}) collective-permute-start(bf16[4,48,128]{2,1,0:T(8,128)(2,1)S(1)} %pad_maximum_fusion.10), channel_id=1, source_target_pairs={{0,32},{1,33},{2,34},{3,35},{4,36},{5,37},{6,38},{7,39},{8,40},{9,... | collective-permute-start | bytes 147464 | tf_op jit(solution)/shard_map/ppermute | solution.py:419
  40.7 8.0 %collective-permute-start.10 = (bf16[1,688,128]{2,1,0:T(8,128)(2,1)S(1)}, bf16[1,688,128]{2,1,0:T(8,128)(2,1)S(1)}, u32[]{:S(2)}, u32[]{:S(2)}) collective-permute-start(bf16[1,688,128]{2,1,0:T(8,128)(2,1)S(1)} %shard_map.95), channel_id=1, source_target_pairs={{0,16},{1,17},{2,18},{3,19},{4,20},{5,21},{6,22},{7,23},{8,24},{9,... | collective-permute-start | bytes 528392 | tf_op jit(solution)/shard_map/ppermute | solution.py:419
  48.7 9.9 %collective-permute-start.11 = (bf16[2,688,128]{2,1,0:T(8,128)(2,1)S(1)}, bf16[2,688,128]{2,1,0:T(8,128)(2,1)S(1)}, u32[]{:S(2)}, u32[]{:S(2)}) collective-permute-start(bf16[2,688,128]{2,1,0:T(8,128)(2,1)S(1)} %pad_maximum_fusion.4), channel_id=1, source_target_pairs={{0,8},{1,9},{2,10},{3,11},{4,12},{5,13},{6,14},{7,15},{8,0},{9,1},... | collective-permute-start | bytes 1056776 | tf_op jit(solution)/shard_map/ppermute | solution.py:419
  59.1 10.2 %collective-permute-start.13 = (bf16[32,48,128]{2,1,0:T(8,128)(2,1)S(1)}, bf16[32,48,128]{2,1,0:T(8,128)(2,1)S(1)}, u32[]{:S(2)}, u32[]{:S(2)}) collective-permute-start(bf16[32,48,128]{2,1,0:T(8,128)(2,1)S(1)} %get-tuple-element.73), channel_id=1, source_target_pairs={{0,2},{1,3},{2,0},{3,1},{4,6},{5,7},{6,4},{7,5},{8,10},{9,11},{10,... | collective-permute-start | bytes 1179656 | tf_op jit(solution)/shard_map/ppermute | solution.py:419
  60.2 9.0 %collective-permute-start.12 = (bf16[1,480,128]{2,1,0:T(8,128)(2,1)S(1)}, bf16[1,480,128]{2,1,0:T(8,128)(2,1)S(1)}, u32[]{:S(2)}, u32[]{:S(2)}) collective-permute-start(bf16[1,480,128]{2,1,0:T(8,128)(2,1)S(1)} %get-tuple-element.72), channel_id=1, source_target_pairs={{0,64},{1,65},{2,66},{3,67},{4,68},{5,69},{6,70},{7,71},{8,72},{9,... | collective-permute-start | bytes 368648 | tf_op jit(solution)/shard_map/ppermute | solution.py:419
  69.3 8.8 %collective-permute-start.15 = (bf16[64,48,128]{2,1,0:T(8,128)(2,1)S(1)}, bf16[64,48,128]{2,1,0:T(8,128)(2,1)S(1)}, u32[]{:S(2)}, u32[]{:S(2)}) collective-permute-start(bf16[64,48,128]{2,1,0:T(8,128)(2,1)S(1)} %pad_maximum_fusion.own_roots), channel_id=1, source_target_pairs={{0,1},{1,0},{2,3},{3,2},{4,5},{5,4},{6,7},{7,6},{8,9},{9,8},{10,11... | collective-permute-start | bytes 2359304 | tf_op jit(solution)/shard_map/ppermute | solution.py:419
  69.4 15.3 %copy-start.2 = (s32[32,32]{1,0:T(8,128)S(1)}, s32[32,32]{1,0:T(8,128)}, u32[]{:S(2)}) copy-start(s32[32,32]{1,0:T(8,128)} %lists.1) | copy-start | bytes 12292
  69.4 8.6 %collective-permute-start.14 = (bf16[2,480,128]{2,1,0:T(8,128)(2,1)S(1)}, bf16[2,480,128]{2,1,0:T(8,128)(2,1)S(1)}, u32[]{:S(2)}, u32[]{:S(2)}) collective-permute-start(bf16[2,480,128]{2,1,0:T(8,128)(2,1)S(1)} %pad_maximum_fusion.6), channel_id=1, source_target_pairs={{0,32},{1,33},{2,34},{3,35},{4,36},{5,37},{6,38},{7,39},{8,40},{9,... | collective-permute-start | bytes 737288 | tf_op jit(solution)/shard_map/ppermute | solution.py:419

commit v5 on v4

--- a/solution.py
+++ b/solution.py
@@ -231,24 +231,40 @@
     )(points, weights)
 
 
-def other_kernel(first, second, w_first, w_second, _, __, sources, ws):
-    per = first.shape[0]
-    fill_forms(per, first, w_first, sources, ws)
-    fill_forms(2 * per, second, w_second, sources, ws)
-
-
-def other_forms(first, second, w_first, w_second, sources, ws):
+def other_kernel(first, second, _, __, sources, ws):
+    per = sources.shape[0] // 3
+    rhs = ws.shape[1]
+    rows = first.shape[1]
+    for i, ref in enumerate((first, second)):
+
+        def prepare(step, carry, i=i, ref=ref):
+            found = []
+            for u in range(16):
+                found.append(source_form(ref[step * 16 + u]))
+            for k in range(16 * rhs // rows):
+                block = ref[per + step * (16 * rhs // rows) + k]
+                for u in range(rows // rhs):
+                    at = (i + 1) * per + step * 16 + k * (rows // rhs) + u
+                    ws[at] = block[u * rhs : (u + 1) * rhs]
+            for u in range(16):
+                sources[(i + 1) * per + step * 16 + u] = found[u]
+            return carry
+
+        lax.fori_loop(0, per // 16, prepare, 0)
+
+
+def other_forms(first, second, sources, ws):
     return pl.pallas_call(
         other_kernel,
-        in_specs=[VMEM] * 6,
+        in_specs=[VMEM] * 4,
         out_specs=[VMEM] * 2,
         out_shape=[
             jax.ShapeDtypeStruct(sources.shape, bf16),
             jax.ShapeDtypeStruct(ws.shape, bf16),
         ],
-        input_output_aliases={4: 0, 5: 1},
+        input_output_aliases={2: 0, 3: 1},
         compiler_params=params(24),
-    )(first, second, w_first, w_second, sources, ws)
+    )(first, second, sources, ws)
 
 
 def near_place(place, per, leaf):
@@ -300,7 +316,40 @@
     )(place, lists, sources, targets, ws, *init)
 
 
-def tables_kernel(rhs, place, spots, own_roots, other_roots, held, sources, ws, x_all, picks):
+def root_forms(held, roots, spots, sources):
+    count = roots.shape[0]
+    nodes = sources.shape[0] // 2
+    dims = ROOT_ROWS - 16
+
+    def prepare(step, carry):
+        found = []
+        for u in range(0, 16, 2):
+            i = step * 16 + u
+            found.append(source_form(jnp.concatenate([roots[i, :dims], roots[i + 1, :dims]], axis=1)))
+        for u in range(16):
+            half = found[u // 2][u % 2 * WIDE : (u % 2 + 1) * WIDE]
+            sources[nodes + spots[held + step * 16 + u]] = half
+        return carry
+
+    lax.fori_loop(0, count // 16, prepare, 0)
+
+
+def own_roots_kernel(spots, roots, sources):
+    root_forms(0, roots, spots, sources)
+
+
+def own_root_forms(spots, roots):
+    rank = roots.shape[2]
+    return pl.pallas_call(
+        own_roots_kernel,
+        in_specs=[SMEM, VMEM],
+        out_specs=VMEM,
+        out_shape=jax.ShapeDtypeStruct((4 * roots.shape[0], rank, WIDE), bf16),
+        compiler_params=params(24),
+    )(spots, roots)
+
+
+def tables_kernel(rhs, place, spots, own_roots, other_roots, held, _, sources, ws, x_all, picks):
     half_roots, _, rank = own_roots.shape
     nodes = 2 * half_roots
     dims = x_all.shape[1]
@@ -365,6 +414,8 @@
         lax.fori_loop(0, half // group, select, 0)
         half //= 2
 
+    root_forms(half_roots, other_roots, spots, sources)
+
     def prepare(step, carry):
         found = []
         for u in range(16):
@@ -376,27 +427,28 @@
             sources[2 * i + 1] = found[u][rank:]
         return carry
 
-    lax.fori_loop(0, nodes // 16, prepare, 0)
-
-
-def far_tables(rhs, place, spots, own_roots, other_roots, held):
+    lax.fori_loop(0, nodes // 32, prepare, 0)
+
+
+def far_tables(rhs, place, spots, own_roots, other_roots, held, sources):
     nodes = 2 * own_roots.shape[0]
     rank = own_roots.shape[2]
     dims = ROOT_ROWS - 16
     return pl.pallas_call(
         functools.partial(tables_kernel, rhs),
-        in_specs=[SMEM] * 2 + [VMEM] * 3,
+        in_specs=[SMEM] * 2 + [VMEM] * 4,
         out_specs=[VMEM] * 2,
         out_shape=[
-            jax.ShapeDtypeStruct((2 * nodes, rank, WIDE), bf16),
+            jax.ShapeDtypeStruct(sources.shape, bf16),
             jax.ShapeDtypeStruct((2 * nodes, rhs, rank), bf16),
         ],
         scratch_shapes=[
             pltpu.VMEM((2 * nodes, dims, rank), bf16),
             pltpu.VMEM((nodes, 1, rank), f32),
         ],
+        input_output_aliases={5: 0},
         compiler_params=params(24),
-    )(place, spots, own_roots, other_roots, held)
+    )(place, spots, own_roots, other_roots, held, sources)
 
 
 def home_of(node):
@@ -436,10 +488,9 @@
     bridges = [(i, i + 1) for i in range(1, size - 1, 2)]
     bridges = bridges + [(j, i) for i, j in bridges]
     maps = lax.ppermute(top_maps, "leaf", [(n, home_of(n)) for n in range(size)])
-    first = lax.ppermute(points, "leaf", pairs)
-    w_first = lax.ppermute(weights, "leaf", pairs)
-    second = lax.ppermute(points, "leaf", bridges)
-    w_second = lax.ppermute(weights, "leaf", bridges)
+    own = jnp.concatenate([points, weights.reshape(-1, dims, leaf_size)], axis=0)
+    first = lax.ppermute(own, "leaf", pairs)
+    second = lax.ppermute(own, "leaf", bridges)
 
     root = upward(points, weights, leaf_maps, root_maps, root_picks, top_picks)
 
@@ -461,7 +512,7 @@
     sources, ws, targets = own_forms(points, weights)
     held, sources = tie((held, sources))
     root = held[:, MAP_ROWS:]
-    sources, ws = other_forms(first, second, w_first, w_second, sources, ws)
+    sources, ws = other_forms(first, second, sources, ws)
     sources, columns, held, root = tie((sources, columns, held, root))
     held, root = swaps(1, 2, held, root)
     near_part(4)
@@ -480,17 +531,20 @@
     held, root = swaps(5, 64, held, root)
     near_part(8)
     nears[-1], columns, held, root = tie((nears[-1], columns, held, root))
-    held = both(held, 32, size)
-    other_roots = swap(root, ROOT_STEPS[6], size)
-    near_part(4)
-    nears[-1], held, root, other_roots = tie((nears[-1], held, root, other_roots))
-
     index = jnp.arange(size, dtype=jnp.int32)
     spots = place
     for k, mask in enumerate(ROOT_STEPS):
         spots = spots ^ jnp.where(((index >> k) & 1) != 0, mask, 0)
+    held = both(held, 32, size)
+    other_roots = swap(root, ROOT_STEPS[6], size)
+    root_sources = own_root_forms(spots, root)
+    near_part(4)
+    nears[-1], root_sources, held, root, other_roots = tie(
+        (nears[-1], root_sources, held, root, other_roots)
+    )
+
     near = jnp.concatenate(nears, axis=0)
-    far_sources, far_ws = far_tables(rhs, place, spots, root, other_roots, held)
+    far_sources, far_ws = far_tables(rhs, place, spots, root, other_roots, held, root_sources)
     return field(False, 0, per, place, far_lists, far_sources, targets, far_ws, near)
 
 

time: 115 us -> 114 us (level)
  starting transfers between devices: 26.5 us -> 20.2 us
  local copies, waits for them, and re-layouts: 1.94 us -> 3.89 us
  waiting for transfers between devices: 9.68 us -> 11.6 us
  Pallas kernels: 75.1 us -> 76.3 us
    ppermute x11, starting transfers between devices: 15.9 us -> 9.72 us  [swap(): return lax.ppermute(x, 'leaf', [(i, i ^ mask) for i in range(size)])]
    ppermute x11, waiting for transfers between devices: 9.66 us -> 11.6 us  [swap(): return lax.ppermute(x, 'leaf', [(i, i ^ mask) for i in range(size)])]
    pallas_call x1 -> x2, Pallas kernels: 1.47 us -> 2.9 us  [the longest x1 1.46 us: other_forms(): pl.pallas_call(other_kernel, in_specs=[VMEM] * 4, out_specs=[VMEM] * 2, o...]
    unnamed x12 -> x13, local copies, waits for them, and re-layouts: 1.92 us -> 3.01 us
    ppermute x4 -> x2, starting transfers between devices: 2.3 us -> 2.3 us  [the longest x1 1.6 us: on_device(): first = lax.ppermute(own, 'leaf', pairs)]
  transfers between devices with their start and end apart: 16 -> 14, of which waited for: 5 -> 6; matrix products, arithmetic and copies ran while one was open for 1% -> 3% of each run, Pallas kernels for 32% -> 33%
where the time goes in v5:
time: 114 us; the launch traced here: 113 us
  Pallas kernels  76.3 us (67%)
  starting transfers between devices  20.2 us (18%)
  waiting for transfers between devices  11.6 us (10%)
  local copies, waits for them, and re-layouts  3.89 us (3%)
    pallas_call x6, Pallas kernels, field(): pl.pallas_call(functools.partial(field_kernel, 4, 1024 // columns, start,...  61.7 us
    ppermute x11, waiting for transfers between devices, swap(): return lax.ppermute(x, 'leaf', [(i, i ^ mask) for i in range(size)])  11.6 us
    ppermute x11, starting transfers between devices, swap(): return lax.ppermute(x, 'leaf', [(i, i ^ mask) for i in range(size)])  9.72 us
    ppermute x1, starting transfers between devices, on_device(): lax.ppermute(top_maps, 'leaf', [(n, home_of(n)) for n in range(size)])  8.21 us
    pallas_call x1, Pallas kernels, far_tables(): pl.pallas_call(functools.partial(tables_kernel, rhs), in_specs=[SMEM] * 2...  6 us
    pallas_call x1, Pallas kernels, upward(): pl.pallas_call(upward_kernel, in_specs=[VMEM] * 6, out_specs=VMEM, out_sh...  4.12 us
    unnamed x13, local copies, waits for them, and re-layouts  3.01 us
  transfers between devices with their start and end apart: 14, of which 6 were waited for; matrix products, arithmetic and copies ran while one was open for 3% of the time, Pallas kernels for 33%

profile of v5, /device:TPU:0, one launch (start us, length us, event | category | flops | bytes accessed | tf_op | source)
XLA Modules:
  0.0 113.4 jit_solution(8560175404397752418)
XLA Ops:
  0.0 8.2 %collective-permute-start.2 = (bf16[1,128,256]{2,1,0:T(8,128)(2,1)}, bf16[1,128,256]{2,1,0:T(8,128)(2,1)S(1)}, u32[]{:S(2)}, u32[]{:S(2)}) collective-permute-start(bf16[1,128,256]{2,1,0:T(8,128)(2,1)} %param.13), channel_id=1, source_target_pairs={{0,127},{1,95},{2,31},{3,63},{4,23},{5,55},{6,87},{7,119},{8,7},{9... | collective-permute-start | bytes 196616 | tf_op jit(solution)/shard_map/ppermute | solution.py:490
  8.2 0.9 reshape.8
  9.1 1.1 constant_dynamic-update-slice_fusion.1
  10.2 0.0 copy-start.3
  10.2 0.7 collective-permute-start.1
  10.9 1.6 %collective-permute-start = (bf16[36,32,256]{2,1,0:T(8,128)(2,1)S(1)}, bf16[36,32,256]{2,1,0:T(8,128)(2,1)S(1)}, u32[]{:S(2)}, u32[]{:S(2)}) collective-permute-start(bf16[36,32,256]{2,1,0:T(8,128)(2,1)S(1)} %constant_dynamic-update-slice_fusion), channel_id=1, source_target_pairs={{0,1},{1,0},{2,3},{3,2},{4,5},{5,4},{6,7},{7,6},{8,9},{9,8},{10,11... | collective-permute-start | bytes 1769480 | tf_op jit(solution)/shard_map/ppermute | solution.py:492
  12.5 4.1 %shard_map.91 = bf16[1,48,128]{2,1,0:T(8,128)(2,1)} custom-call(bf16[32,32,256]{2,1,0:T(8,128)(2,1)} %points.2, bf16[32,4,256]{2,1,0:T(4,128)(2,1)} %weights.2, bf16[32,128,256]{2,1,0:T(8,128)(2,1)} %leaf_maps.1, bf16[1,128,4096]{2,1,0:T(8,128)(2,1)} %root_maps.1, s32[1,128]{1,0:T(1,128)} %picks.1, s32[1,128]{1,0:T(1,128)} %top_picks.1), custom_call_target="tpu_custom_call" | custom-call | tf_op jit(solution)/shard_map/pallas_call | solution.py:99
  16.6 0.0 collective-permute-done.2
  16.6 0.7 pad_maximum_fusion.9
  17.3 1.9 %collective-permute-start.3 = (bf16[1,304,128]{2,1,0:T(8,128)(2,1)S(1)}, bf16[1,304,128]{2,1,0:T(8,128)(2,1)S(1)}, u32[]{:S(2)}, u32[]{:S(2)}) collective-permute-start(bf16[1,304,128]{2,1,0:T(8,128)(2,1)S(1)} %pad_maximum_fusion.9), channel_id=1, source_target_pairs={{0,4},{1,5},{2,6},{3,7},{4,0},{5,1},{6,2},{7,3},{8,12},{9,13},{10,... | collective-permute-start | bytes 233480 | tf_op jit(solution)/shard_map/ppermute | solution.py:471
  19.2 1.0 copy-done
  20.2 0.8 copy-done.1
  21.1 0.8 shard_map.92
  21.8 1.4 %collective-permute-done.3 = bf16[1,304,128]{2,1,0:T(8,128)(2,1)S(1)} collective-permute-done((bf16[1,304,128]{2,1,0:T(8,128)(2,1)S(1)}, bf16[1,304,128]{2,1,0:T(8,128)(2,1)S(1)}, u32[]{:S(2)}, u32[]{:S(2)}) %collective-permute-start.3) | collective-permute-done | bytes 77856 | tf_op jit(solution)/shard_map/ppermute | solution.py:471
  23.3 0.0 collective-permute-done.1.second
  23.3 1.5 %shard_map.93 = (bf16[96,256,128]{2,1,0:T(8,128)(2,1)S(1)}, bf16[96,4,256]{2,1,0:T(4,128)(2,1)S(1)}) custom-call(bf16[36,32,256]{2,1,0:T(8,128)(2,1)S(1)} %collective-permute-done.first, bf16[36,32,256]{2,1,0:T(8,128)(2,1)S(1)} %collective-permute-done.1.second, ...), custom_call_target="tpu_custom_call", output_to_operand_aliasing={{0}: (2, {}), {1}: (3, {})} | custom-call | tf_op jit(solution)/shard_map/pallas_call | solution.py:257
  24.8 3.1 %collective-permute-start.5 = (bf16[2,48,128]{2,1,0:T(8,128)(2,1)S(1)}, bf16[2,48,128]{2,1,0:T(8,128)(2,1)S(1)}, u32[]{:S(2)}, u32[]{:S(2)}) collective-permute-start(bf16[2,48,128]{2,1,0:T(8,128)(2,1)S(1)} %slice.11), channel_id=1, source_target_pairs={{0,64},{1,65},{2,66},{3,67},{4,68},{5,69},{6,70},{7,71},{8,72},{9,... | collective-permute-start | bytes 73736 | tf_op jit(solution)/shard_map/ppermute | solution.py:471
  27.8 4.2 %shard_map.94 = f32[4,4,256]{2,1,0:T(4,128)S(1)} custom-call(s32[1]{0:T(128)} %bitcast.place, s32[16,32]{1,0:T(8,128)S(1)} %bitcast.2, bf16[96,256,128]{2,1,0:T(8,128)(2,1)S(1)} %get-tuple-element.56.sources, bf16[32,128,256]{2,1,0:T(8,128)(2,1)S(1)} %get-tuple-element.57.targets, bf16[96,4,256]{2,1,0:T(4,128)(2,1)S(1)} %get-tuple-element.58.ws), custom_call_target="tpu_custom_call" | custom-call | flops 4294967296 | bytes 1048576 | tf_op jit(solution)/shard_map/pallas_call | solution.py:309
  32.0 0.0 collective-permute-done.5
  32.0 1.1 %collective-permute-done.4 = bf16[2,304,128]{2,1,0:T(8,128)(2,1)S(1)} collective-permute-done((bf16[2,304,128]{2,1,0:T(8,128)(2,1)S(1)}, bf16[2,304,128]{2,1,0:T(8,128)(2,1)S(1)}, u32[]{:S(2)}, u32[]{:S(2)}) %collective-permute-start.4) | collective-permute-done | bytes 155680 | tf_op jit(solution)/shard_map/ppermute | solution.py:471
  33.2 0.1 collective-permute-start.6
  33.3 0.1 collective-permute-start.7
  33.4 4.1 %collective-permute-done.7 = bf16[4,48,128]{2,1,0:T(8,128)(2,1)S(1)} collective-permute-done((bf16[4,48,128]{2,1,0:T(8,128)(2,1)S(1)}, bf16[4,48,128]{2,1,0:T(8,128)(2,1)S(1)}, u32[]{:S(2)}, u32[]{:S(2)}) %collective-permute-start.7) | collective-permute-done | bytes 49184 | tf_op jit(solution)/shard_map/ppermute | solution.py:471
  37.5 0.0 collective-permute-done.6
  37.6 0.1 pad_maximum_fusion.2.held
  37.6 0.5 shard_map.95
  38.1 1.4 %collective-permute-start.8 = (bf16[1,688,128]{2,1,0:T(8,128)(2,1)S(1)}, bf16[1,688,128]{2,1,0:T(8,128)(2,1)S(1)}, u32[]{:S(2)}, u32[]{:S(2)}) collective-permute-start(bf16[1,688,128]{2,1,0:T(8,128)(2,1)S(1)} %shard_map.95), channel_id=1, source_target_pairs={{0,16},{1,17},{2,18},{3,19},{4,20},{5,21},{6,22},{7,23},{8,24},{9,... | collective-permute-start | bytes 528392 | tf_op jit(solution)/shard_map/ppermute | solution.py:471
  39.4 7.7 %shard_map.96 = f32[8,4,256]{2,1,0:T(4,128)S(1)} custom-call(s32[1]{0:T(128)} %bitcast.place, s32[16,32]{1,0:T(8,128)S(1)} %bitcast.3, bf16[96,256,128]{2,1,0:T(8,128)(2,1)S(1)} %get-tuple-element.56.sources, bf16[32,128,256]{2,1,0:T(8,128)(2,1)S(1)} %get-tuple-element.57.targets, bf16[96,4,256]{2,1,0:T(4,128)(2,1)S(1)} %get-tuple-element.58.ws), custom_call_target="tpu_custom_call" | custom-call | flops 8589934592 | bytes 1048576 | tf_op jit(solution)/shard_map/pallas_call | solution.py:309
  47.2 0.0 collective-permute-done.8
  47.2 0.1 collective-permute-start.9
  47.3 7.7 %shard_map.97 = f32[8,4,256]{2,1,0:T(4,128)S(1)} custom-call(s32[1]{0:T(128)} %bitcast.place, s32[16,32]{1,0:T(8,128)S(1)} %bitcast.4, bf16[96,256,128]{2,1,0:T(8,128)(2,1)S(1)} %get-tuple-element.56.sources, bf16[32,128,256]{2,1,0:T(8,128)(2,1)S(1)} %get-tuple-element.57.targets, bf16[96,4,256]{2,1,0:T(4,128)(2,1)S(1)} %get-tuple-element.58.ws), custom_call_target="tpu_custom_call" | custom-call | flops 8589934592 | bytes 1048576 | tf_op jit(solution)/shard_map/pallas_call | solution.py:309
  55.1 1.8 %collective-permute-done.9 = bf16[2,688,128]{2,1,0:T(8,128)(2,1)S(1)} collective-permute-done((bf16[2,688,128]{2,1,0:T(8,128)(2,1)S(1)}, bf16[2,688,128]{2,1,0:T(8,128)(2,1)S(1)}, u32[]{:S(2)}, u32[]{:S(2)}) %collective-permute-start.9) | collective-permute-done | bytes 352288 | tf_op jit(solution)/shard_map/ppermute | solution.py:471
  56.9 0.1 pad_maximum_fusion.1.held
  57.0 0.3 shard_map.98
  57.3 1.3 %collective-permute-start.10 = (bf16[1,480,128]{2,1,0:T(8,128)(2,1)S(1)}, bf16[1,480,128]{2,1,0:T(8,128)(2,1)S(1)}, u32[]{:S(2)}, u32[]{:S(2)}) collective-permute-start(bf16[1,480,128]{2,1,0:T(8,128)(2,1)S(1)} %get-tuple-element.73), channel_id=1, source_target_pairs={{0,64},{1,65},{2,66},{3,67},{4,68},{5,69},{6,70},{7,71},{8,72},{9,... | collective-permute-start | bytes 368648 | tf_op jit(solution)/shard_map/ppermute | solution.py:471
  58.5 0.8 collective-permute-start.11
  59.3 7.7 %shard_map.99 = f32[8,4,256]{2,1,0:T(4,128)S(1)} custom-call(s32[1]{0:T(128)} %bitcast.place, s32[16,32]{1,0:T(8,128)S(1)} %bitcast.5, bf16[96,256,128]{2,1,0:T(8,128)(2,1)S(1)} %get-tuple-element.56.sources, bf16[32,128,256]{2,1,0:T(8,128)(2,1)S(1)} %get-tuple-element.57.targets, bf16[96,4,256]{2,1,0:T(4,128)(2,1)S(1)} %get-tuple-element.58.ws), custom_call_target="tpu_custom_call" | custom-call | flops 8589934592 | bytes 1048576 | tf_op jit(solution)/shard_map/pallas_call | solution.py:309
  67.1 0.0 collective-permute-done.10
  67.1 1.2 %collective-permute-done.11 = bf16[32,48,128]{2,1,0:T(8,128)(2,1)S(1)} collective-permute-done((bf16[32,48,128]{2,1,0:T(8,128)(2,1)S(1)}, bf16[32,48,128]{2,1,0:T(8,128)(2,1)S(1)}, u32[]{:S(2)}, u32[]{:S(2)}) %collective-permute-start.11) | collective-permute-done | bytes 393248 | tf_op jit(solution)/shard_map/ppermute | solution.py:471
  68.3 0.1 pad_maximum_fusion.roots.own_roots
  68.4 0.1 collective-permute-start.13
  68.5 1.1 collective-permute-start.12
  69.6 4.2 %shard_map.100 = f32[4,4,256]{2,1,0:T(4,128)S(1)} custom-call(s32[1]{0:T(128)} %bitcast.place, s32[16,32]{1,0:T(8,128)S(1)} %bitcast.6, bf16[96,256,128]{2,1,0:T(8,128)(2,1)S(1)} %get-tuple-element.56.sources, bf16[32,128,256]{2,1,0:T(8,128)(2,1)S(1)} %get-tuple-element.57.targets, bf16[96,4,256]{2,1,0:T(4,128)(2,1)S(1)} %get-tuple-element.58.ws), custom_call_target="tpu_custom_call" | custom-call | flops 4294967296 | bytes 1048576 | tf_op jit(solution)/shard_map/pallas_call | solution.py:309
  73.8 1.4 %shard_map.101._ = bf16[256,128,128]{2,1,0:T(8,128)(2,1)S(1)} custom-call(s32[128]{0:T(128)S(1)} %fusion.6.spots, bf16[64,48,128]{2,1,0:T(8,128)(2,1)S(1)} %pad_maximum_fusion.roots.own_roots), custom_call_target="tpu_custom_call" | custom-call | tf_op jit(solution)/shard_map/pallas_call | solution.py:343
  75.2 0.0 copy-start.2
  75.2 1.9 %collective-permute-done.12 = bf16[2,480,128]{2,1,0:T(8,128)(2,1)S(1)} collective-permute-done((bf16[2,480,128]{2,1,0:T(8,128)(2,1)S(1)}, bf16[2,480,128]{2,1,0:T(8,128)(2,1)S(1)}, u32[]{:S(2)}, u32[]{:S(2)}) %collective-permute-start.12) | collective-permute-done | bytes 245792 | tf_op jit(solution)/shard_map/ppermute | solution.py:471
  77.2 6.0 %shard_map.102 = (bf16[256,128,128]{2,1,0:T(8,128)(2,1)S(1)}, bf16[256,4,128]{2,1,0:T(4,128)(2,1)S(1)}) custom-call(s32[1]{0:T(128)} %bitcast.place, s32[128]{0:T(128)S(1)} %fusion.6.spots, bf16[64,48,128]{2,1,0:T(8,128)(2,1)S(1)} %pad_maximum_fusion.roots.own_roots, ...), custom_call_target="tpu_custom_call", output_to_operand_aliasing={{0}: (5, {})} | custom-call | tf_op jit(solution)/shard_map/pallas_call | solution.py:437
  83.2 30.1 %shard_map.103 = f32[32,4,256]{2,1,0:T(4,128)} custom-call(s32[1]{0:T(128)} %bitcast.place, s32[32,32]{1,0:T(8,128)S(1)} %copy-done.2, bf16[256,128,128]{2,1,0:T(8,128)(2,1)S(1)} %get-tuple-element.82.sources, bf16[32,128,256]{2,1,0:T(8,128)(2,1)S(1)} %get-tuple-element.57.targets, bf16[256,4,128]{2,1,0:T(4,128)(2,1)S(1)} %get-tuple-element.83.ws, ...), custom_call_target="tpu_custom_call" | custom-call | flops 34359738368 | bytes 1048576 | tf_op jit(solution)/shard_map/pallas_call | solution.py:309
  (23 shorter events, 0.3 us)
Async XLA Ops:
  0.0 16.6 %collective-permute-start.2 = (bf16[1,128,256]{2,1,0:T(8,128)(2,1)}, bf16[1,128,256]{2,1,0:T(8,128)(2,1)S(1)}, u32[]{:S(2)}, u32[]{:S(2)}) collective-permute-start(bf16[1,128,256]{2,1,0:T(8,128)(2,1)} %param.13), channel_id=1, source_target_pairs={{0,127},{1,95},{2,31},{3,63},{4,23},{5,55},{6,87},{7,119},{8,7},{9... | collective-permute-start | bytes 196616 | tf_op jit(solution)/shard_map/ppermute | solution.py:490
  10.2 17.7 %copy-start.3 = (s32[32,16]{0,1:T(8,128)S(1)}, s32[32,16]{0,1:T(8,128)}, u32[]{:S(2)}) copy-start(s32[32,16]{0,1:T(8,128)} %param.16) | copy-start | bytes 6148
  10.2 13.1 %collective-permute-start.1 = (bf16[36,32,256]{2,1,0:T(8,128)(2,1)S(1)}, bf16[36,32,256]{2,1,0:T(8,128)(2,1)S(1)}, u32[]{:S(2)}, u32[]{:S(2)}) collective-permute-start(bf16[36,32,256]{2,1,0:T(8,128)(2,1)S(1)} %constant_dynamic-update-slice_fusion), channel_id=1, source_target_pairs={{1,2},{3,4},{5,6},{7,8},{9,10},{11,12},{13,14},{15,16},{17,18},{19... | collective-permute-start | bytes 1769480 | tf_op jit(solution)/shard_map/ppermute | solution.py:493
  10.9 12.4 %collective-permute-start = (bf16[36,32,256]{2,1,0:T(8,128)(2,1)S(1)}, bf16[36,32,256]{2,1,0:T(8,128)(2,1)S(1)}, u32[]{:S(2)}, u32[]{:S(2)}) collective-permute-start(bf16[36,32,256]{2,1,0:T(8,128)(2,1)S(1)} %constant_dynamic-update-slice_fusion), channel_id=1, source_target_pairs={{0,1},{1,0},{2,3},{3,2},{4,5},{5,4},{6,7},{7,6},{8,9},{9,8},{10,11... | collective-permute-start | bytes 1769480 | tf_op jit(solution)/shard_map/ppermute | solution.py:492
  17.3 5.9 %collective-permute-start.3 = (bf16[1,304,128]{2,1,0:T(8,128)(2,1)S(1)}, bf16[1,304,128]{2,1,0:T(8,128)(2,1)S(1)}, u32[]{:S(2)}, u32[]{:S(2)}) collective-permute-start(bf16[1,304,128]{2,1,0:T(8,128)(2,1)S(1)} %pad_maximum_fusion.9), channel_id=1, source_target_pairs={{0,4},{1,5},{2,6},{3,7},{4,0},{5,1},{6,2},{7,3},{8,12},{9,13},{10,... | collective-permute-start | bytes 233480 | tf_op jit(solution)/shard_map/ppermute | solution.py:471
  19.2 1.0 copy-start
  20.2 0.8 copy-start.1
  24.8 7.3 %collective-permute-start.5 = (bf16[2,48,128]{2,1,0:T(8,128)(2,1)S(1)}, bf16[2,48,128]{2,1,0:T(8,128)(2,1)S(1)}, u32[]{:S(2)}, u32[]{:S(2)}) collective-permute-start(bf16[2,48,128]{2,1,0:T(8,128)(2,1)S(1)} %slice.11), channel_id=1, source_target_pairs={{0,64},{1,65},{2,66},{3,67},{4,68},{5,69},{6,70},{7,71},{8,72},{9,... | collective-permute-start | bytes 73736 | tf_op jit(solution)/shard_map/ppermute | solution.py:471
  27.8 5.4 %collective-permute-start.4 = (bf16[2,304,128]{2,1,0:T(8,128)(2,1)S(1)}, bf16[2,304,128]{2,1,0:T(8,128)(2,1)S(1)}, u32[]{:S(2)}, u32[]{:S(2)}) collective-permute-start(bf16[2,304,128]{2,1,0:T(8,128)(2,1)S(1)} %pad_maximum_fusion.7), channel_id=1, source_target_pairs={{0,2},{1,3},{2,0},{3,1},{4,6},{5,7},{6,4},{7,5},{8,10},{9,11},{10,... | collective-permute-start | bytes 466952 | tf_op jit(solution)/shard_map/ppermute | solution.py:471
  33.2 4.3 %collective-permute-start.6 = (bf16[4,304,128]{2,1,0:T(8,128)(2,1)S(1)}, bf16[4,304,128]{2,1,0:T(8,128)(2,1)S(1)}, u32[]{:S(2)}, u32[]{:S(2)}) collective-permute-start(bf16[4,304,128]{2,1,0:T(8,128)(2,1)S(1)} %pad_maximum_fusion.5), channel_id=1, source_target_pairs={{0,1},{1,0},{2,3},{3,2},{4,5},{5,4},{6,7},{7,6},{8,9},{9,8},{10,11... | collective-permute-start | bytes 933896 | tf_op jit(solution)/shard_map/ppermute | solution.py:471
  33.3 4.2 %collective-permute-start.7 = (bf16[4,48,128]{2,1,0:T(8,128)(2,1)S(1)}, bf16[4,48,128]{2,1,0:T(8,128)(2,1)S(1)}, u32[]{:S(2)}, u32[]{:S(2)}) collective-permute-start(bf16[4,48,128]{2,1,0:T(8,128)(2,1)S(1)} %pad_maximum_fusion.10), channel_id=1, source_target_pairs={{0,32},{1,33},{2,34},{3,35},{4,36},{5,37},{6,38},{7,39},{8,40},{9,... | collective-permute-start | bytes 147464 | tf_op jit(solution)/shard_map/ppermute | solution.py:471
  38.1 9.1 %collective-permute-start.8 = (bf16[1,688,128]{2,1,0:T(8,128)(2,1)S(1)}, bf16[1,688,128]{2,1,0:T(8,128)(2,1)S(1)}, u32[]{:S(2)}, u32[]{:S(2)}) collective-permute-start(bf16[1,688,128]{2,1,0:T(8,128)(2,1)S(1)} %shard_map.95), channel_id=1, source_target_pairs={{0,16},{1,17},{2,18},{3,19},{4,20},{5,21},{6,22},{7,23},{8,24},{9,... | collective-permute-start | bytes 528392 | tf_op jit(solution)/shard_map/ppermute | solution.py:471
  47.2 9.7 %collective-permute-start.9 = (bf16[2,688,128]{2,1,0:T(8,128)(2,1)S(1)}, bf16[2,688,128]{2,1,0:T(8,128)(2,1)S(1)}, u32[]{:S(2)}, u32[]{:S(2)}) collective-permute-start(bf16[2,688,128]{2,1,0:T(8,128)(2,1)S(1)} %pad_maximum_fusion.4), channel_id=1, source_target_pairs={{0,8},{1,9},{2,10},{3,11},{4,12},{5,13},{6,14},{7,15},{8,0},{9,1},... | collective-permute-start | bytes 1056776 | tf_op jit(solution)/shard_map/ppermute | solution.py:471
  57.3 9.8 %collective-permute-start.10 = (bf16[1,480,128]{2,1,0:T(8,128)(2,1)S(1)}, bf16[1,480,128]{2,1,0:T(8,128)(2,1)S(1)}, u32[]{:S(2)}, u32[]{:S(2)}) collective-permute-start(bf16[1,480,128]{2,1,0:T(8,128)(2,1)S(1)} %get-tuple-element.73), channel_id=1, source_target_pairs={{0,64},{1,65},{2,66},{3,67},{4,68},{5,69},{6,70},{7,71},{8,72},{9,... | collective-permute-start | bytes 368648 | tf_op jit(solution)/shard_map/ppermute | solution.py:471
  58.5 9.8 %collective-permute-start.11 = (bf16[32,48,128]{2,1,0:T(8,128)(2,1)S(1)}, bf16[32,48,128]{2,1,0:T(8,128)(2,1)S(1)}, u32[]{:S(2)}, u32[]{:S(2)}) collective-permute-start(bf16[32,48,128]{2,1,0:T(8,128)(2,1)S(1)} %get-tuple-element.74), channel_id=1, source_target_pairs={{0,2},{1,3},{2,0},{3,1},{4,6},{5,7},{6,4},{7,5},{8,10},{9,11},{10,... | collective-permute-start | bytes 1179656 | tf_op jit(solution)/shard_map/ppermute | solution.py:471
  68.4 8.8 %collective-permute-start.13 = (bf16[64,48,128]{2,1,0:T(8,128)(2,1)S(1)}, bf16[64,48,128]{2,1,0:T(8,128)(2,1)S(1)}, u32[]{:S(2)}, u32[]{:S(2)}) collective-permute-start(bf16[64,48,128]{2,1,0:T(8,128)(2,1)S(1)} %pad_maximum_fusion.roots.own_roots), channel_id=1, source_target_pairs={{0,1},{1,0},{2,3},{3,2},{4,5},{5,4},{6,7},{7,6},{8,9},{9,8},{10,11... | collective-permute-start | bytes 2359304 | tf_op jit(solution)/shard_map/ppermute | solution.py:471
  68.5 8.6 %collective-permute-start.12 = (bf16[2,480,128]{2,1,0:T(8,128)(2,1)S(1)}, bf16[2,480,128]{2,1,0:T(8,128)(2,1)S(1)}, u32[]{:S(2)}, u32[]{:S(2)}) collective-permute-start(bf16[2,480,128]{2,1,0:T(8,128)(2,1)S(1)} %pad_maximum_fusion.6), channel_id=1, source_target_pairs={{0,32},{1,33},{2,34},{3,35},{4,36},{5,37},{6,38},{7,39},{8,40},{9,... | collective-permute-start | bytes 737288 | tf_op jit(solution)/shard_map/ppermute | solution.py:471
  75.2 8.0 %copy-start.2 = (s32[32,32]{1,0:T(8,128)S(1)}, s32[32,32]{1,0:T(8,128)}, u32[]{:S(2)}) copy-start(s32[32,32]{1,0:T(8,128)} %lists.1) | copy-start | bytes 12292

commit v6 on v5

--- a/solution.py
+++ b/solution.py
@@ -193,18 +193,24 @@
     )(place, held)
 
 
-def fill_forms(first, points, weights, sources, ws, targets=None):
-    per = points.shape[0]
+def fill_forms(first, leaves, sources, ws, targets=None):
+    per = sources.shape[0] // 3
+    rhs = ws.shape[1]
+    rows = leaves.shape[1]
 
     def prepare(step, carry):
         found = []
         for u in range(16):
-            x = points[step * 16 + u]
+            x = leaves[step * 16 + u]
             found.append((source_form(x), None if targets is None else target_form(x)))
+        for k in range(16 * rhs // rows):
+            block = leaves[per + step * (16 * rhs // rows) + k]
+            for u in range(rows // rhs):
+                at = first + step * 16 + k * (rows // rhs) + u
+                ws[at] = block[u * rhs : (u + 1) * rhs]
         for u in range(16):
             g = step * 16 + u
             sources[first + g] = found[u][0]
-            ws[first + g] = weights[g]
             if targets is not None:
                 targets[g] = found[u][1]
         return carry
@@ -212,45 +218,29 @@
     lax.fori_loop(0, per // 16, prepare, 0)
 
 
-def own_kernel(points, weights, sources, ws, targets):
-    fill_forms(0, points, weights, sources, ws, targets)
-
-
-def own_forms(points, weights):
-    per, _, leaf_size = points.shape
+def own_kernel(own, sources, ws, targets):
+    fill_forms(0, own, sources, ws, targets)
+
+
+def own_forms(own, per, rhs):
+    leaf_size = own.shape[2]
     return pl.pallas_call(
         own_kernel,
-        in_specs=[VMEM] * 2,
+        in_specs=[VMEM],
         out_specs=[VMEM] * 3,
         out_shape=[
             jax.ShapeDtypeStruct((3 * per, leaf_size, WIDE), bf16),
-            jax.ShapeDtypeStruct((3 * per,) + weights.shape[1:], bf16),
+            jax.ShapeDtypeStruct((3 * per, rhs, leaf_size), bf16),
             jax.ShapeDtypeStruct((per, WIDE, leaf_size), bf16),
         ],
         compiler_params=params(24),
-    )(points, weights)
+    )(own)
 
 
 def other_kernel(first, second, _, __, sources, ws):
     per = sources.shape[0] // 3
-    rhs = ws.shape[1]
-    rows = first.shape[1]
-    for i, ref in enumerate((first, second)):
-
-        def prepare(step, carry, i=i, ref=ref):
-            found = []
-            for u in range(16):
-                found.append(source_form(ref[step * 16 + u]))
-            for k in range(16 * rhs // rows):
-                block = ref[per + step * (16 * rhs // rows) + k]
-                for u in range(rows // rhs):
-                    at = (i + 1) * per + step * 16 + k * (rows // rhs) + u
-                    ws[at] = block[u * rhs : (u + 1) * rhs]
-            for u in range(16):
-                sources[(i + 1) * per + step * 16 + u] = found[u]
-            return carry
-
-        lax.fori_loop(0, per // 16, prepare, 0)
+    fill_forms(per, first, sources, ws)
+    fill_forms(2 * per, second, sources, ws)
 
 
 def other_forms(first, second, sources, ws):
@@ -298,8 +288,10 @@
         return carry
 
     lax.fori_loop(0, out.shape[0] // unroll, leaves, 0)
-    if len(rest) > 1:
-        out[...] = out[...] + rest[0][...]
+    at = 0
+    for part in rest[:-1]:
+        out[at : at + part.shape[0]] = out[at : at + part.shape[0]] + part[...]
+        at += part.shape[0]
 
 
 def field(near, start, count, place, lists, sources, targets, ws, *init):
@@ -507,9 +499,9 @@
 
     half = maps.shape[2] // 2
     held = jnp.concatenate([maps[:, :, :half], maps[:, :, half:], root], axis=1)
-    held, points, weights = tie((held, points, weights))
+    held, own = tie((held, own))
     held = both(held, 4, size)
-    sources, ws, targets = own_forms(points, weights)
+    sources, ws, targets = own_forms(own, per, rhs)
     held, sources = tie((held, sources))
     root = held[:, MAP_ROWS:]
     sources, ws = other_forms(first, second, sources, ws)
@@ -543,9 +535,8 @@
         (nears[-1], root_sources, held, root, other_roots)
     )
 
-    near = jnp.concatenate(nears, axis=0)
     far_sources, far_ws = far_tables(rhs, place, spots, root, other_roots, held, root_sources)
-    return field(False, 0, per, place, far_lists, far_sources, targets, far_ws, near)
+    return field(False, 0, per, place, far_lists, far_sources, targets, far_ws, *nears)
 
 
 def solution(mesh):

time: 114 us -> 114 us (level)
  local copies, waits for them, and re-layouts: 3.89 us -> 1.96 us
  waiting for transfers between devices: 11.6 us -> 13.4 us
    unnamed x13 -> x5, local copies, waits for them, and re-layouts: 3.01 us -> 1.09 us
    ppermute x11, waiting for transfers between devices: 11.6 us -> 13.4 us  [swap(): return lax.ppermute(x, 'leaf', [(i, i ^ mask) for i in range(size)])]
  transfers between devices with their start and end apart: 14 -> 14, of which waited for: 6 -> 6; matrix products, arithmetic and copies ran while one was open for 3% -> 2% of each run, Pallas kernels for 33% -> 34%
where the time goes in v6:
time: 114 us; the launch traced here: 113 us
  Pallas kernels  76.5 us (67%)
  starting transfers between devices  20 us (18%)
  waiting for transfers between devices  13.4 us (12%)
  local copies, waits for them, and re-layouts  1.96 us (2%)
    pallas_call x6, Pallas kernels, field(): pl.pallas_call(functools.partial(field_kernel, 4, 1024 // columns, start,...  61.9 us
    ppermute x11, waiting for transfers between devices, swap(): return lax.ppermute(x, 'leaf', [(i, i ^ mask) for i in range(size)])  13.4 us
    ppermute x11, starting transfers between devices, swap(): return lax.ppermute(x, 'leaf', [(i, i ^ mask) for i in range(size)])  9.46 us
    ppermute x1, starting transfers between devices, on_device(): lax.ppermute(top_maps, 'leaf', [(n, home_of(n)) for n in range(size)])  8.21 us
    pallas_call x1, Pallas kernels, far_tables(): pl.pallas_call(functools.partial(tables_kernel, rhs), in_specs=[SMEM] * 2...  6 us
    pallas_call x1, Pallas kernels, upward(): pl.pallas_call(upward_kernel, in_specs=[VMEM] * 6, out_specs=VMEM, out_sh...  4.12 us
  transfers between devices with their start and end apart: 14, of which 6 were waited for; matrix products, arithmetic and copies ran while one was open for 2% of the time, Pallas kernels for 34%

profile of v6, /device:TPU:0, one launch (start us, length us, event | category | flops | bytes accessed | tf_op | source)
XLA Modules:
  0.0 113.2 jit_solution(15574440973823162215)
XLA Ops:
  0.0 8.2 %collective-permute-start.2 = (bf16[1,128,256]{2,1,0:T(8,128)(2,1)}, bf16[1,128,256]{2,1,0:T(8,128)(2,1)S(1)}, u32[]{:S(2)}, u32[]{:S(2)}) collective-permute-start(bf16[1,128,256]{2,1,0:T(8,128)(2,1)} %param.13), channel_id=1, source_target_pairs={{0,127},{1,95},{2,31},{3,63},{4,23},{5,55},{6,87},{7,119},{8,7},{9... | collective-permute-start | bytes 196616 | tf_op jit(solution)/shard_map/ppermute | solution.py:482
  8.2 0.9 reshape.8
  9.1 1.1 constant_dynamic-update-slice_fusion.1
  10.2 0.0 copy-start.1
  10.2 0.7 collective-permute-start.1
  10.9 1.6 %collective-permute-start = (bf16[36,32,256]{2,1,0:T(8,128)(2,1)S(1)}, bf16[36,32,256]{2,1,0:T(8,128)(2,1)S(1)}, u32[]{:S(2)}, u32[]{:S(2)}) collective-permute-start(bf16[36,32,256]{2,1,0:T(8,128)(2,1)S(1)} %constant_dynamic-update-slice_fusion.own), channel_id=1, source_target_pairs={{0,1},{1,0},{2,3},{3,2},{4,5},{5,4},{6,7},{7,6},{8,9},{9,8},{10,11... | collective-permute-start | bytes 1769480 | tf_op jit(solution)/shard_map/ppermute | solution.py:484
  12.5 4.1 %shard_map.91 = bf16[1,48,128]{2,1,0:T(8,128)(2,1)} custom-call(bf16[32,32,256]{2,1,0:T(8,128)(2,1)} %points.1, bf16[32,4,256]{2,1,0:T(4,128)(2,1)} %weights.1, bf16[32,128,256]{2,1,0:T(8,128)(2,1)} %leaf_maps.1, bf16[1,128,4096]{2,1,0:T(8,128)(2,1)} %root_maps.1, s32[1,128]{1,0:T(1,128)} %picks.1, s32[1,128]{1,0:T(1,128)} %top_picks.1), custom_call_target="tpu_custom_call" | custom-call | tf_op jit(solution)/shard_map/pallas_call | solution.py:99
  16.6 0.0 collective-permute-done.2
  16.6 0.7 pad_maximum_fusion.9
  17.3 1.9 %collective-permute-start.3 = (bf16[1,304,128]{2,1,0:T(8,128)(2,1)S(1)}, bf16[1,304,128]{2,1,0:T(8,128)(2,1)S(1)}, u32[]{:S(2)}, u32[]{:S(2)}) collective-permute-start(bf16[1,304,128]{2,1,0:T(8,128)(2,1)S(1)} %pad_maximum_fusion.9), channel_id=1, source_target_pairs={{0,4},{1,5},{2,6},{3,7},{4,0},{5,1},{6,2},{7,3},{8,12},{9,13},{10,... | collective-permute-start | bytes 233480 | tf_op jit(solution)/shard_map/ppermute | solution.py:463
  19.2 0.8 shard_map.92
  20.0 3.3 %collective-permute-done.3 = bf16[1,304,128]{2,1,0:T(8,128)(2,1)S(1)} collective-permute-done((bf16[1,304,128]{2,1,0:T(8,128)(2,1)S(1)}, bf16[1,304,128]{2,1,0:T(8,128)(2,1)S(1)}, u32[]{:S(2)}, u32[]{:S(2)}) %collective-permute-start.3) | collective-permute-done | bytes 77856 | tf_op jit(solution)/shard_map/ppermute | solution.py:463
  23.3 0.0 collective-permute-done.1.second
  23.3 0.0 collective-permute-done.first
  23.3 1.5 %shard_map.93 = (bf16[96,256,128]{2,1,0:T(8,128)(2,1)S(1)}, bf16[96,4,256]{2,1,0:T(4,128)(2,1)S(1)}) custom-call(bf16[36,32,256]{2,1,0:T(8,128)(2,1)S(1)} %collective-permute-done.first, bf16[36,32,256]{2,1,0:T(8,128)(2,1)S(1)} %collective-permute-done.1.second, ...), custom_call_target="tpu_custom_call", output_to_operand_aliasing={{0}: (2, {}), {1}: (3, {})} | custom-call | tf_op jit(solution)/shard_map/pallas_call | solution.py:247
  24.8 3.1 %collective-permute-start.5 = (bf16[2,48,128]{2,1,0:T(8,128)(2,1)S(1)}, bf16[2,48,128]{2,1,0:T(8,128)(2,1)S(1)}, u32[]{:S(2)}, u32[]{:S(2)}) collective-permute-start(bf16[2,48,128]{2,1,0:T(8,128)(2,1)S(1)} %slice.11), channel_id=1, source_target_pairs={{0,64},{1,65},{2,66},{3,67},{4,68},{5,69},{6,70},{7,71},{8,72},{9,... | collective-permute-start | bytes 73736 | tf_op jit(solution)/shard_map/ppermute | solution.py:463
  27.8 0.0 collective-permute-start.4
  27.8 4.2 %shard_map.94.rest_0_ = f32[4,4,256]{2,1,0:T(4,128)S(1)} custom-call(s32[1]{0:T(128)} %bitcast.place, s32[16,32]{1,0:T(8,128)S(1)} %bitcast.2, bf16[96,256,128]{2,1,0:T(8,128)(2,1)S(1)} %get-tuple-element.54.sources, bf16[32,128,256]{2,1,0:T(8,128)(2,1)S(1)} %get-tuple-element.55.targets, bf16[96,4,256]{2,1,0:T(4,128)(2,1)S(1)} %get-tuple-element.56.ws), custom_call_target="tpu_custom_call" | custom-call | flops 4294967296 | bytes 1048576 | tf_op jit(solution)/shard_map/pallas_call | solution.py:301
  32.0 0.0 collective-permute-done.5
  32.1 1.1 collective-permute-done.4
  33.2 0.1 collective-permute-start.6
  33.3 0.1 collective-permute-start.7
  33.4 4.1 %collective-permute-done.7 = bf16[4,48,128]{2,1,0:T(8,128)(2,1)S(1)} collective-permute-done((bf16[4,48,128]{2,1,0:T(8,128)(2,1)S(1)}, bf16[4,48,128]{2,1,0:T(8,128)(2,1)S(1)}, u32[]{:S(2)}, u32[]{:S(2)}) %collective-permute-start.7) | collective-permute-done | bytes 49184 | tf_op jit(solution)/shard_map/ppermute | solution.py:463
  37.5 0.0 collective-permute-done.6
  37.5 0.1 pad_maximum_fusion.2.held
  37.6 0.5 shard_map.95
  38.0 1.4 %collective-permute-start.8 = (bf16[1,688,128]{2,1,0:T(8,128)(2,1)S(1)}, bf16[1,688,128]{2,1,0:T(8,128)(2,1)S(1)}, u32[]{:S(2)}, u32[]{:S(2)}) collective-permute-start(bf16[1,688,128]{2,1,0:T(8,128)(2,1)S(1)} %shard_map.95), channel_id=1, source_target_pairs={{0,16},{1,17},{2,18},{3,19},{4,20},{5,21},{6,22},{7,23},{8,24},{9,... | collective-permute-start | bytes 528392 | tf_op jit(solution)/shard_map/ppermute | solution.py:463
  39.4 7.8 %shard_map.96.rest_1_ = f32[8,4,256]{2,1,0:T(4,128)S(1)} custom-call(s32[1]{0:T(128)} %bitcast.place, s32[16,32]{1,0:T(8,128)S(1)} %bitcast.3, bf16[96,256,128]{2,1,0:T(8,128)(2,1)S(1)} %get-tuple-element.54.sources, bf16[32,128,256]{2,1,0:T(8,128)(2,1)S(1)} %get-tuple-element.55.targets, bf16[96,4,256]{2,1,0:T(4,128)(2,1)S(1)} %get-tuple-element.56.ws), custom_call_target="tpu_custom_call" | custom-call | flops 8589934592 | bytes 1048576 | tf_op jit(solution)/shard_map/pallas_call | solution.py:301
  47.2 0.0 collective-permute-done.8
  47.2 0.1 collective-permute-start.9
  47.3 7.8 %shard_map.97.rest_2_ = f32[8,4,256]{2,1,0:T(4,128)S(1)} custom-call(s32[1]{0:T(128)} %bitcast.place, s32[16,32]{1,0:T(8,128)S(1)} %bitcast.4, bf16[96,256,128]{2,1,0:T(8,128)(2,1)S(1)} %get-tuple-element.54.sources, bf16[32,128,256]{2,1,0:T(8,128)(2,1)S(1)} %get-tuple-element.55.targets, bf16[96,4,256]{2,1,0:T(4,128)(2,1)S(1)} %get-tuple-element.56.ws), custom_call_target="tpu_custom_call" | custom-call | flops 8589934592 | bytes 1048576 | tf_op jit(solution)/shard_map/pallas_call | solution.py:301
  55.1 1.3 %collective-permute-done.9 = bf16[2,688,128]{2,1,0:T(8,128)(2,1)S(1)} collective-permute-done((bf16[2,688,128]{2,1,0:T(8,128)(2,1)S(1)}, bf16[2,688,128]{2,1,0:T(8,128)(2,1)S(1)}, u32[]{:S(2)}, u32[]{:S(2)}) %collective-permute-start.9) | collective-permute-done | bytes 352288 | tf_op jit(solution)/shard_map/ppermute | solution.py:463
  56.5 0.1 pad_maximum_fusion.1.held
  56.5 0.3 shard_map.98
  56.8 1.6 %collective-permute-start.10 = (bf16[1,480,128]{2,1,0:T(8,128)(2,1)S(1)}, bf16[1,480,128]{2,1,0:T(8,128)(2,1)S(1)}, u32[]{:S(2)}, u32[]{:S(2)}) collective-permute-start(bf16[1,480,128]{2,1,0:T(8,128)(2,1)S(1)} %get-tuple-element.71), channel_id=1, source_target_pairs={{0,64},{1,65},{2,66},{3,67},{4,68},{5,69},{6,70},{7,71},{8,72},{9,... | collective-permute-start | bytes 368648 | tf_op jit(solution)/shard_map/ppermute | solution.py:463
  58.4 0.9 collective-permute-start.11
  59.4 7.8 %shard_map.99.rest_3_ = f32[8,4,256]{2,1,0:T(4,128)S(1)} custom-call(s32[1]{0:T(128)} %bitcast.place, s32[16,32]{1,0:T(8,128)S(1)} %bitcast.5, bf16[96,256,128]{2,1,0:T(8,128)(2,1)S(1)} %get-tuple-element.54.sources, bf16[32,128,256]{2,1,0:T(8,128)(2,1)S(1)} %get-tuple-element.55.targets, bf16[96,4,256]{2,1,0:T(4,128)(2,1)S(1)} %get-tuple-element.56.ws), custom_call_target="tpu_custom_call" | custom-call | flops 8589934592 | bytes 1048576 | tf_op jit(solution)/shard_map/pallas_call | solution.py:301
  67.2 0.0 collective-permute-done.10
  67.2 0.9 collective-permute-done.11
  68.1 0.1 pad_maximum_fusion.roots.own_roots
  68.2 0.1 collective-permute-start.13
  68.3 0.3 collective-permute-start.12
  68.6 1.4 %shard_map.101._ = bf16[256,128,128]{2,1,0:T(8,128)(2,1)S(1)} custom-call(s32[128]{0:T(128)S(1)} %fusion.6.spots, bf16[64,48,128]{2,1,0:T(8,128)(2,1)S(1)} %pad_maximum_fusion.roots.own_roots), custom_call_target="tpu_custom_call" | custom-call | tf_op jit(solution)/shard_map/pallas_call | solution.py:335
  70.1 4.2 %shard_map.100.rest_4_ = f32[4,4,256]{2,1,0:T(4,128)S(1)} custom-call(s32[1]{0:T(128)} %bitcast.place, s32[16,32]{1,0:T(8,128)S(1)} %bitcast.6, bf16[96,256,128]{2,1,0:T(8,128)(2,1)S(1)} %get-tuple-element.54.sources, bf16[32,128,256]{2,1,0:T(8,128)(2,1)S(1)} %get-tuple-element.55.targets, bf16[96,4,256]{2,1,0:T(4,128)(2,1)S(1)} %get-tuple-element.56.ws), custom_call_target="tpu_custom_call" | custom-call | flops 4294967296 | bytes 1048576 | tf_op jit(solution)/shard_map/pallas_call | solution.py:301
  74.3 2.7 %collective-permute-done.12 = bf16[2,480,128]{2,1,0:T(8,128)(2,1)S(1)} collective-permute-done((bf16[2,480,128]{2,1,0:T(8,128)(2,1)S(1)}, bf16[2,480,128]{2,1,0:T(8,128)(2,1)S(1)}, u32[]{:S(2)}, u32[]{:S(2)}) %collective-permute-start.12) | collective-permute-done | bytes 245792 | tf_op jit(solution)/shard_map/ppermute | solution.py:463
  77.0 0.0 collective-permute-done.13.other_roots
  77.0 6.0 %shard_map.102 = (bf16[256,128,128]{2,1,0:T(8,128)(2,1)S(1)}, bf16[256,4,128]{2,1,0:T(4,128)(2,1)S(1)}) custom-call(s32[1]{0:T(128)} %bitcast.place, s32[128]{0:T(128)S(1)} %fusion.6.spots, bf16[64,48,128]{2,1,0:T(8,128)(2,1)S(1)} %pad_maximum_fusion.roots.own_roots, ...), custom_call_target="tpu_custom_call", output_to_operand_aliasing={{0}: (5, {})} | custom-call | tf_op jit(solution)/shard_map/pallas_call | solution.py:429
  83.1 30.1 %shard_map.103 = f32[32,4,256]{2,1,0:T(4,128)} custom-call(s32[1]{0:T(128)} %bitcast.place, s32[32,32]{1,0:T(8,128)S(1)} %copy-done, bf16[256,128,128]{2,1,0:T(8,128)(2,1)S(1)} %get-tuple-element.80.sources, bf16[32,128,256]{2,1,0:T(8,128)(2,1)S(1)} %get-tuple-element.55.targets, bf16[256,4,128]{2,1,0:T(4,128)(2,1)S(1)} %get-tuple-element.81.ws, ...), custom_call_target="tpu_custom_call" | custom-call | flops 34359738368 | bytes 1048576 | tf_op jit(solution)/shard_map/pallas_call | solution.py:301
  (14 shorter events, 0.2 us)
Async XLA Ops:
  0.0 16.6 %collective-permute-start.2 = (bf16[1,128,256]{2,1,0:T(8,128)(2,1)}, bf16[1,128,256]{2,1,0:T(8,128)(2,1)S(1)}, u32[]{:S(2)}, u32[]{:S(2)}) collective-permute-start(bf16[1,128,256]{2,1,0:T(8,128)(2,1)} %param.13), channel_id=1, source_target_pairs={{0,127},{1,95},{2,31},{3,63},{4,23},{5,55},{6,87},{7,119},{8,7},{9... | collective-permute-start | bytes 196616 | tf_op jit(solution)/shard_map/ppermute | solution.py:482
  10.2 17.7 %copy-start.1 = (s32[32,16]{0,1:T(8,128)S(1)}, s32[32,16]{0,1:T(8,128)}, u32[]{:S(2)}) copy-start(s32[32,16]{0,1:T(8,128)} %param.16) | copy-start | bytes 6148
  10.2 13.1 %collective-permute-start.1 = (bf16[36,32,256]{2,1,0:T(8,128)(2,1)S(1)}, bf16[36,32,256]{2,1,0:T(8,128)(2,1)S(1)}, u32[]{:S(2)}, u32[]{:S(2)}) collective-permute-start(bf16[36,32,256]{2,1,0:T(8,128)(2,1)S(1)} %constant_dynamic-update-slice_fusion.own), channel_id=1, source_target_pairs={{1,2},{3,4},{5,6},{7,8},{9,10},{11,12},{13,14},{15,16},{17,18},{19... | collective-permute-start | bytes 1769480 | tf_op jit(solution)/shard_map/ppermute | solution.py:485
  10.9 12.4 %collective-permute-start = (bf16[36,32,256]{2,1,0:T(8,128)(2,1)S(1)}, bf16[36,32,256]{2,1,0:T(8,128)(2,1)S(1)}, u32[]{:S(2)}, u32[]{:S(2)}) collective-permute-start(bf16[36,32,256]{2,1,0:T(8,128)(2,1)S(1)} %constant_dynamic-update-slice_fusion.own), channel_id=1, source_target_pairs={{0,1},{1,0},{2,3},{3,2},{4,5},{5,4},{6,7},{7,6},{8,9},{9,8},{10,11... | collective-permute-start | bytes 1769480 | tf_op jit(solution)/shard_map/ppermute | solution.py:484
  17.3 5.9 %collective-permute-start.3 = (bf16[1,304,128]{2,1,0:T(8,128)(2,1)S(1)}, bf16[1,304,128]{2,1,0:T(8,128)(2,1)S(1)}, u32[]{:S(2)}, u32[]{:S(2)}) collective-permute-start(bf16[1,304,128]{2,1,0:T(8,128)(2,1)S(1)} %pad_maximum_fusion.9), channel_id=1, source_target_pairs={{0,4},{1,5},{2,6},{3,7},{4,0},{5,1},{6,2},{7,3},{8,12},{9,13},{10,... | collective-permute-start | bytes 233480 | tf_op jit(solution)/shard_map/ppermute | solution.py:463
  24.8 7.3 %collective-permute-start.5 = (bf16[2,48,128]{2,1,0:T(8,128)(2,1)S(1)}, bf16[2,48,128]{2,1,0:T(8,128)(2,1)S(1)}, u32[]{:S(2)}, u32[]{:S(2)}) collective-permute-start(bf16[2,48,128]{2,1,0:T(8,128)(2,1)S(1)} %slice.11), channel_id=1, source_target_pairs={{0,64},{1,65},{2,66},{3,67},{4,68},{5,69},{6,70},{7,71},{8,72},{9,... | collective-permute-start | bytes 73736 | tf_op jit(solution)/shard_map/ppermute | solution.py:463
  27.8 5.4 %collective-permute-start.4 = (bf16[2,304,128]{2,1,0:T(8,128)(2,1)S(1)}, bf16[2,304,128]{2,1,0:T(8,128)(2,1)S(1)}, u32[]{:S(2)}, u32[]{:S(2)}) collective-permute-start(bf16[2,304,128]{2,1,0:T(8,128)(2,1)S(1)} %pad_maximum_fusion.7), channel_id=1, source_target_pairs={{0,2},{1,3},{2,0},{3,1},{4,6},{5,7},{6,4},{7,5},{8,10},{9,11},{10,... | collective-permute-start | bytes 466952 | tf_op jit(solution)/shard_map/ppermute | solution.py:463
  33.2 4.3 %collective-permute-start.6 = (bf16[4,304,128]{2,1,0:T(8,128)(2,1)S(1)}, bf16[4,304,128]{2,1,0:T(8,128)(2,1)S(1)}, u32[]{:S(2)}, u32[]{:S(2)}) collective-permute-start(bf16[4,304,128]{2,1,0:T(8,128)(2,1)S(1)} %pad_maximum_fusion.5), channel_id=1, source_target_pairs={{0,1},{1,0},{2,3},{3,2},{4,5},{5,4},{6,7},{7,6},{8,9},{9,8},{10,11... | collective-permute-start | bytes 933896 | tf_op jit(solution)/shard_map/ppermute | solution.py:463
  33.3 4.2 %collective-permute-start.7 = (bf16[4,48,128]{2,1,0:T(8,128)(2,1)S(1)}, bf16[4,48,128]{2,1,0:T(8,128)(2,1)S(1)}, u32[]{:S(2)}, u32[]{:S(2)}) collective-permute-start(bf16[4,48,128]{2,1,0:T(8,128)(2,1)S(1)} %pad_maximum_fusion.10), channel_id=1, source_target_pairs={{0,32},{1,33},{2,34},{3,35},{4,36},{5,37},{6,38},{7,39},{8,40},{9,... | collective-permute-start | bytes 147464 | tf_op jit(solution)/shard_map/ppermute | solution.py:463
  38.0 9.1 %collective-permute-start.8 = (bf16[1,688,128]{2,1,0:T(8,128)(2,1)S(1)}, bf16[1,688,128]{2,1,0:T(8,128)(2,1)S(1)}, u32[]{:S(2)}, u32[]{:S(2)}) collective-permute-start(bf16[1,688,128]{2,1,0:T(8,128)(2,1)S(1)} %shard_map.95), channel_id=1, source_target_pairs={{0,16},{1,17},{2,18},{3,19},{4,20},{5,21},{6,22},{7,23},{8,24},{9,... | collective-permute-start | bytes 528392 | tf_op jit(solution)/shard_map/ppermute | solution.py:463
  47.2 9.2 %collective-permute-start.9 = (bf16[2,688,128]{2,1,0:T(8,128)(2,1)S(1)}, bf16[2,688,128]{2,1,0:T(8,128)(2,1)S(1)}, u32[]{:S(2)}, u32[]{:S(2)}) collective-permute-start(bf16[2,688,128]{2,1,0:T(8,128)(2,1)S(1)} %pad_maximum_fusion.4), channel_id=1, source_target_pairs={{0,8},{1,9},{2,10},{3,11},{4,12},{5,13},{6,14},{7,15},{8,0},{9,1},... | collective-permute-start | bytes 1056776 | tf_op jit(solution)/shard_map/ppermute | solution.py:463
  56.8 10.3 %collective-permute-start.10 = (bf16[1,480,128]{2,1,0:T(8,128)(2,1)S(1)}, bf16[1,480,128]{2,1,0:T(8,128)(2,1)S(1)}, u32[]{:S(2)}, u32[]{:S(2)}) collective-permute-start(bf16[1,480,128]{2,1,0:T(8,128)(2,1)S(1)} %get-tuple-element.71), channel_id=1, source_target_pairs={{0,64},{1,65},{2,66},{3,67},{4,68},{5,69},{6,70},{7,71},{8,72},{9,... | collective-permute-start | bytes 368648 | tf_op jit(solution)/shard_map/ppermute | solution.py:463
  58.4 9.7 %collective-permute-start.11 = (bf16[32,48,128]{2,1,0:T(8,128)(2,1)S(1)}, bf16[32,48,128]{2,1,0:T(8,128)(2,1)S(1)}, u32[]{:S(2)}, u32[]{:S(2)}) collective-permute-start(bf16[32,48,128]{2,1,0:T(8,128)(2,1)S(1)} %get-tuple-element.72), channel_id=1, source_target_pairs={{0,2},{1,3},{2,0},{3,1},{4,6},{5,7},{6,4},{7,5},{8,10},{9,11},{10,... | collective-permute-start | bytes 1179656 | tf_op jit(solution)/shard_map/ppermute | solution.py:463
  68.2 8.8 %collective-permute-start.13 = (bf16[64,48,128]{2,1,0:T(8,128)(2,1)S(1)}, bf16[64,48,128]{2,1,0:T(8,128)(2,1)S(1)}, u32[]{:S(2)}, u32[]{:S(2)}) collective-permute-start(bf16[64,48,128]{2,1,0:T(8,128)(2,1)S(1)} %pad_maximum_fusion.roots.own_roots), channel_id=1, source_target_pairs={{0,1},{1,0},{2,3},{3,2},{4,5},{5,4},{6,7},{7,6},{8,9},{9,8},{10,11... | collective-permute-start | bytes 2359304 | tf_op jit(solution)/shard_map/ppermute | solution.py:463
  68.3 8.7 %collective-permute-start.12 = (bf16[2,480,128]{2,1,0:T(8,128)(2,1)S(1)}, bf16[2,480,128]{2,1,0:T(8,128)(2,1)S(1)}, u32[]{:S(2)}, u32[]{:S(2)}) collective-permute-start(bf16[2,480,128]{2,1,0:T(8,128)(2,1)S(1)} %pad_maximum_fusion.6), channel_id=1, source_target_pairs={{0,32},{1,33},{2,34},{3,35},{4,36},{5,37},{6,38},{7,39},{8,40},{9,... | collective-permute-start | bytes 737288 | tf_op jit(solution)/shard_map/ppermute | solution.py:463
  74.3 8.8 %copy-start = (s32[32,32]{1,0:T(8,128)S(1)}, s32[32,32]{1,0:T(8,128)}, u32[]{:S(2)}) copy-start(s32[32,32]{1,0:T(8,128)} %lists.1) | copy-start | bytes 12292

commit v7 on v6

--- a/solution.py
+++ b/solution.py
@@ -218,15 +218,16 @@
     lax.fori_loop(0, per // 16, prepare, 0)
 
 
-def own_kernel(own, sources, ws, targets):
+def own_kernel(own, first, sources, ws, targets):
     fill_forms(0, own, sources, ws, targets)
-
-
-def own_forms(own, per, rhs):
+    fill_forms(sources.shape[0] // 3, first, sources, ws)
+
+
+def own_forms(own, first, per, rhs):
     leaf_size = own.shape[2]
     return pl.pallas_call(
         own_kernel,
-        in_specs=[VMEM],
+        in_specs=[VMEM] * 2,
         out_specs=[VMEM] * 3,
         out_shape=[
             jax.ShapeDtypeStruct((3 * per, leaf_size, WIDE), bf16),
@@ -234,27 +235,25 @@
             jax.ShapeDtypeStruct((per, WIDE, leaf_size), bf16),
         ],
         compiler_params=params(24),
-    )(own)
-
-
-def other_kernel(first, second, _, __, sources, ws):
-    per = sources.shape[0] // 3
-    fill_forms(per, first, sources, ws)
-    fill_forms(2 * per, second, sources, ws)
-
-
-def other_forms(first, second, sources, ws):
+    )(own, first)
+
+
+def other_kernel(second, _, __, sources, ws):
+    fill_forms(sources.shape[0] // 3 * 2, second, sources, ws)
+
+
+def other_forms(second, sources, ws):
     return pl.pallas_call(
         other_kernel,
-        in_specs=[VMEM] * 4,
+        in_specs=[VMEM] * 3,
         out_specs=[VMEM] * 2,
         out_shape=[
             jax.ShapeDtypeStruct(sources.shape, bf16),
             jax.ShapeDtypeStruct(ws.shape, bf16),
         ],
-        input_output_aliases={2: 0, 3: 1},
+        input_output_aliases={1: 0, 2: 1},
         compiler_params=params(24),
-    )(first, second, sources, ws)
+    )(second, sources, ws)
 
 
 def near_place(place, per, leaf):
@@ -499,12 +498,12 @@
 
     half = maps.shape[2] // 2
     held = jnp.concatenate([maps[:, :, :half], maps[:, :, half:], root], axis=1)
-    held, own = tie((held, own))
+    held, own, first = tie((held, own, first))
     held = both(held, 4, size)
-    sources, ws, targets = own_forms(own, per, rhs)
+    sources, ws, targets = own_forms(own, first, per, rhs)
     held, sources = tie((held, sources))
     root = held[:, MAP_ROWS:]
-    sources, ws = other_forms(first, second, sources, ws)
+    sources, ws = other_forms(second, sources, ws)
     sources, columns, held, root = tie((sources, columns, held, root))
     held, root = swaps(1, 2, held, root)
     near_part(4)

time: 114 us -> 113 us (level)
  waiting for transfers between devices: 13.4 us -> 11.6 us
    ppermute x11, waiting for transfers between devices: 13.4 us -> 11.6 us  [swap(): return lax.ppermute(x, 'leaf', [(i, i ^ mask) for i in range(size)])]
    ppermute x1, starting transfers between devices: 1.6 us -> 0.09 us  [on_device(): first = lax.ppermute(own, 'leaf', pairs)]
    ppermute x11, starting transfers between devices: 9.46 us -> 10.6 us  [swap(): return lax.ppermute(x, 'leaf', [(i, i ^ mask) for i in range(size)])]
  transfers between devices with their start and end apart: 14 -> 14, of which waited for: 6 -> 6; matrix products, arithmetic and copies ran while one was open for 2% -> 1% of each run, Pallas kernels for 34% -> 35%
where the time goes in v7:
time: 113 us; the launch traced here: 112 us
  Pallas kernels  76.5 us (68%)
  starting transfers between devices  20.3 us (18%)
  waiting for transfers between devices  11.6 us (10%)
  local copies, waits for them, and re-layouts  1.96 us (2%)
    pallas_call x6, Pallas kernels, field(): pl.pallas_call(functools.partial(field_kernel, 4, 1024 // columns, start,...  61.9 us
    ppermute x11, waiting for transfers between devices, swap(): return lax.ppermute(x, 'leaf', [(i, i ^ mask) for i in range(size)])  11.6 us
    ppermute x11, starting transfers between devices, swap(): return lax.ppermute(x, 'leaf', [(i, i ^ mask) for i in range(size)])  10.6 us
    ppermute x1, starting transfers between devices, on_device(): lax.ppermute(top_maps, 'leaf', [(n, home_of(n)) for n in range(size)])  8.87 us
    pallas_call x1, Pallas kernels, far_tables(): pl.pallas_call(functools.partial(tables_kernel, rhs), in_specs=[SMEM] * 2...  6 us
    pallas_call x1, Pallas kernels, upward(): pl.pallas_call(upward_kernel, in_specs=[VMEM] * 6, out_specs=VMEM, out_sh...  4.13 us
  transfers between devices with their start and end apart: 14, of which 6 were waited for; matrix products, arithmetic and copies ran while one was open for 1% of the time, Pallas kernels for 35%

profile of v7, /device:TPU:0, one launch (start us, length us, event | category | flops | bytes accessed | tf_op | source)
XLA Modules:
  0.0 111.7 jit_solution(4774106707821679779)
XLA Ops:
  0.0 0.9 reshape.8
  0.9 1.1 constant_dynamic-update-slice_fusion.1
  2.0 0.0 copy-start.1
  2.0 0.1 collective-permute-start.2
  2.1 8.9 %collective-permute-start.1 = (bf16[1,128,256]{2,1,0:T(8,128)(2,1)}, bf16[1,128,256]{2,1,0:T(8,128)(2,1)S(1)}, u32[]{:S(2)}, u32[]{:S(2)}) collective-permute-start(bf16[1,128,256]{2,1,0:T(8,128)(2,1)} %param.13), channel_id=1, source_target_pairs={{0,127},{1,95},{2,31},{3,63},{4,23},{5,55},{6,87},{7,119},{8,7},{9... | collective-permute-start | bytes 196616 | tf_op jit(solution)/shard_map/ppermute | solution.py:481
  10.9 0.7 collective-permute-start
  11.6 4.1 %shard_map.91 = bf16[1,48,128]{2,1,0:T(8,128)(2,1)} custom-call(bf16[32,32,256]{2,1,0:T(8,128)(2,1)} %points.1, bf16[32,4,256]{2,1,0:T(4,128)(2,1)} %weights.1, bf16[32,128,256]{2,1,0:T(8,128)(2,1)} %leaf_maps.1, bf16[1,128,4096]{2,1,0:T(8,128)(2,1)} %root_maps.1, s32[1,128]{1,0:T(1,128)} %picks.1, s32[1,128]{1,0:T(1,128)} %top_picks.1), custom_call_target="tpu_custom_call" | custom-call | tf_op jit(solution)/shard_map/pallas_call | solution.py:99
  15.7 0.0 collective-permute-done.1
  15.8 0.7 pad_maximum_fusion.9
  16.5 0.0 collective-permute-done.2.first
  16.5 2.5 %collective-permute-start.3 = (bf16[1,304,128]{2,1,0:T(8,128)(2,1)S(1)}, bf16[1,304,128]{2,1,0:T(8,128)(2,1)S(1)}, u32[]{:S(2)}, u32[]{:S(2)}) collective-permute-start(bf16[1,304,128]{2,1,0:T(8,128)(2,1)S(1)} %pad_maximum_fusion.9), channel_id=1, source_target_pairs={{0,4},{1,5},{2,6},{3,7},{4,0},{5,1},{6,2},{7,3},{8,12},{9,13},{10,... | collective-permute-start | bytes 233480 | tf_op jit(solution)/shard_map/ppermute | solution.py:462
  19.0 1.5 %shard_map.92 = (bf16[96,256,128]{2,1,0:T(8,128)(2,1)S(1)}, bf16[96,4,256]{2,1,0:T(4,128)(2,1)S(1)}, bf16[32,128,256]{2,1,0:T(8,128)(2,1)S(1)}) custom-call(bf16[36,32,256]{2,1,0:T(8,128)(2,1)S(1)} %constant_dynamic-update-slice_fusion.own, bf16[36,32,256]{2,1,0:T(8,128)(2,1)S(1)} %collective-permute-done.2.first), custom_call_target="tpu_custom_call" | custom-call | tf_op jit(solution)/shard_map/pallas_call | solution.py:228
  20.5 2.9 %collective-permute-done.3 = bf16[1,304,128]{2,1,0:T(8,128)(2,1)S(1)} collective-permute-done((bf16[1,304,128]{2,1,0:T(8,128)(2,1)S(1)}, bf16[1,304,128]{2,1,0:T(8,128)(2,1)S(1)}, u32[]{:S(2)}, u32[]{:S(2)}) %collective-permute-start.3) | collective-permute-done | bytes 77856 | tf_op jit(solution)/shard_map/ppermute | solution.py:462
  23.4 0.0 collective-permute-done.second
  23.4 0.7 shard_map.93
  24.1 3.3 %collective-permute-start.5 = (bf16[2,48,128]{2,1,0:T(8,128)(2,1)S(1)}, bf16[2,48,128]{2,1,0:T(8,128)(2,1)S(1)}, u32[]{:S(2)}, u32[]{:S(2)}) collective-permute-start(bf16[2,48,128]{2,1,0:T(8,128)(2,1)S(1)} %slice.11), channel_id=1, source_target_pairs={{0,64},{1,65},{2,66},{3,67},{4,68},{5,69},{6,70},{7,71},{8,72},{9,... | collective-permute-start | bytes 73736 | tf_op jit(solution)/shard_map/ppermute | solution.py:462
  27.5 0.0 collective-permute-start.4
  27.5 4.2 %shard_map.94.rest_0_ = f32[4,4,256]{2,1,0:T(4,128)S(1)} custom-call(s32[1]{0:T(128)} %bitcast.place, s32[16,32]{1,0:T(8,128)S(1)} %bitcast.2, bf16[96,256,128]{2,1,0:T(8,128)(2,1)S(1)} %get-tuple-element.56.sources, bf16[32,128,256]{2,1,0:T(8,128)(2,1)S(1)} %get-tuple-element.57.targets, bf16[96,4,256]{2,1,0:T(4,128)(2,1)S(1)} %get-tuple-element.58.ws), custom_call_target="tpu_custom_call" | custom-call | flops 4294967296 | bytes 1048576 | tf_op jit(solution)/shard_map/pallas_call | solution.py:300
  31.7 0.0 collective-permute-done.5
  31.7 1.0 collective-permute-done.4
  32.7 0.1 collective-permute-start.6
  32.8 0.1 collective-permute-start.7
  32.9 4.1 %collective-permute-done.7 = bf16[4,48,128]{2,1,0:T(8,128)(2,1)S(1)} collective-permute-done((bf16[4,48,128]{2,1,0:T(8,128)(2,1)S(1)}, bf16[4,48,128]{2,1,0:T(8,128)(2,1)S(1)}, u32[]{:S(2)}, u32[]{:S(2)}) %collective-permute-start.7) | collective-permute-done | bytes 49184 | tf_op jit(solution)/shard_map/ppermute | solution.py:462
  37.0 0.0 collective-permute-done.6
  37.0 0.1 pad_maximum_fusion.2.held
  37.1 0.5 shard_map.95
  37.5 1.4 %collective-permute-start.8 = (bf16[1,688,128]{2,1,0:T(8,128)(2,1)S(1)}, bf16[1,688,128]{2,1,0:T(8,128)(2,1)S(1)}, u32[]{:S(2)}, u32[]{:S(2)}) collective-permute-start(bf16[1,688,128]{2,1,0:T(8,128)(2,1)S(1)} %shard_map.95), channel_id=1, source_target_pairs={{0,16},{1,17},{2,18},{3,19},{4,20},{5,21},{6,22},{7,23},{8,24},{9,... | collective-permute-start | bytes 528392 | tf_op jit(solution)/shard_map/ppermute | solution.py:462
  38.9 7.8 %shard_map.96.rest_1_ = f32[8,4,256]{2,1,0:T(4,128)S(1)} custom-call(s32[1]{0:T(128)} %bitcast.place, s32[16,32]{1,0:T(8,128)S(1)} %bitcast.3, bf16[96,256,128]{2,1,0:T(8,128)(2,1)S(1)} %get-tuple-element.56.sources, bf16[32,128,256]{2,1,0:T(8,128)(2,1)S(1)} %get-tuple-element.57.targets, bf16[96,4,256]{2,1,0:T(4,128)(2,1)S(1)} %get-tuple-element.58.ws), custom_call_target="tpu_custom_call" | custom-call | flops 8589934592 | bytes 1048576 | tf_op jit(solution)/shard_map/pallas_call | solution.py:300
  46.7 0.0 collective-permute-done.8
  46.8 0.1 collective-permute-start.9
  46.8 7.8 %shard_map.97.rest_2_ = f32[8,4,256]{2,1,0:T(4,128)S(1)} custom-call(s32[1]{0:T(128)} %bitcast.place, s32[16,32]{1,0:T(8,128)S(1)} %bitcast.4, bf16[96,256,128]{2,1,0:T(8,128)(2,1)S(1)} %get-tuple-element.56.sources, bf16[32,128,256]{2,1,0:T(8,128)(2,1)S(1)} %get-tuple-element.57.targets, bf16[96,4,256]{2,1,0:T(4,128)(2,1)S(1)} %get-tuple-element.58.ws), custom_call_target="tpu_custom_call" | custom-call | flops 8589934592 | bytes 1048576 | tf_op jit(solution)/shard_map/pallas_call | solution.py:300
  54.6 1.3 %collective-permute-done.9 = bf16[2,688,128]{2,1,0:T(8,128)(2,1)S(1)} collective-permute-done((bf16[2,688,128]{2,1,0:T(8,128)(2,1)S(1)}, bf16[2,688,128]{2,1,0:T(8,128)(2,1)S(1)}, u32[]{:S(2)}, u32[]{:S(2)}) %collective-permute-start.9) | collective-permute-done | bytes 352288 | tf_op jit(solution)/shard_map/ppermute | solution.py:462
  56.0 0.1 pad_maximum_fusion.1.held
  56.0 0.3 shard_map.98
  56.4 1.0 collective-permute-start.10
  57.4 1.1 collective-permute-start.11
  58.5 7.8 %shard_map.99.rest_3_ = f32[8,4,256]{2,1,0:T(4,128)S(1)} custom-call(s32[1]{0:T(128)} %bitcast.place, s32[16,32]{1,0:T(8,128)S(1)} %bitcast.5, bf16[96,256,128]{2,1,0:T(8,128)(2,1)S(1)} %get-tuple-element.56.sources, bf16[32,128,256]{2,1,0:T(8,128)(2,1)S(1)} %get-tuple-element.57.targets, bf16[96,4,256]{2,1,0:T(4,128)(2,1)S(1)} %get-tuple-element.58.ws), custom_call_target="tpu_custom_call" | custom-call | flops 8589934592 | bytes 1048576 | tf_op jit(solution)/shard_map/pallas_call | solution.py:300
  66.2 0.0 collective-permute-done.10
  66.3 0.4 collective-permute-done.11
  66.7 0.1 pad_maximum_fusion.roots.own_roots
  66.8 0.1 collective-permute-start.13
  66.9 1.0 collective-permute-start.12
  67.9 1.4 %shard_map.101._ = bf16[256,128,128]{2,1,0:T(8,128)(2,1)S(1)} custom-call(s32[128]{0:T(128)S(1)} %fusion.6.spots, bf16[64,48,128]{2,1,0:T(8,128)(2,1)S(1)} %pad_maximum_fusion.roots.own_roots), custom_call_target="tpu_custom_call" | custom-call | tf_op jit(solution)/shard_map/pallas_call | solution.py:334
  69.3 4.2 %shard_map.100.rest_4_ = f32[4,4,256]{2,1,0:T(4,128)S(1)} custom-call(s32[1]{0:T(128)} %bitcast.place, s32[16,32]{1,0:T(8,128)S(1)} %bitcast.6, bf16[96,256,128]{2,1,0:T(8,128)(2,1)S(1)} %get-tuple-element.56.sources, bf16[32,128,256]{2,1,0:T(8,128)(2,1)S(1)} %get-tuple-element.57.targets, bf16[96,4,256]{2,1,0:T(4,128)(2,1)S(1)} %get-tuple-element.58.ws), custom_call_target="tpu_custom_call" | custom-call | flops 4294967296 | bytes 1048576 | tf_op jit(solution)/shard_map/pallas_call | solution.py:300
  73.5 2.0 %collective-permute-done.12 = bf16[2,480,128]{2,1,0:T(8,128)(2,1)S(1)} collective-permute-done((bf16[2,480,128]{2,1,0:T(8,128)(2,1)S(1)}, bf16[2,480,128]{2,1,0:T(8,128)(2,1)S(1)}, u32[]{:S(2)}, u32[]{:S(2)}) %collective-permute-start.12) | collective-permute-done | bytes 245792 | tf_op jit(solution)/shard_map/ppermute | solution.py:462
  75.6 0.0 collective-permute-done.13.other_roots
  75.6 6.0 %shard_map.102 = (bf16[256,128,128]{2,1,0:T(8,128)(2,1)S(1)}, bf16[256,4,128]{2,1,0:T(4,128)(2,1)S(1)}) custom-call(s32[1]{0:T(128)} %bitcast.place, s32[128]{0:T(128)S(1)} %fusion.6.spots, bf16[64,48,128]{2,1,0:T(8,128)(2,1)S(1)} %pad_maximum_fusion.roots.own_roots, ...), custom_call_target="tpu_custom_call", output_to_operand_aliasing={{0}: (5, {})} | custom-call | tf_op jit(solution)/shard_map/pallas_call | solution.py:428
  81.6 30.1 %shard_map.103 = f32[32,4,256]{2,1,0:T(4,128)} custom-call(s32[1]{0:T(128)} %bitcast.place, s32[32,32]{1,0:T(8,128)S(1)} %copy-done, bf16[256,128,128]{2,1,0:T(8,128)(2,1)S(1)} %get-tuple-element.82.sources, bf16[32,128,256]{2,1,0:T(8,128)(2,1)S(1)} %get-tuple-element.57.targets, bf16[256,4,128]{2,1,0:T(4,128)(2,1)S(1)} %get-tuple-element.83.ws, ...), custom_call_target="tpu_custom_call" | custom-call | flops 34359738368 | bytes 1048576 | tf_op jit(solution)/shard_map/pallas_call | solution.py:300
  (14 shorter events, 0.2 us)
Async XLA Ops:
  2.0 25.5 %copy-start.1 = (s32[32,16]{0,1:T(8,128)S(1)}, s32[32,16]{0,1:T(8,128)}, u32[]{:S(2)}) copy-start(s32[32,16]{0,1:T(8,128)} %param.16) | copy-start | bytes 6148
  2.0 14.5 %collective-permute-start.2 = (bf16[36,32,256]{2,1,0:T(8,128)(2,1)S(1)}, bf16[36,32,256]{2,1,0:T(8,128)(2,1)S(1)}, u32[]{:S(2)}, u32[]{:S(2)}) collective-permute-start(bf16[36,32,256]{2,1,0:T(8,128)(2,1)S(1)} %constant_dynamic-update-slice_fusion.own), channel_id=1, source_target_pairs={{0,1},{1,0},{2,3},{3,2},{4,5},{5,4},{6,7},{7,6},{8,9},{9,8},{10,11... | collective-permute-start | bytes 1769480 | tf_op jit(solution)/shard_map/ppermute | solution.py:483
  2.1 13.7 %collective-permute-start.1 = (bf16[1,128,256]{2,1,0:T(8,128)(2,1)}, bf16[1,128,256]{2,1,0:T(8,128)(2,1)S(1)}, u32[]{:S(2)}, u32[]{:S(2)}) collective-permute-start(bf16[1,128,256]{2,1,0:T(8,128)(2,1)} %param.13), channel_id=1, source_target_pairs={{0,127},{1,95},{2,31},{3,63},{4,23},{5,55},{6,87},{7,119},{8,7},{9... | collective-permute-start | bytes 196616 | tf_op jit(solution)/shard_map/ppermute | solution.py:481
  10.9 12.5 %collective-permute-start = (bf16[36,32,256]{2,1,0:T(8,128)(2,1)S(1)}, bf16[36,32,256]{2,1,0:T(8,128)(2,1)S(1)}, u32[]{:S(2)}, u32[]{:S(2)}) collective-permute-start(bf16[36,32,256]{2,1,0:T(8,128)(2,1)S(1)} %constant_dynamic-update-slice_fusion.own), channel_id=1, source_target_pairs={{1,2},{3,4},{5,6},{7,8},{9,10},{11,12},{13,14},{15,16},{17,18},{19... | collective-permute-start | bytes 1769480 | tf_op jit(solution)/shard_map/ppermute | solution.py:484
  16.5 6.9 %collective-permute-start.3 = (bf16[1,304,128]{2,1,0:T(8,128)(2,1)S(1)}, bf16[1,304,128]{2,1,0:T(8,128)(2,1)S(1)}, u32[]{:S(2)}, u32[]{:S(2)}) collective-permute-start(bf16[1,304,128]{2,1,0:T(8,128)(2,1)S(1)} %pad_maximum_fusion.9), channel_id=1, source_target_pairs={{0,4},{1,5},{2,6},{3,7},{4,0},{5,1},{6,2},{7,3},{8,12},{9,13},{10,... | collective-permute-start | bytes 233480 | tf_op jit(solution)/shard_map/ppermute | solution.py:462
  24.1 7.5 %collective-permute-start.5 = (bf16[2,48,128]{2,1,0:T(8,128)(2,1)S(1)}, bf16[2,48,128]{2,1,0:T(8,128)(2,1)S(1)}, u32[]{:S(2)}, u32[]{:S(2)}) collective-permute-start(bf16[2,48,128]{2,1,0:T(8,128)(2,1)S(1)} %slice.11), channel_id=1, source_target_pairs={{0,64},{1,65},{2,66},{3,67},{4,68},{5,69},{6,70},{7,71},{8,72},{9,... | collective-permute-start | bytes 73736 | tf_op jit(solution)/shard_map/ppermute | solution.py:462
  27.5 5.2 %collective-permute-start.4 = (bf16[2,304,128]{2,1,0:T(8,128)(2,1)S(1)}, bf16[2,304,128]{2,1,0:T(8,128)(2,1)S(1)}, u32[]{:S(2)}, u32[]{:S(2)}) collective-permute-start(bf16[2,304,128]{2,1,0:T(8,128)(2,1)S(1)} %pad_maximum_fusion.7), channel_id=1, source_target_pairs={{0,2},{1,3},{2,0},{3,1},{4,6},{5,7},{6,4},{7,5},{8,10},{9,11},{10,... | collective-permute-start | bytes 466952 | tf_op jit(solution)/shard_map/ppermute | solution.py:462
  32.7 4.3 %collective-permute-start.6 = (bf16[4,304,128]{2,1,0:T(8,128)(2,1)S(1)}, bf16[4,304,128]{2,1,0:T(8,128)(2,1)S(1)}, u32[]{:S(2)}, u32[]{:S(2)}) collective-permute-start(bf16[4,304,128]{2,1,0:T(8,128)(2,1)S(1)} %pad_maximum_fusion.5), channel_id=1, source_target_pairs={{0,1},{1,0},{2,3},{3,2},{4,5},{5,4},{6,7},{7,6},{8,9},{9,8},{10,11... | collective-permute-start | bytes 933896 | tf_op jit(solution)/shard_map/ppermute | solution.py:462
  32.8 4.2 %collective-permute-start.7 = (bf16[4,48,128]{2,1,0:T(8,128)(2,1)S(1)}, bf16[4,48,128]{2,1,0:T(8,128)(2,1)S(1)}, u32[]{:S(2)}, u32[]{:S(2)}) collective-permute-start(bf16[4,48,128]{2,1,0:T(8,128)(2,1)S(1)} %pad_maximum_fusion.10), channel_id=1, source_target_pairs={{0,32},{1,33},{2,34},{3,35},{4,36},{5,37},{6,38},{7,39},{8,40},{9,... | collective-permute-start | bytes 147464 | tf_op jit(solution)/shard_map/ppermute | solution.py:462
  37.5 9.2 %collective-permute-start.8 = (bf16[1,688,128]{2,1,0:T(8,128)(2,1)S(1)}, bf16[1,688,128]{2,1,0:T(8,128)(2,1)S(1)}, u32[]{:S(2)}, u32[]{:S(2)}) collective-permute-start(bf16[1,688,128]{2,1,0:T(8,128)(2,1)S(1)} %shard_map.95), channel_id=1, source_target_pairs={{0,16},{1,17},{2,18},{3,19},{4,20},{5,21},{6,22},{7,23},{8,24},{9,... | collective-permute-start | bytes 528392 | tf_op jit(solution)/shard_map/ppermute | solution.py:462
  46.8 9.2 %collective-permute-start.9 = (bf16[2,688,128]{2,1,0:T(8,128)(2,1)S(1)}, bf16[2,688,128]{2,1,0:T(8,128)(2,1)S(1)}, u32[]{:S(2)}, u32[]{:S(2)}) collective-permute-start(bf16[2,688,128]{2,1,0:T(8,128)(2,1)S(1)} %pad_maximum_fusion.4), channel_id=1, source_target_pairs={{0,8},{1,9},{2,10},{3,11},{4,12},{5,13},{6,14},{7,15},{8,0},{9,1},... | collective-permute-start | bytes 1056776 | tf_op jit(solution)/shard_map/ppermute | solution.py:462
  56.4 9.9 %collective-permute-start.10 = (bf16[1,480,128]{2,1,0:T(8,128)(2,1)S(1)}, bf16[1,480,128]{2,1,0:T(8,128)(2,1)S(1)}, u32[]{:S(2)}, u32[]{:S(2)}) collective-permute-start(bf16[1,480,128]{2,1,0:T(8,128)(2,1)S(1)} %get-tuple-element.73), channel_id=1, source_target_pairs={{0,64},{1,65},{2,66},{3,67},{4,68},{5,69},{6,70},{7,71},{8,72},{9,... | collective-permute-start | bytes 368648 | tf_op jit(solution)/shard_map/ppermute | solution.py:462
  57.4 9.3 %collective-permute-start.11 = (bf16[32,48,128]{2,1,0:T(8,128)(2,1)S(1)}, bf16[32,48,128]{2,1,0:T(8,128)(2,1)S(1)}, u32[]{:S(2)}, u32[]{:S(2)}) collective-permute-start(bf16[32,48,128]{2,1,0:T(8,128)(2,1)S(1)} %get-tuple-element.74), channel_id=1, source_target_pairs={{0,2},{1,3},{2,0},{3,1},{4,6},{5,7},{6,4},{7,5},{8,10},{9,11},{10,... | collective-permute-start | bytes 1179656 | tf_op jit(solution)/shard_map/ppermute | solution.py:462
  66.8 8.8 %collective-permute-start.13 = (bf16[64,48,128]{2,1,0:T(8,128)(2,1)S(1)}, bf16[64,48,128]{2,1,0:T(8,128)(2,1)S(1)}, u32[]{:S(2)}, u32[]{:S(2)}) collective-permute-start(bf16[64,48,128]{2,1,0:T(8,128)(2,1)S(1)} %pad_maximum_fusion.roots.own_roots), channel_id=1, source_target_pairs={{0,1},{1,0},{2,3},{3,2},{4,5},{5,4},{6,7},{7,6},{8,9},{9,8},{10,11... | collective-permute-start | bytes 2359304 | tf_op jit(solution)/shard_map/ppermute | solution.py:462
  66.9 8.7 %collective-permute-start.12 = (bf16[2,480,128]{2,1,0:T(8,128)(2,1)S(1)}, bf16[2,480,128]{2,1,0:T(8,128)(2,1)S(1)}, u32[]{:S(2)}, u32[]{:S(2)}) collective-permute-start(bf16[2,480,128]{2,1,0:T(8,128)(2,1)S(1)} %pad_maximum_fusion.6), channel_id=1, source_target_pairs={{0,32},{1,33},{2,34},{3,35},{4,36},{5,37},{6,38},{7,39},{8,40},{9,... | collective-permute-start | bytes 737288 | tf_op jit(solution)/shard_map/ppermute | solution.py:462
  73.5 8.0 %copy-start = (s32[32,32]{1,0:T(8,128)S(1)}, s32[32,32]{1,0:T(8,128)}, u32[]{:S(2)}) copy-start(s32[32,32]{1,0:T(8,128)} %lists.1) | copy-start | bytes 12292
